TPU v7x, 32 devices: a whole 2x2x4 slice. The times are simulated.
32 devices in a mesh: shard: 4 (over z), ctx: 2 (over core), tp: 4 (over y, x).
Axes of the slice: x: 2, y: 2, z: 4, core: 2. Of those that a mesh axis runs over, the one named last changes fastest.
Arguments:
- hidden_in: bfloat16 [16384, 768], P(('shard', 'ctx', 'tp')), may hold values from -6 to 6
- cotangent: bfloat16 [16384, 768], P(('shard', 'ctx', 'tp')), may hold values from -6 to 6
- lengths: int32 [4], P('shard'), may hold values from 1024 to 4096, as said below
- routes: int32 [16384, 2], P(('shard', 'ctx')), may hold values from 0 to 11, all different within a row; in each aligned block of 2048 rows (0 to 2047, 2048 to 4095, ...) at most 512 rows name the same one
- prev_logits: float32 [16384, 12], P(('shard', 'ctx')), may hold values from -4 to 4
- norm_attn: bfloat16 [768], P('shard'), may hold values from 0.5 to 1.5
- w_query: bfloat16 [768, 768], P('shard', 'tp'), may hold values from -0.21875 to 0.21875
- w_key: bfloat16 [768, 768], P('shard', 'tp'), may hold values from -0.21875 to 0.21875
- w_value: bfloat16 [768, 768], P('shard', 'tp'), may hold values from -0.21875 to 0.21875
- w_out: bfloat16 [768, 768], P('tp', 'shard'), may hold values from -1.75 to 1.75
- norm_moe: bfloat16 [768], P('shard'), may hold values from 0.5 to 1.5
- w_router: bfloat16 [768, 12], P('shard'), may hold values from -0.109375 to 0.109375
- w_const: bfloat16 [768, 4], P('shard'), may hold values from -0.21875 to 0.21875
- const_vec: bfloat16 [2, 768], P(None, 'shard'), may hold values from -5 to 5
- w_gate: bfloat16 [8, 768, 2048], P(None, 'shard', 'tp'), may hold values from -0.21875 to 0.21875
- w_up: bfloat16 [8, 768, 2048], P(None, 'shard', 'tp'), may hold values from -0.21875 to 0.21875
- w_down: bfloat16 [8, 768, 2048], P(None, 'shard', 'tp'), may hold values from -0.125 to 0.125
- threshold: float32 [1], replicated, may hold values from 0.5 to 1.5
Outputs:
- output: bfloat16 [16384, 768], P(('shard', 'ctx', 'tp'))
- grad_input: float32 [16384, 768], P(('shard', 'ctx', 'tp'))
- grad_norm_attn: float32 [768], P('shard')
- grad_w_query: float32 [768, 768], P('shard', 'tp')
- grad_w_key: float32 [768, 768], P('shard', 'tp')
- grad_w_value: float32 [768, 768], P('shard', 'tp')
- grad_w_out: float32 [768, 768], P('tp', 'shard')
- grad_norm_moe: float32 [768], P('shard')
- grad_w_router: float32 [768, 12], P('shard')
- grad_w_const: float32 [768, 4], P('shard')
- grad_const_vec: float32 [2, 768], P(None, 'shard')
- grad_w_gate: float32 [8, 768, 2048], P(None, 'shard', 'tp')
- grad_w_up: float32 [8, 768, 2048], P(None, 'shard', 'tp')
- grad_w_down: float32 [8, 768, 2048], P(None, 'shard', 'tp')
- clip_factors: float32 [12], P('tp')
- clipped_query: bfloat16 [768, 768], P('shard', 'tp')
- clipped_key: bfloat16 [768, 768], P('shard', 'tp')
Inputs may be any that keep to these rules, and one draw needn't show every extreme that they name: `lengths`: valid length of each sequence; some sequence is full (4096) in every draw. `routes`: each row names two different experts; in each aligned block of 2048 rows no expert is named by more than 512 rows, a bound that some block reaches.
All inputs are finite; a program needn't handle non-finite values.
Results may differ from a plain program's by a relative error of at most 0.013.
Values may be sent and summed in bfloat16 or wider, within the bound.
A program may use at most 320 MiB of HBM per device.

v0:
```python
import jax
import jax.numpy as jnp
from jax import lax
from jax.sharding import PartitionSpec as P

HEAD_DIM = 64
EXPERTS = 12
FFN_EXPERTS = 8
CAP = 512
QBLOCK = 512


epsilon = 1e-06
highest = lax.Precision.HIGHEST
rope_base = 10000.0


def product(left, right):
    return jnp.dot(left, right, precision=highest)


def rms_norm(values, gain):
    return values * lax.rsqrt(jnp.mean(values * values, axis=-1, keepdims=True) + epsilon) * gain


def angle_tables(positions, width):
    half = width // 2
    freqs = rope_base ** (-2.0 * jnp.arange(half).astype(jnp.float32) / width)
    angles = positions.astype(jnp.float32)[:, None] * freqs[None, :]
    return (jnp.cos(angles)[:, None, :], jnp.sin(angles)[:, None, :])


def rotate(values, positions):
    half = values.shape[-1] // 2
    cosine, sine = angle_tables(positions, values.shape[-1])
    first = values[..., :half]
    second = values[..., half:]
    return jnp.concatenate(
        [first * cosine - second * sine, second * cosine + first * sine], axis=-1
    )


def unrotate(grads, positions):
    half = grads.shape[-1] // 2
    cosine, sine = angle_tables(positions, grads.shape[-1])
    first = grads[..., :half]
    second = grads[..., half:]
    return jnp.concatenate(
        [first * cosine + second * sine, second * cosine - first * sine], axis=-1
    )


def mixture(normed, router, const_weights, const_vectors, previous, chosen):
    logits = product(normed, router) + previous
    picked = jnp.take_along_axis(logits, chosen, axis=1)
    gates = jax.nn.softmax(picked, axis=-1)
    experts = jnp.arange(EXPERTS)
    combine = jnp.sum(
        gates[:, :, None] * (chosen[:, :, None] == experts[None, None, :]).astype(jnp.float32),
        axis=1,
    )
    mixed = combine[:, FFN_EXPERTS + 1 : FFN_EXPERTS + 2] * normed
    for which in range(2):
        alphas = jax.nn.softmax(
            product(normed, const_weights[:, 2 * which : 2 * which + 2]), axis=-1
        )
        column = FFN_EXPERTS + 2 + which
        mixed = mixed + combine[:, column : column + 1] * (
            alphas[:, :1] * normed + alphas[:, 1:] * const_vectors[which][None, :]
        )
    return (gates, mixed)


def shards(
    hidden_in,
    cotangent,
    lengths,
    routes,
    prev_logits,
    norm_attn,
    w_query,
    w_key,
    w_value,
    w_out,
    norm_moe,
    w_router,
    w_const,
    const_vec,
    w_gate,
    w_up,
    w_down,
    threshold,
):
    rows_whole, cot_whole = (
        lax.all_gather(hidden_in, "tp", axis=0, tiled=True),
        lax.all_gather(cotangent, "tp", axis=0, tiled=True),
    )
    (
        gain_attn,
        query_w,
        key_w,
        value_w,
        out_w,
        gain_moe,
        router_w,
        const_w,
        const_v,
        gate_w,
        up_w,
        down_w,
    ) = (
        lax.all_gather(norm_attn, "shard", axis=0, tiled=True),
        lax.all_gather(w_query, "shard", axis=0, tiled=True),
        lax.all_gather(w_key, "shard", axis=0, tiled=True),
        lax.all_gather(w_value, "shard", axis=0, tiled=True),
        lax.all_gather(w_out, "shard", axis=1, tiled=True),
        lax.all_gather(norm_moe, "shard", axis=0, tiled=True),
        lax.all_gather(w_router, "shard", axis=0, tiled=True),
        lax.all_gather(w_const, "shard", axis=0, tiled=True),
        lax.all_gather(const_vec, "shard", axis=1, tiled=True),
        lax.all_gather(w_gate, "shard", axis=1, tiled=True),
        lax.all_gather(w_up, "shard", axis=1, tiled=True),
        lax.all_gather(w_down, "shard", axis=1, tiled=True),
    )
    tokens = rows_whole.shape[0]
    width = rows_whole.shape[1]
    local_heads = query_w.shape[1] // HEAD_DIM
    seq_total = tokens * lax.axis_size("ctx")
    positions = lax.axis_index("ctx") * tokens + jnp.arange(tokens, dtype=jnp.int32)
    key_positions = jnp.arange(seq_total, dtype=jnp.int32)
    length = lengths[0]
    valid = positions < length
    mask = valid[:, None].astype(jnp.float32)
    key_valid = key_positions < length
    scale = HEAD_DIM ** (-0.5)
    head_shape = (tokens, local_heads, HEAD_DIM)
    slots = FFN_EXPERTS * CAP
    inputs = rows_whole.astype(jnp.float32)
    normed, norm_attn_back = jax.vjp(rms_norm, inputs, gain_attn.astype(jnp.float32))
    lowered = normed.astype(jnp.bfloat16)
    query = rotate(
        jnp.dot(lowered, query_w, preferred_element_type=jnp.float32).reshape(head_shape), positions
    ).astype(jnp.bfloat16)
    key_own = rotate(
        jnp.dot(lowered, key_w, preferred_element_type=jnp.float32).reshape(head_shape), positions
    ).astype(jnp.bfloat16)
    value_own = (
        jnp.dot(lowered, value_w, preferred_element_type=jnp.float32)
        .astype(jnp.bfloat16)
        .reshape(head_shape)
    )
    keys, values = (
        lax.all_gather(key_own, "ctx", axis=0, tiled=True),
        lax.all_gather(value_own, "ctx", axis=0, tiled=True),
    )

    def allowed_for(rows_here):
        return (key_positions[None, :] <= rows_here[:, None]) & key_valid[None, :]

    def attend(start):
        block = lax.dynamic_slice_in_dim(query, start, QBLOCK, 0)
        scores = jnp.einsum("qhd,khd->hqk", block, keys, preferred_element_type=jnp.float32) * scale
        rows_here = lax.dynamic_slice_in_dim(positions, start, QBLOCK, 0)
        allowed = allowed_for(rows_here)
        masked = jnp.where(allowed[None], scores, -1e30)
        peak = jnp.max(masked, axis=-1, keepdims=True)
        weights = jnp.exp(masked - peak)
        total = jnp.sum(weights, axis=-1, keepdims=True)
        probs = (weights / total).astype(jnp.bfloat16)
        mixed = jnp.einsum("hqk,khd->qhd", probs, values, preferred_element_type=jnp.float32)
        counted = allowed & (rows_here < length)[:, None]
        largest = jnp.max(jnp.where(counted[None], scores, -1e30), axis=(1, 2))
        return (mixed, (peak + jnp.log(total))[..., 0], largest)

    starts = jnp.arange(tokens // QBLOCK, dtype=jnp.int32) * QBLOCK
    mixed_all, log_totals, largest = lax.map(attend, starts)
    head_max = lax.pmax(jnp.max(largest, axis=0), ("shard", "ctx"))
    factors = threshold[0] / jnp.maximum(head_max, threshold[0])
    root = jnp.repeat(jnp.sqrt(factors), HEAD_DIM)
    clipped_query = (w_query.astype(jnp.float32) * root[None, :]).astype(jnp.bfloat16)
    clipped_key = (w_key.astype(jnp.float32) * root[None, :]).astype(jnp.bfloat16)
    attended = mixed_all.reshape(tokens, local_heads * HEAD_DIM).astype(jnp.bfloat16)
    attn_part = jnp.dot(attended, out_w, preferred_element_type=jnp.float32)
    residual = inputs + lax.psum(attn_part, "tp")
    normed_moe, norm_moe_back = jax.vjp(rms_norm, residual, gain_moe.astype(jnp.float32))
    lowered_moe = normed_moe.astype(jnp.bfloat16)

    def mixing(normed_in, router_in, const_in, vector_in):
        return mixture(normed_in, router_in, const_in, vector_in, prev_logits, routes)

    (gates, others), mix_back = jax.vjp(
        mixing,
        normed_moe,
        router_w.astype(jnp.float32),
        const_w.astype(jnp.float32),
        const_v.astype(jnp.float32),
    )
    flat_experts = routes.reshape(-1)
    assignments = flat_experts.shape[0]
    chosen = (flat_experts[:, None] == jnp.arange(EXPERTS)[None, :]).astype(jnp.int32)
    earlier = jnp.sum((jnp.cumsum(chosen, axis=0) - chosen) * chosen, axis=1)
    target = jnp.where(flat_experts < FFN_EXPERTS, flat_experts * CAP + earlier, slots)
    order = jnp.arange(assignments, dtype=jnp.int32)
    slot_source = jnp.zeros((slots + 1,), jnp.int32).at[target].set(order)[:slots]
    slot_used = jnp.zeros((slots + 1,), jnp.float32).at[target].set(1.0)[:slots]
    slot_token = slot_source // 2
    expert_in = lowered_moe[slot_token].reshape(FFN_EXPERTS, CAP, width)
    gate_pre = jnp.einsum("ecd,edf->ecf", expert_in, gate_w, preferred_element_type=jnp.float32)
    up_pre = jnp.einsum("ecd,edf->ecf", expert_in, up_w, preferred_element_type=jnp.float32)
    activated = jax.nn.silu(gate_pre)
    inner = (activated * up_pre).astype(jnp.bfloat16)
    expert_out = jnp.einsum("ecf,edf->ecd", inner, down_w, preferred_element_type=jnp.float32)
    expert_out_flat = expert_out.reshape(slots, width)
    padded_out = jnp.concatenate([expert_out_flat, jnp.zeros((1, width), jnp.float32)], axis=0)
    per_assign = padded_out[target].reshape(tokens, 2, width)
    feed_part = jnp.sum(gates[:, :, None] * per_assign, axis=1)
    feed_slice = lax.psum_scatter(
        feed_part.astype(jnp.bfloat16), "tp", scatter_dimension=0, tiled=True
    ).astype(jnp.float32)
    slice_rows = tokens // lax.axis_size("tp")
    first_row = lax.axis_index("tp") * slice_rows

    def own_rows(array):
        return lax.dynamic_slice_in_dim(array, first_row, slice_rows, 0)

    output = (own_rows(mask) * (own_rows(residual) + own_rows(others) + feed_slice)).astype(
        jnp.bfloat16
    )
    query_w, key_w, value_w, out_w = (
        lax.all_gather(w_query, "shard", axis=0, tiled=True),
        lax.all_gather(w_key, "shard", axis=0, tiled=True),
        lax.all_gather(w_value, "shard", axis=0, tiled=True),
        lax.all_gather(w_out, "shard", axis=1, tiled=True),
    )
    upstream = mask * cot_whole.astype(jnp.float32)
    grad_gates_part = jnp.sum(per_assign * upstream[:, None, :], axis=2)
    grad_assign = (gates.reshape(-1)[:, None] * jnp.repeat(upstream, 2, axis=0)).astype(
        jnp.bfloat16
    )
    grad_slots = jnp.where(slot_used[:, None] > 0, grad_assign[slot_source], 0).reshape(
        FFN_EXPERTS, CAP, width
    )
    grad_down_w = jnp.einsum("ecd,ecf->edf", grad_slots, inner, preferred_element_type=jnp.float32)
    grad_inner = jnp.einsum("ecd,edf->ecf", grad_slots, down_w, preferred_element_type=jnp.float32)
    sigmoid = jax.nn.sigmoid(gate_pre)
    grad_gate_pre = (grad_inner * up_pre * sigmoid * (1.0 + gate_pre * (1.0 - sigmoid))).astype(
        jnp.bfloat16
    )
    grad_up_pre = (grad_inner * activated).astype(jnp.bfloat16)
    grad_gate_w = jnp.einsum(
        "ecd,ecf->edf", expert_in, grad_gate_pre, preferred_element_type=jnp.float32
    )
    grad_up_w = jnp.einsum(
        "ecd,ecf->edf", expert_in, grad_up_pre, preferred_element_type=jnp.float32
    )
    grad_expert_in = jnp.einsum(
        "ecf,edf->ecd", grad_gate_pre, gate_w, preferred_element_type=jnp.float32
    ) + jnp.einsum("ecf,edf->ecd", grad_up_pre, up_w, preferred_element_type=jnp.float32)
    grad_expert_flat = grad_expert_in.reshape(slots, width)
    grad_normed_part = (
        jnp.zeros((tokens, width), jnp.float32)
        .at[slot_token]
        .add(grad_expert_flat * slot_used[:, None])
    )
    grad_normed_ffn, grad_gates = lax.psum((grad_normed_part, grad_gates_part), "tp")
    grad_normed_mix, grad_router, grad_const, grad_vectors = mix_back((grad_gates, upstream))
    grad_residual_norm, grad_gain_moe = norm_moe_back(grad_normed_ffn + grad_normed_mix)
    grad_residual = upstream + grad_residual_norm
    grad_attn = grad_residual.astype(jnp.bfloat16)
    grad_out_w = jnp.dot(attended.T, grad_attn, preferred_element_type=jnp.float32)
    grad_attended = (
        jnp.dot(grad_attn, out_w.T, preferred_element_type=jnp.float32)
        .astype(jnp.bfloat16)
        .reshape(head_shape)
    )

    def revisit(carry, step_input):
        key_total, value_total = carry
        start, log_total = step_input
        block = lax.dynamic_slice_in_dim(query, start, QBLOCK, 0)
        grad_block = lax.dynamic_slice_in_dim(grad_attended, start, QBLOCK, 0)
        scores = jnp.einsum("qhd,khd->hqk", block, keys, preferred_element_type=jnp.float32) * scale
        allowed = allowed_for(lax.dynamic_slice_in_dim(positions, start, QBLOCK, 0))
        probs = jnp.where(allowed[None], jnp.exp(scores - log_total[..., None]), 0.0)
        grad_probs = jnp.einsum(
            "qhd,khd->hqk", grad_block, values, preferred_element_type=jnp.float32
        )
        centre = jnp.sum(probs * grad_probs, axis=-1, keepdims=True)
        grad_scores = (probs * (grad_probs - centre) * scale).astype(jnp.bfloat16)
        grad_query = jnp.einsum(
            "hqk,khd->qhd", grad_scores, keys, preferred_element_type=jnp.float32
        )
        key_total = key_total + jnp.einsum(
            "hqk,qhd->khd", grad_scores, block, preferred_element_type=jnp.float32
        )
        value_total = value_total + jnp.einsum(
            "hqk,qhd->khd",
            probs.astype(jnp.bfloat16),
            grad_block,
            preferred_element_type=jnp.float32,
        )
        return ((key_total, value_total), grad_query)

    empty = jnp.zeros((seq_total, local_heads, HEAD_DIM), jnp.float32)
    (key_total, value_total), grad_queries = lax.scan(revisit, (empty, empty), (starts, log_totals))
    grad_keys, grad_values = (
        lax.psum_scatter(key_total, "ctx", scatter_dimension=0, tiled=True),
        lax.psum_scatter(value_total, "ctx", scatter_dimension=0, tiled=True),
    )
    flat_shape = (tokens, local_heads * HEAD_DIM)
    grad_query_pre = (
        unrotate(grad_queries.reshape(head_shape), positions)
        .astype(jnp.bfloat16)
        .reshape(flat_shape)
    )
    grad_key_pre = unrotate(grad_keys, positions).astype(jnp.bfloat16).reshape(flat_shape)
    grad_value_pre = grad_values.astype(jnp.bfloat16).reshape(flat_shape)
    grad_query_w = jnp.dot(lowered.T, grad_query_pre, preferred_element_type=jnp.float32)
    grad_key_w = jnp.dot(lowered.T, grad_key_pre, preferred_element_type=jnp.float32)
    grad_value_w = jnp.dot(lowered.T, grad_value_pre, preferred_element_type=jnp.float32)
    grad_lowered_part = (
        jnp.dot(grad_query_pre, query_w.T, preferred_element_type=jnp.float32)
        + jnp.dot(grad_key_pre, key_w.T, preferred_element_type=jnp.float32)
        + jnp.dot(grad_value_pre, value_w.T, preferred_element_type=jnp.float32)
    )
    grad_normed_attn = lax.psum(grad_lowered_part, "tp")
    grad_inputs_norm, grad_gain_attn = norm_attn_back(grad_normed_attn)
    grad_input = own_rows(grad_residual + grad_inputs_norm)
    summed = (
        lax.psum_scatter(grad_gain_attn, ("shard", "ctx"), scatter_dimension=0, tiled=True),
        lax.psum_scatter(grad_query_w, ("shard", "ctx"), scatter_dimension=0, tiled=True),
        lax.psum_scatter(grad_key_w, ("shard", "ctx"), scatter_dimension=0, tiled=True),
        lax.psum_scatter(grad_value_w, ("shard", "ctx"), scatter_dimension=0, tiled=True),
        lax.psum_scatter(grad_out_w, ("shard", "ctx"), scatter_dimension=1, tiled=True),
        lax.psum_scatter(grad_gain_moe, ("shard", "ctx"), scatter_dimension=0, tiled=True),
        lax.psum_scatter(grad_router, ("shard", "ctx"), scatter_dimension=0, tiled=True),
        lax.psum_scatter(grad_const, ("shard", "ctx"), scatter_dimension=0, tiled=True),
        lax.psum_scatter(grad_vectors, ("shard", "ctx"), scatter_dimension=1, tiled=True),
        lax.psum_scatter(grad_gate_w, ("shard", "ctx"), scatter_dimension=1, tiled=True),
        lax.psum_scatter(grad_up_w, ("shard", "ctx"), scatter_dimension=1, tiled=True),
        lax.psum_scatter(grad_down_w, ("shard", "ctx"), scatter_dimension=1, tiled=True),
    )
    sharded = (
        lax.all_gather(summed[0], "ctx", axis=0, tiled=True),
        lax.all_gather(summed[1], "ctx", axis=0, tiled=True),
        lax.all_gather(summed[2], "ctx", axis=0, tiled=True),
        lax.all_gather(summed[3], "ctx", axis=0, tiled=True),
        lax.all_gather(summed[4], "ctx", axis=1, tiled=True),
        lax.all_gather(summed[5], "ctx", axis=0, tiled=True),
        lax.all_gather(summed[6], "ctx", axis=0, tiled=True),
        lax.all_gather(summed[7], "ctx", axis=0, tiled=True),
        lax.all_gather(summed[8], "ctx", axis=1, tiled=True),
        lax.all_gather(summed[9], "ctx", axis=1, tiled=True),
        lax.all_gather(summed[10], "ctx", axis=1, tiled=True),
        lax.all_gather(summed[11], "ctx", axis=1, tiled=True),
    )
    return (
        output,
        grad_input,
        sharded[0],
        sharded[1],
        sharded[2],
        sharded[3],
        sharded[4],
        sharded[5],
        sharded[6],
        sharded[7],
        sharded[8],
        sharded[9],
        sharded[10],
        sharded[11],
        factors,
        clipped_query,
        clipped_key,
    )


def solution(mesh):
    return jax.shard_map(
        shards,
        mesh=mesh,
        in_specs=(
            P(("shard", "ctx", "tp"), None),
            P(("shard", "ctx", "tp"), None),
            P("shard"),
            P(("shard", "ctx"), None),
            P(("shard", "ctx"), None),
            P("shard"),
            P("shard", "tp"),
            P("shard", "tp"),
            P("shard", "tp"),
            P("tp", "shard"),
            P("shard"),
            P("shard", None),
            P("shard", None),
            P(None, "shard"),
            P(None, "shard", "tp"),
            P(None, "shard", "tp"),
            P(None, "shard", "tp"),
            P(),
        ),
        out_specs=(
            P(("shard", "ctx", "tp"), None),
            P(("shard", "ctx", "tp"), None),
            P("shard"),
            P("shard", "tp"),
            P("shard", "tp"),
            P("shard", "tp"),
            P("tp", "shard"),
            P("shard"),
            P("shard", None),
            P("shard", None),
            P(None, "shard"),
            P(None, "shard", "tp"),
            P(None, "shard", "tp"),
            P(None, "shard", "tp"),
            P("tp"),
            P("shard", "tp"),
            P("shard", "tp"),
        ),
        check_vma=False,
    )
```

profile of v0, /device:TPU:0, one launch (start us, length us, event | category | flops | bytes accessed | tf_op | source)
XLA Modules:
  0.0 2484.3 jit_solution(16169166722357812203)
XLA Ops:
  103.7 197.9 %while.32 = (s32[]{:T(128)}, bf16[4,512,3,64]{1,3,2,0:T(8,128)(2,1)S(1)}, f32[4,3,512]{2,1,0:T(4,128)}, f32[4,3]{1,0:T(4,128)}, s32[4]{0:T(128)S(1)}, /*index=5*...) while((s32[]{:T(128)}, ...), condition=%wide.region_5.6_spmd.clone.clone, body=%wide.region_1.5_spmd.clone.clone.sunk | while | flops 1704987648 | bytes 91886832 | solution.py:176
  401.9 43.3 %all-reduce.25.cloned.1.call-done = f32[2048,768]{1,0:T(8,128)} async-done(((f32[2048,768]{1,0:T(8,128)}), f32[2048,768]{1,0:T(8,128)}) %all-reduce.25.cloned.1.call-update) | async-done | bytes 6291472 | tf_op jit(solution)/shard_map/psum | solution.py:184
  458.0 33.2 %gather_fusion.3 = f32[4096]{0:T(1024)S(1)} fusion(f32[2048,12]{0,1:T(8,128)S(1)} %convolution_add_fusion.1, s32[4096]{0:T(1024)S(1)} %reshape.608), kind=kCustom, calls=%fused_computation.3 | custom fusion | bytes 65536 | tf_op jit(solution)/shard_map/jvp(jit(take_along_axis))/gather | solution.py:55
  551.9 22.8 gather_fusion.2
  583.5 17.8 gather_fusion
  619.3 103.6 %all-gather.25.cloned.1.call-done = bf16[8,768,512]{2,1,0:T(8,128)(2,1)} async-done(((bf16[8,192,512]{2,1,0:T(8,128)(2,1)}), bf16[8,768,512]{2,1,0:T(8,128)(2,1)}) %all-gather.25.cloned.1.call-update) | async-done | bytes 6291472 | tf_op jit(solution)/shard_map/all_gather | solution.py:122
  734.4 103.6 %all-gather.27.cloned.1.call-done = bf16[8,768,512]{2,1,0:T(8,128)(2,1)} async-done(((bf16[8,192,512]{2,1,0:T(8,128)(2,1)}), bf16[8,768,512]{2,1,0:T(8,128)(2,1)}) %all-gather.27.cloned.1.call-update) | async-done | bytes 6291472 | tf_op jit(solution)/shard_map/all_gather | solution.py:123
  891.6 31.2 %scatter_custom_fusion.2 = f32[2048,768]{1,0:T(8,128)} fusion(s32[4096]{0:T(1024)} %get-tuple-element.439, f32[4096,768]{1,0:T(8,128)} %bitcast_multiply_fusion, f32[]{:T(128)} %constant.76.clone.1), kind=kCustom, calls=%fused_computation.117 | custom fusion | flops 3145728 | bytes 6291968 | tf_op jit(solution)/shard_map/scatter-add | solution.py:263
  947.8 25.0 %gather_fusion.1 = f32[4096,768]{1,0:T(8,128)} fusion(f32[4097,768]{1,0:T(8,128)} %concatenate.21, s32[4096]{0:T(1024)S(1)} %broadcast_clamp_fusion), kind=kCustom, calls=%fused_computation.1 | custom fusion | bytes 25182208 | tf_op jit(solution)/shard_map/gather | solution.py:215
  988.3 31.8 %multiply_reduce_fusion.1 = (f32[2048,2]{1,0:T(8,128)S(1)}, bf16[2048,768]{1,0:T(8,128)(2,1)}) fusion(f32[2048,2,768]{2,1,0:T(2,128)} %reshape.565, f32[2048,768]{1,0:T(8,128)} %copy-done.7, f32[2048,2]{1,0:T(8,128)S(1)} %copy-done.14), kind=kLoop, calls=%fused_computation.75 | loop fusion | flops 11005952 | bytes 22052864 | tf_op jit(solution)/shard_map/reduce_sum | solution.py:236
  1020.4 17.0 psum.30
  1038.6 21.9 scatter_custom_fusion.3
  1090.7 508.3 %while.31 = (s32[]{:T(128)}, f32[4096,3,64]{0,2,1:T(8,128)}, f32[4096,3,64]{0,2,1:T(8,128)}, f32[4,512,3,64]{1,0,3,2:T(4,128)}, s32[4]{0:T(128)S(1)}, /*index=5*...) while((s32[]{:T(128)}, f32[4096,3,64]{0,2,1:T(8,128)}, ...), condition=%wide.region_41.42_spmd.clone, body=%wide.region_39.41_spmd.clone.sunk | while | flops 4197465088 | bytes 257089776 | solution.py:305
  1122.4 37.1 %fusion.247 = f32[4096,3,64]{0,2,1:T(8,128)} fusion(f32[3,512,4096]{2,1,0:T(8,128)} %fusion.244, f32[3,512,4096]{2,1,0:T(8,128)} %fusion.245, f32[3,512]{1,0:T(4,128)S(1)} %dynamic-slice_bitcast_fusion.2, pred[512,4096]{1,0:T(8,128)(4,1)S(1)} %fusion.246, f32[4096,3,64]{0,2,1:T(8,128)} %get-tuple-element.690, pred[]{:T(512)S(6)} %compare.21, ...), kind=kOutput, calls=%fused_computation.34.clone.1 | convolution fusion | flops 876090880 | bytes 111362056 | tf_op jit(solution)/shard_map/while/body/eval_jaxpr/hqk,qhd->khd/dot_general | solution.py:293
  1172.6 34.9 %fusion.249 = f32[1,512,3,64]{1,3,2,0:T(8,128)S(1)} fusion(bf16[4096,3,64]{0,2,1:T(8,128)(2,1)} %get-tuple-element.711, f32[3,512,4096]{2,1,0:T(8,128)} %fusion.244, f32[3,512,4096]{2,1,0:T(8,128)} %fusion.245, f32[3,512]{1,0:T(4,128)S(1)} %dynamic-slice_bitcast_fusion.2, pred[512,4096]{1,0:T(8,128)(4,1)S(1)} %fusion.246), kind=kOutput, calls=%fused_computation.36.clone.1 | convolution fusion | flops 874518016 | bytes 54401024 | tf_op jit(solution)/shard_map/while/body/eval_jaxpr/hqk,khd->qhd/dot_general | solution.py:290
  1248.1 37.8 %fusion.247 = f32[4096,3,64]{0,2,1:T(8,128)} fusion(f32[3,512,4096]{2,1,0:T(8,128)} %fusion.244, f32[3,512,4096]{2,1,0:T(8,128)} %fusion.245, f32[3,512]{1,0:T(4,128)S(1)} %dynamic-slice_bitcast_fusion.2, pred[512,4096]{1,0:T(8,128)(4,1)S(1)} %fusion.246, f32[4096,3,64]{0,2,1:T(8,128)} %get-tuple-element.690, pred[]{:T(512)S(6)} %compare.21, ...), kind=kOutput, calls=%fused_computation.34.clone.1 | convolution fusion | flops 876090880 | bytes 111362056 | tf_op jit(solution)/shard_map/while/body/eval_jaxpr/hqk,qhd->khd/dot_general | solution.py:293
  1299.9 34.9 %fusion.249 = f32[1,512,3,64]{1,3,2,0:T(8,128)S(1)} fusion(bf16[4096,3,64]{0,2,1:T(8,128)(2,1)} %get-tuple-element.711, f32[3,512,4096]{2,1,0:T(8,128)} %fusion.244, f32[3,512,4096]{2,1,0:T(8,128)} %fusion.245, f32[3,512]{1,0:T(4,128)S(1)} %dynamic-slice_bitcast_fusion.2, pred[512,4096]{1,0:T(8,128)(4,1)S(1)} %fusion.246), kind=kOutput, calls=%fused_computation.36.clone.1 | convolution fusion | flops 874518016 | bytes 54401024 | tf_op jit(solution)/shard_map/while/body/eval_jaxpr/hqk,khd->qhd/dot_general | solution.py:290
  1375.3 38.0 %fusion.247 = f32[4096,3,64]{0,2,1:T(8,128)} fusion(f32[3,512,4096]{2,1,0:T(8,128)} %fusion.244, f32[3,512,4096]{2,1,0:T(8,128)} %fusion.245, f32[3,512]{1,0:T(4,128)S(1)} %dynamic-slice_bitcast_fusion.2, pred[512,4096]{1,0:T(8,128)(4,1)S(1)} %fusion.246, f32[4096,3,64]{0,2,1:T(8,128)} %get-tuple-element.690, pred[]{:T(512)S(6)} %compare.21, ...), kind=kOutput, calls=%fused_computation.34.clone.1 | convolution fusion | flops 876090880 | bytes 111362056 | tf_op jit(solution)/shard_map/while/body/eval_jaxpr/hqk,qhd->khd/dot_general | solution.py:293
  1427.3 34.9 %fusion.249 = f32[1,512,3,64]{1,3,2,0:T(8,128)S(1)} fusion(bf16[4096,3,64]{0,2,1:T(8,128)(2,1)} %get-tuple-element.711, f32[3,512,4096]{2,1,0:T(8,128)} %fusion.244, f32[3,512,4096]{2,1,0:T(8,128)} %fusion.245, f32[3,512]{1,0:T(4,128)S(1)} %dynamic-slice_bitcast_fusion.2, pred[512,4096]{1,0:T(8,128)(4,1)S(1)} %fusion.246), kind=kOutput, calls=%fused_computation.36.clone.1 | convolution fusion | flops 874518016 | bytes 54401024 | tf_op jit(solution)/shard_map/while/body/eval_jaxpr/hqk,khd->qhd/dot_general | solution.py:290
  1502.8 37.8 %fusion.247 = f32[4096,3,64]{0,2,1:T(8,128)} fusion(f32[3,512,4096]{2,1,0:T(8,128)} %fusion.244, f32[3,512,4096]{2,1,0:T(8,128)} %fusion.245, f32[3,512]{1,0:T(4,128)S(1)} %dynamic-slice_bitcast_fusion.2, pred[512,4096]{1,0:T(8,128)(4,1)S(1)} %fusion.246, f32[4096,3,64]{0,2,1:T(8,128)} %get-tuple-element.690, pred[]{:T(512)S(6)} %compare.21, ...), kind=kOutput, calls=%fused_computation.34.clone.1 | convolution fusion | flops 876090880 | bytes 111362056 | tf_op jit(solution)/shard_map/while/body/eval_jaxpr/hqk,qhd->khd/dot_general | solution.py:293
  1554.6 34.9 %fusion.249 = f32[1,512,3,64]{1,3,2,0:T(8,128)S(1)} fusion(bf16[4096,3,64]{0,2,1:T(8,128)(2,1)} %get-tuple-element.711, f32[3,512,4096]{2,1,0:T(8,128)} %fusion.244, f32[3,512,4096]{2,1,0:T(8,128)} %fusion.245, f32[3,512]{1,0:T(4,128)S(1)} %dynamic-slice_bitcast_fusion.2, pred[512,4096]{1,0:T(8,128)(4,1)S(1)} %fusion.246), kind=kOutput, calls=%fused_computation.36.clone.1 | convolution fusion | flops 874518016 | bytes 54401024 | tf_op jit(solution)/shard_map/while/body/eval_jaxpr/hqk,khd->qhd/dot_general | solution.py:290
  1696.3 57.6 %reduce-scatter.34.cloned.1.call-done = f32[8,96,512]{2,1,0:T(8,128)} async-done(((f32[8,768,512]{2,1,0:T(8,128)}), f32[8,96,512]{2,1,0:T(8,128)}) %reduce-scatter.34.cloned.1.call-update) | async-done | bytes 1572880 | tf_op jit(solution)/shard_map/reduce_scatter | solution.py:339
  1754.0 129.8 %reduce-scatter.36.cloned.1.call-done = f32[8,96,512]{2,1,0:T(8,128)} async-done(((f32[8,768,512]{2,1,0:T(8,128)}), f32[8,96,512]{2,1,0:T(8,128)}) %reduce-scatter.36.cloned.1.call-update) | async-done | bytes 1572880 | tf_op jit(solution)/shard_map/reduce_scatter | solution.py:340
  1883.9 129.7 %reduce-scatter.38.cloned.1.call-done = f32[8,96,512]{2,1,0:T(8,128)} async-done(((f32[8,768,512]{2,1,0:T(8,128)}), f32[8,96,512]{2,1,0:T(8,128)}) %reduce-scatter.38.cloned.1.call-update) | async-done | bytes 1572880 | tf_op jit(solution)/shard_map/reduce_scatter | solution.py:341
  2048.1 27.9 %reduce-scatter.44.cloned.1.call-done = f32[96,4]{1,0:T(8,128)} async-done(((f32[768,4]{1,0:T(8,128)}), f32[96,4]{1,0:T(8,128)}) %reduce-scatter.44.cloned.1.call-update) | async-done | bytes 1552
  2079.3 27.5 %reduce-scatter.42.cloned.1.call-done = f32[96,12]{1,0:T(8,128)} async-done(((f32[768,12]{1,0:T(8,128)}), f32[96,12]{1,0:T(8,128)}) %reduce-scatter.42.cloned.1.call-update) | async-done | bytes 4624
  2110.2 42.5 %reduce-scatter.22.cloned.1.call-done = bf16[512,768]{1,0:T(8,128)(2,1)} async-done(((bf16[2048,768]{1,0:T(8,128)(2,1)}), bf16[512,768]{1,0:T(8,128)(2,1)}) %reduce-scatter.22.cloned.1.call-update) | async-done | bytes 786448 | tf_op jit(solution)/shard_map/reduce_scatter | solution.py:217
  2157.2 29.4 %reduce-scatter.40.cloned.1.call-done = f32[96,192]{1,0:T(8,128)} async-done(((f32[768,192]{1,0:T(8,128)}), f32[96,192]{1,0:T(8,128)}) %reduce-scatter.40.cloned.1.call-update) | async-done | bytes 73744
  2189.6 29.0 %reduce-scatter.28.cloned.1.call-done = f32[96,192]{1,0:T(8,128)} async-done(((f32[768,192]{1,0:T(8,128)}), f32[96,192]{1,0:T(8,128)}) %reduce-scatter.28.cloned.1.call-update) | async-done | bytes 73744 | tf_op jit(solution)/shard_map/reduce_scatter | solution.py:331
  2220.7 30.1 %reduce-scatter.30.cloned.1.call-done = f32[96,192]{1,0:T(8,128)} async-done(((f32[768,192]{1,0:T(8,128)}), f32[96,192]{1,0:T(8,128)}) %reduce-scatter.30.cloned.1.call-update) | async-done | bytes 73744 | tf_op jit(solution)/shard_map/reduce_scatter | solution.py:332
  2253.0 30.5 %reduce-scatter.32.cloned.1.call-done = f32[96,192]{1,0:T(8,128)} async-done(((f32[768,192]{1,0:T(8,128)}), f32[96,192]{1,0:T(8,128)}) %reduce-scatter.32.cloned.1.call-update) | async-done | bytes 73744 | tf_op jit(solution)/shard_map/reduce_scatter | solution.py:333
  2286.9 137.0 %all-reduce.29.cloned.1.call-done = f32[2048,768]{1,0:T(8,128)} async-done(((f32[2048,768]{1,0:T(8,128)}), f32[2048,768]{1,0:T(8,128)}) %all-reduce.29.cloned.1.call-update) | async-done | bytes 6291472 | tf_op jit(solution)/shard_map/psum | solution.py:326
  (619 shorter events, 1035.1 us)
Async XLA Ops:
  7.2 50.3 %all-gather.17.cloned.1.call-start = ((), (), s32[]{:S(2)}) async-start(), calls=%async_computation.13 | async-start | bytes 3932160 | tf_op jit(solution)/shard_map/all_gather | solution.py:95
  7.9 95.7 %all-gather.19.cloned.1.call-start = ((), (), s32[]{:S(2)}) async-start(), calls=%async_computation.14 | async-start | bytes 2359296 | tf_op jit(solution)/shard_map/all_gather | solution.py:153
  68.0 35.7 %all-gather.21.cloned.1.call-start = ((), (), s32[]{:S(2)}) async-start(), calls=%async_computation.15 | async-start | bytes 2359296 | tf_op jit(solution)/shard_map/all_gather | solution.py:154
  84.8 360.4 %all-reduce.25.cloned.1.call-start = ((), (), s32[]{:S(2)}) async-start(), calls=%async_computation.16 | async-start | bytes 12582912 | tf_op jit(solution)/shard_map/psum | solution.py:184
  307.1 197.4 %all-gather.29.cloned.1.call-start = ((), (), s32[]{:S(2)}) async-start(), calls=%async_computation.21 | async-start | bytes 3932160 | tf_op jit(solution)/shard_map/all_gather | solution.py:96
  307.7 300.1 %all-gather.23.cloned.1.call-start = ((), (), s32[]{:S(2)}) async-start(), calls=%async_computation.17 | async-start | bytes 7864320 | tf_op jit(solution)/shard_map/all_gather | solution.py:121
  308.3 414.6 %all-gather.25.cloned.1.call-start = ((), (), s32[]{:S(2)}) async-start(), calls=%async_computation.18 | async-start | bytes 7864320 | tf_op jit(solution)/shard_map/all_gather | solution.py:122
  309.0 529.0 %all-gather.27.cloned.1.call-start = ((), (), s32[]{:S(2)}) async-start(), calls=%async_computation.19 | async-start | bytes 7864320 | tf_op jit(solution)/shard_map/all_gather | solution.py:123
  309.8 760.5 %all-reduce.27.cloned.1.call-start = ((), (), s32[]{:S(2)}) async-start(), calls=%async_computation.22 | async-start | bytes 12582912 | tf_op jit(solution)/shard_map/psum | solution.py:265
  619.3 218.7 %copy-start.119 = (pred[8,512]{1,0:T(8,128)(4,1)S(1)}, pred[8,512]{1,0:T(8,128)(4,1)}, u32[]{:S(2)}) copy-start(pred[8,512]{1,0:T(8,128)(4,1)} %gt.13) | copy-start | bytes 12292
  922.8 751.6 %reduce-scatter.24.cloned.1.call-start = ((), (), s32[]{:S(2)}) async-start(), calls=%async_computation.23 | async-start | bytes 4718592 | tf_op jit(solution)/shard_map/reduce_scatter | solution.py:307
  1599.0 85.6 %reduce-scatter.26.cloned.1.call-start = ((), (), s32[]{:S(2)}) async-start(), calls=%async_computation.24 | async-start | bytes 4718592 | tf_op jit(solution)/shard_map/reduce_scatter | solution.py:308
  1599.7 154.2 %reduce-scatter.34.cloned.1.call-start = ((), (), s32[]{:S(2)}) async-start(), calls=%async_computation.29 | async-start | bytes 14155776 | tf_op jit(solution)/shard_map/reduce_scatter | solution.py:339
  1613.0 270.9 %reduce-scatter.36.cloned.1.call-start = ((), (), s32[]{:S(2)}) async-start(), calls=%async_computation.31 | async-start | bytes 14155776 | tf_op jit(solution)/shard_map/reduce_scatter | solution.py:340
  1625.7 387.9 %reduce-scatter.38.cloned.1.call-start = ((), (), s32[]{:S(2)}) async-start(), calls=%async_computation.33 | async-start | bytes 14155776 | tf_op jit(solution)/shard_map/reduce_scatter | solution.py:341
  1638.5 406.3 %reduce-scatter.46.cloned.1.call-start = ((), (), s32[]{:S(2)}) async-start(), calls=%async_computation.38 | async-start | bytes 442368
  1651.1 424.9 %reduce-scatter.44.cloned.1.call-start = ((), (), s32[]{:S(2)}) async-start(), calls=%async_computation.37 | async-start | bytes 442368
  1652.1 454.7 %reduce-scatter.42.cloned.1.call-start = ((), (), s32[]{:S(2)}) async-start(), calls=%async_computation.36 | async-start | bytes 442368
  1665.1 487.6 %reduce-scatter.22.cloned.1.call-start = ((), (), s32[]{:S(2)}) async-start(), calls=%async_computation.20 | async-start | bytes 3932160 | tf_op jit(solution)/shard_map/reduce_scatter | solution.py:217
  1665.7 521.0 %reduce-scatter.40.cloned.1.call-start = ((), (), s32[]{:S(2)}) async-start(), calls=%async_computation.35 | async-start | bytes 884736
  1670.8 547.8 %reduce-scatter.28.cloned.1.call-start = ((), (), s32[]{:S(2)}) async-start(), calls=%async_computation.26 | async-start | bytes 884736 | tf_op jit(solution)/shard_map/reduce_scatter | solution.py:331
  1680.5 570.3 %reduce-scatter.30.cloned.1.call-start = ((), (), s32[]{:S(2)}) async-start(), calls=%async_computation.27 | async-start | bytes 884736 | tf_op jit(solution)/shard_map/reduce_scatter | solution.py:332
  1684.5 599.0 %reduce-scatter.32.cloned.1.call-start = ((), (), s32[]{:S(2)}) async-start(), calls=%async_computation.28 | async-start | bytes 884736 | tf_op jit(solution)/shard_map/reduce_scatter | solution.py:333
  1688.9 735.0 %all-reduce.29.cloned.1.call-start = ((), (), s32[]{:S(2)}) async-start(), calls=%async_computation.25 | async-start | bytes 12582912 | tf_op jit(solution)/shard_map/psum | solution.py:326
  1696.2 317.4 %copy-start.127 = (u32[32]{0:T(128)S(1)}, u32[32]{0:T(128)}, u32[]{:S(2)}) copy-start(u32[32]{0:T(128)} %constant.196) | copy-start | bytes 388
  1696.2 319.3 %copy-start.126 = (u32[32]{0:T(128)S(1)}, u32[32]{0:T(128)}, u32[]{:S(2)}) copy-start(u32[32]{0:T(128)} %constant.210) | copy-start | bytes 388
  1696.2 320.6 %copy-start.85 = (f32[2048]{0:T(1024)S(1)}, f32[2048]{0:T(1024)}, u32[]{:S(2)}) copy-start(f32[2048]{0:T(1024)} %copy-done.84) | copy-start | bytes 24580
  1696.2 321.2 %copy-start.122 = (f32[4,3]{1,0:T(4,128)S(1)}, f32[4,3]{1,0:T(4,128)}, u32[]{:S(2)}) copy-start(f32[4,3]{1,0:T(4,128)} %get-tuple-element.155) | copy-start | bytes 148
  1696.2 321.3 %copy-start.5 = (bf16[2048,768]{1,0:T(8,128)(2,1)S(1)}, bf16[2048,768]{1,0:T(8,128)(2,1)}, u32[]{:S(2)}) copy-start(bf16[2048,768]{1,0:T(8,128)(2,1)} %all-gather.17.cloned.1.call-done) | copy-start | bytes 9437188
  1696.3 758.0 %all-gather.31.cloned.1.call-start = ((), (), s32[]{:S(2)}) async-start(), calls=%async_computation.30 | async-start | bytes 4718592 | tf_op jit(solution)/shard_map/all_gather | solution.py:353
  1753.9 700.4 %all-gather.33.cloned.1.call-start = ((), (), s32[]{:S(2)}) async-start(), calls=%async_computation.32 | async-start | bytes 4718592 | tf_op jit(solution)/shard_map/all_gather | solution.py:354
  1883.8 583.4 %all-gather.35.cloned.1.call-start = ((), (), s32[]{:S(2)}) async-start(), calls=%async_computation.34 | async-start | bytes 4718592 | tf_op jit(solution)/shard_map/all_gather | solution.py:355
  (127 other events, 3405.1 us)
Sparse Core Ops, SparseCore 0:
  9.9 46.6 all-gather.16
  68.1 8.9 all-gather.18
  84.9 9.7 all-gather.20
  307.2 137.9 all-reduce.24
  446.9 43.9 all-gather.28
  492.4 115.3 all-gather.22
  609.3 113.5 all-gather.24
  724.4 113.5 all-gather.26
  922.9 137.0 all-reduce.26
  1599.1 7.2 reduce-scatter.23
  1609.3 12.0 reduce-scatter.25
  1623.5 130.3 reduce-scatter.33
  1756.2 127.5 reduce-scatter.35
  1886.0 127.5 reduce-scatter.37
  2015.7 29.0 reduce-scatter.45
  2047.0 28.9 reduce-scatter.43
  2078.1 28.7 reduce-scatter.41
  2110.5 42.1 reduce-scatter.21
  2155.1 31.5 reduce-scatter.39
  2188.8 29.7 reduce-scatter.27
  2221.0 29.8 reduce-scatter.29
  2253.7 29.6 reduce-scatter.31
  2287.1 136.7 all-reduce.28
  2425.3 12.1 all-gather.30
  2439.1 13.2 all-gather.32
  2453.9 13.2 all-gather.34
where the time goes:
time: 2490 us; the launch traced here: 2480 us
  waiting for transfers between devices  952 us (38%)
  matrix products  748 us (30%)
  local copies, waits for them, and re-layouts  305 us (12%)
  other arithmetic  266 us (11%)
  blocking collectives  176 us (7%)
    dot_general x4, matrix products, revisit(): jnp.einsum('hqk,qhd->khd', grad_scores, block, preferred_element_type=jnp...  151 us
    dot_general x4, matrix products, revisit(): jnp.einsum('hqk,khd->qhd', grad_scores, keys, preferred_element_type=jnp....  140 us
    psum x1, waiting for transfers between devices, shards(): grad_normed_attn = lax.psum(grad_lowered_part, 'tp')  137 us
    reduce_scatter x1, waiting for transfers between devices, shards(): lax.psum_scatter(grad_up_w, ('shard', 'ctx'), scatter_dimension=1, tiled=...  130 us
    reduce_scatter x1, waiting for transfers between devices, shards(): lax.psum_scatter(grad_down_w, ('shard', 'ctx'), scatter_dimension=1, tile...  130 us
    all_gather x1, waiting for transfers between devices, shards(): lax.all_gather(w_up, 'shard', axis=1, tiled=True)  104 us
    all_gather x1, waiting for transfers between devices, shards(): lax.all_gather(w_down, 'shard', axis=1, tiled=True)  104 us
    unnamed x30, waiting for transfers between devices  96.4 us
  transfers between devices with their start and end apart: 26, of which 17 were waited for; matrix products, arithmetic and copies ran while one was open for 20% of the time, Pallas kernels for 0%

commit v1 on v0

v1 whole, which is shorter than its diff:
```python
import functools

import jax
import jax.numpy as jnp
from jax import lax
from jax.experimental import pallas as pl
from jax.experimental.pallas import tpu as pltpu
from jax.sharding import PartitionSpec as P

HEAD_DIM = 64
EXPERTS = 12
FFN_EXPERTS = 8
CAP = 512
BLOCK = 512
EXTRA = 128
SMALL = 32
MESH = pl.DeviceIdType.MESH

epsilon = 1e-06
rope_base = 10000.0
bf16 = jnp.bfloat16
f32 = jnp.float32

NN = (((1,), (0,)), ((), ()))
NT = (((1,), (1,)), ((), ()))
TN = (((0,), (0,)), ((), ()))


def mm(left, right, dims=NN, precision=None):
    return lax.dot_general(
        left, right, dims, preferred_element_type=f32, precision=precision
    )


def params(mib=56, **more):
    return pltpu.CompilerParams(vmem_limit_bytes=mib * 1024 * 1024, **more)


def full(shape):
    return pl.BlockSpec(shape, lambda *_: (0,) * len(shape))


def zig(core, i):
    return 4 * (i // 2) + (core if i % 2 == 0 else 3 - core)


def qkv_kernel(x_ref, gain_ref, wt_ref, cos_ref, sin_ref, a_ref, qt_ref, kt_ref, k_ref, v_ref, vt_ref):
    heads = qt_ref.shape[0]
    width = heads * HEAD_DIM
    half = HEAD_DIM // 2
    x = x_ref[...].astype(f32)
    inverse = lax.rsqrt(jnp.mean(x * x, axis=1, keepdims=True) + epsilon)
    a = (x * inverse * gain_ref[...]).astype(bf16)
    a_ref[...] = a
    y = mm(wt_ref[...], a, NT)
    c, s = cos_ref[...], sin_ref[...]

    def turned(first):
        u, w = y[first : first + half], y[first + half : first + HEAD_DIM]
        return jnp.concatenate([u * c - w * s, w * c + u * s], axis=0)

    for h in range(heads):
        at = h * HEAD_DIM
        qt_ref[h] = (turned(at) * HEAD_DIM**-0.5).astype(bf16)
        key = turned(width + at)
        kt_ref[h] = key.astype(bf16)
        k_ref[h] = key.T.astype(bf16)
        value = y[2 * width + at : 2 * width + at + HEAD_DIM]
        v_ref[h] = value.T.astype(bf16)
        vt_ref[h, :HEAD_DIM] = value.astype(bf16)
        vt_ref[h, HEAD_DIM:] = jnp.ones((16, value.shape[1]), bf16)


def project(rows, gain, wt, cosine, sine, heads):
    total, width = rows.shape
    tile = BLOCK
    out = heads * HEAD_DIM
    return pl.pallas_call(
        qkv_kernel,
        grid=(total // tile,),
        in_specs=[
            pl.BlockSpec((tile, width), lambda i: (i, 0)),
            full((1, width)),
            full((3 * out, width)),
            pl.BlockSpec((HEAD_DIM // 2, tile), lambda i: (0, i)),
            pl.BlockSpec((HEAD_DIM // 2, tile), lambda i: (0, i)),
        ],
        out_specs=[
            pl.BlockSpec((tile, width), lambda i: (i, 0)),
            pl.BlockSpec((heads, HEAD_DIM, tile), lambda i: (0, 0, i)),
            pl.BlockSpec((heads, HEAD_DIM, tile), lambda i: (0, 0, i)),
            pl.BlockSpec((heads, tile, HEAD_DIM), lambda i: (0, i, 0)),
            pl.BlockSpec((heads, tile, HEAD_DIM), lambda i: (0, i, 0)),
            pl.BlockSpec((heads, HEAD_DIM + 16, tile), lambda i: (0, 0, i)),
        ],
        out_shape=[
            jax.ShapeDtypeStruct((total, width), bf16),
            jax.ShapeDtypeStruct((heads, HEAD_DIM, total), bf16),
            jax.ShapeDtypeStruct((heads, HEAD_DIM, total), bf16),
            jax.ShapeDtypeStruct((heads, total, HEAD_DIM), bf16),
            jax.ShapeDtypeStruct((heads, total, HEAD_DIM), bf16),
            jax.ShapeDtypeStruct((heads, HEAD_DIM + 16, total), bf16),
        ],
        compiler_params=params(),
        name="project",
    )(rows, gain, wt, cosine, sine)


def attend_kernel(table, length, qt_ref, k_ref, vt_ref, ot_ref, lse_ref, top_ref):
    index = table[pl.program_id(1)]
    qt = qt_ref[0]
    columns = qt.shape[1]

    def step(at, carry, diagonal):
        peak, total = carry
        start = pl.multiple_of(at * BLOCK, BLOCK)
        scores = mm(k_ref[0, pl.ds(start, BLOCK), :], qt)
        if diagonal:
            keys = lax.broadcasted_iota(jnp.int32, scores.shape, 0)
            queries = lax.broadcasted_iota(jnp.int32, scores.shape, 1)
            scores = jnp.where(keys <= queries, scores, -1e30)
        higher = jnp.maximum(peak, jnp.max(scores, axis=0, keepdims=True))
        weights = jnp.exp(scores - higher).astype(bf16)
        total = total * jnp.exp(peak - higher) + mm(vt_ref[0, :, pl.ds(start, BLOCK)], weights)
        return higher, total

    start = (jnp.full((1, columns), -1e30, f32), jnp.zeros((HEAD_DIM + 16, columns), f32))
    carry = lax.fori_loop(0, index, lambda at, c: step(at, c, False), start)
    peak, total = step(index, carry, True)
    mass = total[HEAD_DIM : HEAD_DIM + 1]
    ot_ref[0] = (total[:HEAD_DIM] / mass).astype(bf16)
    lse_ref[0, 0] = peak + jnp.log(mass)
    position = index * BLOCK + lax.broadcasted_iota(jnp.int32, peak.shape, 1)
    top_ref[0, 0] = jnp.where(position < length[0], peak, -1e30)


def attend(table, length, qt, k, vt):
    heads, _, total = qt.shape
    count = table.shape[0]
    return pl.pallas_call(
        attend_kernel,
        grid_spec=pltpu.PrefetchScalarGridSpec(
            num_scalar_prefetch=2,
            grid=(heads, count),
            in_specs=[
                pl.BlockSpec((1, HEAD_DIM, BLOCK), lambda h, i, t, n: (h, 0, t[i])),
                pl.BlockSpec((1, total, HEAD_DIM), lambda h, i, t, n: (h, 0, 0)),
                pl.BlockSpec((1, HEAD_DIM + 16, total), lambda h, i, t, n: (h, 0, 0)),
            ],
            out_specs=[
                pl.BlockSpec((1, HEAD_DIM, BLOCK), lambda h, i, t, n: (i, h, 0)),
                pl.BlockSpec((1, 1, 1, BLOCK), lambda h, i, t, n: (h, i, 0, 0)),
                pl.BlockSpec((1, 1, 1, BLOCK), lambda h, i, t, n: (h, i, 0, 0)),
            ],
        ),
        out_shape=[
            jax.ShapeDtypeStruct((count, heads * HEAD_DIM, BLOCK), bf16),
            jax.ShapeDtypeStruct((heads, count, 1, BLOCK), f32),
            jax.ShapeDtypeStruct((heads, count, 1, BLOCK), f32),
        ],
        compiler_params=params(),
        name="attend",
    )(table, length, qt, k, vt)


def revisit_kernel(table, qt_ref, k_ref, kt_ref, v_ref, ot_ref, got_ref, lse_ref, dq_ref, dk_ref, dv_ref, sum_k, sum_v):
    i = pl.program_id(1)
    index = table[i]
    qt, got = qt_ref[0], got_ref[0]
    lse = lse_ref[0, 0]
    centre = jnp.sum(ot_ref[0].astype(f32) * got.astype(f32), axis=0, keepdims=True)

    @pl.when(i == 0)
    def _():
        sum_k[...] = jnp.zeros_like(sum_k)
        sum_v[...] = jnp.zeros_like(sum_v)

    def step(at, grad, diagonal):
        start = pl.multiple_of(at * BLOCK, BLOCK)
        here = pl.ds(start, BLOCK)
        scores = mm(k_ref[0, here, :], qt)
        probs = jnp.exp(scores - lse)
        if diagonal:
            keys = lax.broadcasted_iota(jnp.int32, scores.shape, 0)
            queries = lax.broadcasted_iota(jnp.int32, scores.shape, 1)
            probs = jnp.where(keys <= queries, probs, 0.0)
        grad_probs = mm(v_ref[0, here, :], got)
        grad_scores = (probs * (grad_probs - centre)).astype(bf16)
        sum_v[here, :] += mm(probs.astype(bf16), got, NT)
        sum_k[here, :] += mm(grad_scores, qt, NT)
        return grad + mm(kt_ref[0, :, here], grad_scores)

    grad = lax.fori_loop(0, index, lambda at, c: step(at, c, False), jnp.zeros(qt.shape, f32))
    dq_ref[0] = step(index, grad, True) * HEAD_DIM**-0.5

    @pl.when(i == pl.num_programs(1) - 1)
    def _():
        dk_ref[0] = sum_k[...].T
        dv_ref[0] = sum_v[...].T


def revisit(table, qt, k, kt, v, ot, got, lse):
    heads, _, total = qt.shape
    count = table.shape[0]
    whole = pl.BlockSpec((1, HEAD_DIM, total), lambda h, i, t: (h, 0, 0))
    tall = pl.BlockSpec((1, total, HEAD_DIM), lambda h, i, t: (h, 0, 0))
    dealt = pl.BlockSpec((1, HEAD_DIM, BLOCK), lambda h, i, t: (i, h, 0))
    placed = pl.BlockSpec((1, HEAD_DIM, BLOCK), lambda h, i, t: (h, 0, t[i]))
    return pl.pallas_call(
        revisit_kernel,
        grid_spec=pltpu.PrefetchScalarGridSpec(
            num_scalar_prefetch=1,
            grid=(heads, count),
            in_specs=[
                placed,
                tall,
                whole,
                tall,
                dealt,
                dealt,
                pl.BlockSpec((1, 1, 1, BLOCK), lambda h, i, t: (h, i, 0, 0)),
            ],
            out_specs=[placed, whole, whole],
            scratch_shapes=[
                pltpu.VMEM((total, HEAD_DIM), f32),
                pltpu.VMEM((total, HEAD_DIM), f32),
            ],
        ),
        out_shape=[jax.ShapeDtypeStruct((heads, HEAD_DIM, total), f32)] * 3,
        compiler_params=params(),
        name="revisit",
    )(table, qt, k, kt, v, ot, got, lse)


def unproject_kernel(owned, dq_ref, dk_ref, dv_ref, cos_ref, sin_ref, a_ref, wt_ref, part_ref, gw_ref, total):
    heads = dq_ref.shape[0]
    half = HEAD_DIM // 2
    i = pl.program_id(0)
    c, s = cos_ref[...], sin_ref[...]

    def turned(g):
        u, w = g[:half], g[half:]
        return jnp.concatenate([u * c + w * s, w * c - u * s], axis=0)

    mine = owned[i] > 0
    pieces = [turned(jnp.where(mine, dq_ref[h], 0.0)) for h in range(heads)]
    pieces += [turned(dk_ref[h]) for h in range(heads)]
    pieces += [dv_ref[h] for h in range(heads)]
    grads = jnp.concatenate(pieces, axis=0).astype(bf16)
    part_ref[...] = mm(grads, wt_ref[...], TN).astype(bf16)

    @pl.when(i == 0)
    def _():
        total[...] = jnp.zeros_like(total)

    total[...] += mm(grads, a_ref[...])

    @pl.when(i == pl.num_programs(0) - 1)
    def _():
        gw_ref[...] = total[...].astype(bf16)


def unproject(owned, dq, dk, dv, cosine, sine, a, wt):
    heads, _, rows = dq.shape
    width = a.shape[1]
    out = wt.shape[0]
    piece = pl.BlockSpec((heads, HEAD_DIM, BLOCK), lambda i, o: (0, 0, i))
    table = pl.BlockSpec((HEAD_DIM // 2, BLOCK), lambda i, o: (0, i))
    return pl.pallas_call(
        unproject_kernel,
        grid_spec=pltpu.PrefetchScalarGridSpec(
            num_scalar_prefetch=1,
            grid=(rows // BLOCK,),
            in_specs=[
                piece,
                piece,
                piece,
                table,
                table,
                pl.BlockSpec((BLOCK, width), lambda i, o: (i, 0)),
                full((out, width)),
            ],
            out_specs=[pl.BlockSpec((BLOCK, width), lambda i, o: (i, 0)), full((out, width))],
            scratch_shapes=[pltpu.VMEM((out, width), f32)],
        ),
        out_shape=[
            jax.ShapeDtypeStruct((rows, width), bf16),
            jax.ShapeDtypeStruct((out, width), bf16),
        ],
        compiler_params=params(),
        name="unproject",
    )(owned, dq, dk, dv, cosine, sine, a, wt)


def greet(me_c, me_t, nc, nt):
    barrier = pltpu.get_barrier_semaphore()
    for step in range(1, nc * nt):
        other = lax.rem(me_c * nt + me_t + step, nc * nt)
        pl.semaphore_signal(
            barrier,
            inc=1,
            device_id={"ctx": other // nt, "tp": lax.rem(other, nt)},
            device_id_type=MESH,
        )
    pl.semaphore_wait(barrier, nc * nt - 1)


def to_owner_kernel(nc, nt, o_ref, att_ref, send_sem, recv_sem, local_sem):
    c, t = lax.axis_index("ctx"), lax.axis_index("tp")
    own = c * nt + t
    count = o_ref.shape[0]
    greet(c, t, nc, nt)
    copies = []
    for i in range(count):
        block = zig(c, i)
        copy = pltpu.make_async_remote_copy(
            src_ref=o_ref.at[i],
            dst_ref=att_ref.at[t],
            send_sem=send_sem.at[i],
            recv_sem=recv_sem.at[t],
            device_id={"ctx": block // nt, "tp": lax.rem(block, nt)},
            device_id_type=MESH,
        )
        local = pltpu.make_async_copy(o_ref.at[i], att_ref.at[t], local_sem)
        copies.append((block, copy, local))
    for block, copy, local in copies:

        @pl.when(block != own)
        def _():
            copy.start()

        @pl.when(block == own)
        def _():
            local.start()

    for block, copy, local in copies:

        @pl.when(block != own)
        def _():
            copy.wait_send()

        @pl.when(block == own)
        def _():
            local.wait()

    mine = lax.rem((own + 1) // 2, 2) == c
    for source in range(nt):

        @pl.when(jnp.logical_or(jnp.logical_not(mine), source != t))
        def _():
            pltpu.make_async_remote_copy(
                src_ref=o_ref.at[0],
                dst_ref=att_ref.at[source],
                send_sem=send_sem.at[0],
                recv_sem=recv_sem.at[source],
                device_id={"ctx": c, "tp": t},
                device_id_type=MESH,
            ).wait_recv()


def to_heads_kernel(nc, nt, o_ref, got_ref, send_sem, recv_sem, local_sem):
    c, t = lax.axis_index("ctx"), lax.axis_index("tp")
    own = c * nt + t
    count = got_ref.shape[0]
    greet(c, t, nc, nt)
    core = lax.rem((own + 1) // 2, 2)
    slot = 2 * (own // 4) + lax.rem(own, 4) // 2
    for target in range(nt):
        here = jnp.logical_and(core == c, target == t)

        @pl.when(jnp.logical_not(here))
        def _():
            pltpu.make_async_remote_copy(
                src_ref=o_ref.at[target],
                dst_ref=got_ref.at[slot],
                send_sem=send_sem.at[target],
                recv_sem=recv_sem.at[slot],
                device_id={"ctx": core, "tp": target},
                device_id_type=MESH,
            ).start()

        @pl.when(here)
        def _():
            pltpu.make_async_copy(o_ref.at[target], got_ref.at[slot], local_sem).start()

    for target in range(nt):
        here = jnp.logical_and(core == c, target == t)

        @pl.when(jnp.logical_not(here))
        def _():
            pltpu.make_async_remote_copy(
                src_ref=o_ref.at[target],
                dst_ref=got_ref.at[slot],
                send_sem=send_sem.at[target],
                recv_sem=recv_sem.at[slot],
                device_id={"ctx": core, "tp": target},
                device_id_type=MESH,
            ).wait_send()

        @pl.when(here)
        def _():
            pltpu.make_async_copy(o_ref.at[target], got_ref.at[slot], local_sem).wait()

    for i in range(count):

        @pl.when(zig(c, i) != own)
        def _():
            pltpu.make_async_remote_copy(
                src_ref=o_ref.at[0],
                dst_ref=got_ref.at[i],
                send_sem=send_sem.at[0],
                recv_sem=recv_sem.at[i],
                device_id={"ctx": c, "tp": t},
                device_id_type=MESH,
            ).wait_recv()


def exchange(kernel, value, count, number, name):
    nc, nt = lax.axis_size("ctx"), lax.axis_size("tp")
    return pl.pallas_call(
        functools.partial(kernel, nc, nt),
        in_specs=[pl.BlockSpec(memory_space=pltpu.VMEM)],
        out_specs=pl.BlockSpec(memory_space=pltpu.VMEM),
        out_shape=jax.ShapeDtypeStruct((count,) + value.shape[1:], value.dtype),
        scratch_shapes=[
            pltpu.SemaphoreType.DMA((value.shape[0],)),
            pltpu.SemaphoreType.DMA((count,)),
            pltpu.SemaphoreType.DMA,
        ],
        compiler_params=params(collective_id=number, has_side_effects=True),
        name=name,
    )(value)


def mixing(n2, wrc, previous, routes):
    z = mm(n2, wrc, precision=lax.Precision.HIGHEST)
    lane = lax.broadcasted_iota(jnp.int32, z.shape, 1)
    logits = z + previous
    hot = [lane == routes[:, r : r + 1] for r in range(2)]
    picked = [jnp.sum(jnp.where(hot[r], logits, 0.0), axis=1, keepdims=True) for r in range(2)]
    most = jnp.maximum(picked[0], picked[1])
    e = [jnp.exp(p - most) for p in picked]
    gates = [v / (e[0] + e[1]) for v in e]
    combine = jnp.where(hot[0], gates[0], 0.0) + jnp.where(hot[1], gates[1], 0.0)

    def column(array, at):
        return jnp.sum(jnp.where(lane == at, array, 0.0), axis=1, keepdims=True)

    alphas = []
    for j in range(2):
        first, second = column(z, EXPERTS + 2 * j), column(z, EXPERTS + 2 * j + 1)
        most = jnp.maximum(first, second)
        a, b = jnp.exp(first - most), jnp.exp(second - most)
        alphas.append((a / (a + b), b / (a + b)))
    weights = [column(combine, FFN_EXPERTS + 1 + j) for j in range(3)]
    return hot, gates, combine, alphas, weights


def forward_kernel(place, x_ref, att_ref, wo_ref, gain_ref, wrc_ref, vec_ref, prev_ref, routes_ref, res_ref, base_ref, a_ref, comb_ref):
    heads_in = att_ref.shape[0] * att_ref.shape[1]
    att = att_ref[...].reshape(heads_in, att_ref.shape[2])
    res = x_ref[...].astype(f32) + mm(att, wo_ref[...], TN)
    res_ref[...] = res
    inverse = lax.rsqrt(jnp.mean(res * res, axis=1, keepdims=True) + epsilon)
    n2 = res * inverse * gain_ref[...]
    a_ref[...] = n2.astype(bf16)
    _, _, combine, alphas, weights = mixing(n2, wrc_ref[...], prev_ref[...], routes_ref[...])
    scale = weights[0] + weights[1] * alphas[0][0] + weights[2] * alphas[1][0]
    base_ref[...] = (
        res
        + scale * n2
        + (weights[1] * alphas[0][1]) * vec_ref[0:1]
        + (weights[2] * alphas[1][1]) * vec_ref[1:2]
    )
    comb_ref[...] = combine.T[:16]


def forward_rows(place, x, att, wo, gain, wrc, vec, prev, routes):
    rows, width = x.shape
    own = lambda i, p: (p[0], 0)
    return pl.pallas_call(
        forward_kernel,
        grid_spec=pltpu.PrefetchScalarGridSpec(
            num_scalar_prefetch=1,
            grid=(1,),
            in_specs=[
                full(x.shape),
                full(att.shape),
                full(wo.shape),
                full(gain.shape),
                full(wrc.shape),
                full(vec.shape),
                pl.BlockSpec((rows, prev.shape[1]), own),
                pl.BlockSpec((rows, 2), own),
            ],
            out_specs=[full((rows, width)), full((rows, width)), full((rows, width)), full((16, rows))],
        ),
        out_shape=[
            jax.ShapeDtypeStruct((rows, width), f32),
            jax.ShapeDtypeStruct((rows, width), f32),
            jax.ShapeDtypeStruct((rows, width), bf16),
            jax.ShapeDtypeStruct((16, rows), f32),
        ],
        compiler_params=params(),
        name="forward_rows",
    )(place, x, att, wo, gain, wrc, vec, prev, routes)


def backward_kernel(place, res_ref, dn_ref, cot_ref, valid_ref, att_ref, wo_ref, gain_ref, wrc_ref, vec_ref, prev_ref, routes_ref,
                    dres_ref, got_ref, gwo_ref, small_ref):
    width = res_ref.shape[1]
    res = res_ref[...]
    gain = gain_ref[...]
    inverse = lax.rsqrt(jnp.mean(res * res, axis=1, keepdims=True) + epsilon)
    m = res * inverse
    n2 = m * gain
    hot, gates, _, alphas, weights = mixing(n2, wrc_ref[...], prev_ref[...], routes_ref[...])
    g = cot_ref[...].astype(f32) * valid_ref[...]
    inner = jnp.sum(g * n2, axis=1, keepdims=True)
    onto = [jnp.sum(g * vec_ref[j : j + 1], axis=1, keepdims=True) for j in range(2)]
    named = dn_ref[:, width:].astype(f32)
    lane = lax.broadcasted_iota(jnp.int32, hot[0].shape, 1)
    wide = lax.broadcasted_iota(jnp.int32, named.shape, 1)
    local = {
        FFN_EXPERTS + 1: inner,
        FFN_EXPERTS + 2: alphas[0][0] * inner + alphas[0][1] * onto[0],
        FFN_EXPERTS + 3: alphas[1][0] * inner + alphas[1][1] * onto[1],
    }
    routes = routes_ref[...]
    dgates = []
    for r in range(2):
        name = routes[:, r : r + 1]
        there = jnp.where((wide == name) | (wide == name + 16), named, 0.0)
        there = jnp.where(name < FFN_EXPERTS, jnp.sum(there, axis=1, keepdims=True), 0.0)
        for e, value in local.items():
            there = there + jnp.where(name == e, value, 0.0)
        dgates.append(there)
    mean = gates[0] * dgates[0] + gates[1] * dgates[1]
    dz = jnp.where(hot[0], gates[0] * (dgates[0] - mean), 0.0)
    dz = dz + jnp.where(hot[1], gates[1] * (dgates[1] - mean), 0.0)
    for j in range(2):
        da = weights[1 + j] * inner
        db = weights[1 + j] * onto[j]
        centre = alphas[j][0] * da + alphas[j][1] * db
        dz = dz + jnp.where(lane == EXPERTS + 2 * j, alphas[j][0] * (da - centre), 0.0)
        dz = dz + jnp.where(lane == EXPERTS + 2 * j + 1, alphas[j][1] * (db - centre), 0.0)
    scale = weights[0] + weights[1] * alphas[0][0] + weights[2] * alphas[1][0]
    highest = lax.Precision.HIGHEST
    dn2 = dn_ref[:, :width].astype(f32) + scale * g + mm(dz, wrc_ref[...], NT, highest)
    small_ref[0:16] = mm(dz, n2, TN, highest)
    small_ref[16:24] = jnp.zeros((8, width), f32)
    small_ref[16:17] = jnp.sum((weights[1] * alphas[0][1]) * g, axis=0, keepdims=True)
    small_ref[17:18] = jnp.sum((weights[2] * alphas[1][1]) * g, axis=0, keepdims=True)
    small_ref[18:19] = jnp.sum(dn2 * m, axis=0, keepdims=True)
    q = dn2 * gain
    dres = g + inverse * (q - m * jnp.mean(q * m, axis=1, keepdims=True))
    dres_ref[...] = dres
    da = dres.astype(bf16)
    got = mm(wo_ref[...], da, NT).astype(bf16)
    got_ref[...] = got.reshape(got_ref.shape)
    att = att_ref[...].reshape(got.shape)
    gwo_ref[...] = mm(att, da).astype(bf16)


def backward_rows(place, res, dn, cot, valid, att, wo, gain, wrc, vec, prev, routes):
    rows, width = res.shape
    own = lambda i, p: (p[0], 0)
    return pl.pallas_call(
        backward_kernel,
        grid_spec=pltpu.PrefetchScalarGridSpec(
            num_scalar_prefetch=1,
            grid=(1,),
            in_specs=[
                full(res.shape),
                full(dn.shape),
                full(cot.shape),
                full(valid.shape),
                full(att.shape),
                full(wo.shape),
                full(gain.shape),
                full(wrc.shape),
                full(vec.shape),
                pl.BlockSpec((rows, prev.shape[1]), own),
                pl.BlockSpec((rows, 2), own),
            ],
            out_specs=[full((rows, width)), full(att.shape), full((wo.shape[0], width)), full((24, width))],
        ),
        out_shape=[
            jax.ShapeDtypeStruct((rows, width), f32),
            jax.ShapeDtypeStruct(att.shape, bf16),
            jax.ShapeDtypeStruct((wo.shape[0], width), bf16),
            jax.ShapeDtypeStruct((24, width), f32),
        ],
        compiler_params=params(),
        name="backward_rows",
    )(place, res, dn, cot, valid, att, wo, gain, wrc, vec, prev, routes)


def finish_kernel(x_ref, dn_ref, dres_ref, gain_ref, base_ref, feed_ref, valid_ref, gin_ref, out_ref, small_ref):
    x = x_ref[...].astype(f32)
    inverse = lax.rsqrt(jnp.mean(x * x, axis=1, keepdims=True) + epsilon)
    m = x * inverse
    dn = dn_ref[...].astype(f32)
    q = dn * gain_ref[...]
    gin_ref[...] = dres_ref[...] + inverse * (q - m * jnp.mean(q * m, axis=1, keepdims=True))
    small_ref[...] = jnp.sum(dn * m, axis=0, keepdims=True)
    out_ref[...] = (valid_ref[...] * (base_ref[...] + feed_ref[...].astype(f32))).astype(bf16)


def finish_rows(x, dn, dres, gain, base, feed, valid):
    rows, width = x.shape
    return pl.pallas_call(
        finish_kernel,
        out_shape=[
            jax.ShapeDtypeStruct((rows, width), f32),
            jax.ShapeDtypeStruct((rows, width), bf16),
            jax.ShapeDtypeStruct((1, width), f32),
        ],
        compiler_params=params(),
        name="finish_rows",
    )(x, dn, dres, gain, base, feed, valid)


def place_kernel(per, rt_ref, rc_ref, row_ref, col_ref):
    total = rt_ref.shape[1]
    one = lax.broadcasted_iota(jnp.int32, (BLOCK, BLOCK), 0)
    two = lax.broadcasted_iota(jnp.int32, (BLOCK, BLOCK), 1)
    before_row = (one < two).astype(bf16)
    before_col = (two < one).astype(bf16)
    row_carry = col_carry = None
    for at in range(0, total, BLOCK):
        if at % per == 0:
            row_carry = jnp.zeros((16, 1), f32)
            col_carry = jnp.zeros((1, 16), f32)
        here = slice(at, at + BLOCK)
        expert = lax.broadcasted_iota(jnp.int32, (16, BLOCK), 0)
        member = (rt_ref[0:1, here] == expert) | (rt_ref[1:2, here] == expert)
        rank = mm(member.astype(bf16), before_row) + row_carry
        row_ref[:, here] = jnp.where(member, rank, -1.0)
        row_carry = row_carry + jnp.sum(member.astype(f32), axis=1, keepdims=True)
        expert = lax.broadcasted_iota(jnp.int32, (BLOCK, 16), 1)
        member = (rc_ref[here, 0:1] == expert) | (rc_ref[here, 1:2] == expert)
        rank = mm(before_col, member.astype(bf16)) + col_carry
        col_ref[here, :] = jnp.where(member, rank, -1.0)
        col_carry = col_carry + jnp.sum(member.astype(f32), axis=0, keepdims=True)


def place_rows(routes, per):
    total = routes.shape[0]
    return pl.pallas_call(
        functools.partial(place_kernel, per),
        out_shape=[
            jax.ShapeDtypeStruct((16, total), f32),
            jax.ShapeDtypeStruct((total, 16), f32),
        ],
        compiler_params=params(),
        name="place_rows",
    )(routes.T, routes)


def fetch_kernel(first, row_ref, comb_ref, rows_ref, out_ref, gate_ref):
    expert = first[0] + pl.program_id(1)
    slot = lax.broadcasted_iota(jnp.int32, (CAP, row_ref.shape[1]), 0).astype(f32)
    hot = slot == row_ref[pl.ds(expert, 1), :]
    out_ref[0] = mm(hot.astype(bf16), rows_ref[...]).astype(bf16)
    if gate_ref is not None:
        gate_ref[0] = jnp.sum(jnp.where(hot, comb_ref[pl.ds(expert, 1), :], 0.0), axis=1, keepdims=True)


def fetch_rows(first, row, comb, rows, per, local, gated):
    total, width = rows.shape
    blocks = total // per
    outs = [jax.ShapeDtypeStruct((local, blocks * CAP, width), bf16)]
    specs = [pl.BlockSpec((1, CAP, width), lambda b, j, f: (j, b, 0))]
    ins = [
        pl.BlockSpec((16, per), lambda b, j, f: (0, b)),
        pl.BlockSpec((16, per), lambda b, j, f: (0, b)),
        pl.BlockSpec((per, width), lambda b, j, f: (b, 0)),
    ]
    args = (row, comb, rows)
    if gated:
        outs.append(jax.ShapeDtypeStruct((local, blocks * CAP, 1), f32))
        specs.append(pl.BlockSpec((1, CAP, 1), lambda b, j, f: (j, b, 0)))
        body = fetch_kernel
    else:
        body = lambda f, p, r, o: fetch_kernel(f, p, None, r, o, None)
        del ins[1]
        args = (row, rows)
    return pl.pallas_call(
        body,
        grid_spec=pltpu.PrefetchScalarGridSpec(
            num_scalar_prefetch=1, grid=(blocks, local), in_specs=ins, out_specs=specs
        ),
        out_shape=outs,
        compiler_params=params(),
        name="fetch_rows",
    )(first, *args)


def expert_kernel(j, first, x_ref, g_ref, gate_ref, w_ref, feed_ref, back_ref, gw_ref, total):
    i = pl.program_id(0)
    parts, _, depth, hidden = w_ref.shape
    width = parts * depth
    wg, wu, wd = [w_ref[:, k].reshape(width, hidden) for k in range(3)]
    x, g, gate = x_ref[0], g_ref[0], gate_ref[0]
    gate_pre = mm(x, wg)
    up = mm(x, wu)
    sigmoid = 1.0 / (1.0 + jnp.exp(-gate_pre))
    activated = gate_pre * sigmoid
    inner = (activated * up).astype(bf16)
    out = mm(inner, wd, NT)
    g32 = g.astype(f32)
    feed_ref[...] = (gate * out).astype(bf16)
    dgate = jnp.sum(g32 * out, axis=1, keepdims=True)
    dout = (gate * g32).astype(bf16)
    dinner = mm(dout, wd)
    dpre = (dinner * up * sigmoid * (1.0 + gate_pre * (1.0 - sigmoid))).astype(bf16)
    dup = (dinner * activated).astype(bf16)
    back_ref[:, :width] = (mm(dpre, wg, NT) + mm(dup, wu, NT)).astype(bf16)
    lane = lax.broadcasted_iota(jnp.int32, (dgate.shape[0], back_ref.shape[1] - width), 1)
    coarse = dgate.astype(bf16).astype(f32)
    at = first[0] + j
    extra = jnp.where(lane == at, coarse, jnp.where(lane == at + 16, dgate - coarse, 0.0))
    back_ref[:, width:] = extra.astype(bf16)

    @pl.when(i == 0)
    def _():
        total[...] = jnp.zeros_like(total)

    total[0] += mm(x, dpre, TN)
    total[1] += mm(x, dup, TN)
    total[2] += mm(dout, inner, TN)

    @pl.when(i == pl.num_programs(0) - 1)
    def _():
        for k in range(3):
            gw_ref[:, k] = total[k].reshape(parts, depth, hidden).astype(bf16)


def expert(j, first, x, g, gate, w):
    slots, width = x.shape[1:]
    parts, _, depth, hidden = w.shape
    pick = lambda i, f: (j, i, 0)
    return pl.pallas_call(
        functools.partial(expert_kernel, j),
        grid_spec=pltpu.PrefetchScalarGridSpec(
            num_scalar_prefetch=1,
            grid=(slots // CAP,),
            in_specs=[
                pl.BlockSpec((1, CAP, width), pick),
                pl.BlockSpec((1, CAP, width), pick),
                pl.BlockSpec((1, CAP, 1), pick),
                full(w.shape),
            ],
            out_specs=[
                pl.BlockSpec((CAP, width), lambda i, f: (i, 0)),
                pl.BlockSpec((CAP, width + EXTRA), lambda i, f: (i, 0)),
                full(w.shape),
            ],
            scratch_shapes=[pltpu.VMEM((3, width, hidden), f32)],
        ),
        out_shape=[
            jax.ShapeDtypeStruct((slots, width), bf16),
            jax.ShapeDtypeStruct((slots, width + EXTRA), bf16),
            jax.ShapeDtypeStruct(w.shape, bf16),
        ],
        compiler_params=params(),
        name="expert",
    )(first, x, g, gate, w)


def spread_kernel(local, first, col_ref, *refs):
    out_ref = refs[-1]
    lane = lax.broadcasted_iota(jnp.int32, col_ref.shape, 1)
    slot = lax.broadcasted_iota(jnp.int32, (col_ref.shape[0], CAP), 1).astype(f32)
    total = None
    for j in range(local):
        mine = jnp.sum(jnp.where(lane == first[0] + j, col_ref[...], 0.0), axis=1, keepdims=True)
        term = mm((slot == mine).astype(bf16), refs[j][...])
        total = term if total is None else total + term
    out_ref[...] = total.astype(bf16)


def spread_rows(first, col, values, per):
    total = col.shape[0]
    tile = BLOCK
    width = values[0].shape[1]
    return pl.pallas_call(
        functools.partial(spread_kernel, len(values)),
        grid_spec=pltpu.PrefetchScalarGridSpec(
            num_scalar_prefetch=1,
            grid=(total // tile,),
            in_specs=[pl.BlockSpec((tile, 16), lambda i, f: (i, 0))]
            + [pl.BlockSpec((CAP, width), lambda i, f: (i // (per // tile), 0)) for _ in values],
            out_specs=pl.BlockSpec((tile, width), lambda i, f: (i, 0)),
        ),
        out_shape=jax.ShapeDtypeStruct((total, width), bf16),
        compiler_params=params(),
        name="spread_rows",
    )(first, col, *values)


def shards(
    hidden_in,
    cotangent,
    lengths,
    routes,
    prev_logits,
    norm_attn,
    w_query,
    w_key,
    w_value,
    w_out,
    norm_moe,
    w_router,
    w_const,
    const_vec,
    w_gate,
    w_up,
    w_down,
    threshold,
):
    plane = ("ctx", "tp")
    core, lane = lax.axis_index("ctx"), lax.axis_index("tp")
    nc, nt, ns = lax.axis_size("ctx"), lax.axis_size("tp"), lax.axis_size("shard")
    own, width = hidden_in.shape
    per = own * nt
    total = per * nc
    depth = w_gate.shape[1]
    heads = w_query.shape[1] // HEAD_DIM
    head_width = heads * HEAD_DIM
    local = FFN_EXPERTS // nc
    count = total // BLOCK // nc
    first_row = core * per + lane * own
    length = lengths[0]
    valid = (first_row + jnp.arange(own, dtype=jnp.int32) < length).astype(f32)[:, None]
    place = lane.astype(jnp.int32)[None]
    first = (core * local).astype(jnp.int32)[None]

    pack = jnp.concatenate(
        [
            w_query,
            w_key,
            w_value,
            w_out.T,
            norm_attn[:, None],
            norm_moe[:, None],
            w_router,
            w_const,
            const_vec.T,
            jnp.zeros((depth, 12), bf16),
        ],
        axis=1,
    )
    rows_all = lax.all_gather(hidden_in, plane, axis=0, tiled=True)
    packed = lax.all_gather(pack, "shard", axis=0, tiled=True)
    expert_w = []
    for j in range(local):
        pieces = [
            lax.dynamic_index_in_dim(w, core * local + j, 0, keepdims=False)
            for w in (w_gate, w_up, w_down)
        ]
        gathered = lax.all_gather(jnp.stack(pieces), "shard", axis=0, tiled=False)
        expert_w.append(gathered)

    wt = packed[:, : 3 * head_width].T
    out_t = packed[:, 3 * head_width : 4 * head_width]
    wo = lax.all_gather(out_t, "tp", axis=0, tiled=False)
    wo = wo.transpose(0, 2, 1).reshape(nt * head_width, width)
    smalls = packed[:, 4 * head_width :].astype(f32)
    gain_attn = smalls[:, 0][None]
    gain_moe = smalls[:, 1][None]
    wrc = smalls[:, 2 : 2 + EXPERTS + 4]
    vec = smalls[:, 2 + EXPERTS + 4 : 4 + EXPERTS + 4].T
    prev = jnp.pad(prev_logits, ((0, 0), (0, 4)))

    freqs = rope_base ** (-2.0 * jnp.arange(HEAD_DIM // 2).astype(f32) / HEAD_DIM)
    angles = freqs[:, None] * jnp.arange(total).astype(f32)[None, :]
    cosine, sine = jnp.cos(angles), jnp.sin(angles)

    a1, qt, kt, k, v, vt = project(rows_all, gain_attn, wt, cosine, sine, heads)
    table = jnp.stack([zig(core, i) for i in range(count)]).astype(jnp.int32)
    blocks = jnp.arange(total // BLOCK, dtype=jnp.int32)
    owned = jnp.any(blocks[:, None] == table[None, :], axis=1).astype(jnp.int32)
    ot, lse, top = attend(table, lengths, qt, k, vt)
    att = exchange(to_owner_kernel, ot, nt, 0, "to_owner")
    head_max = lax.pmax(jnp.max(top, axis=(1, 2, 3)), ("shard", "ctx"))
    factors = threshold[0] / jnp.maximum(head_max, threshold[0])
    root = jnp.repeat(jnp.sqrt(factors), HEAD_DIM)
    clipped_query = (w_query.astype(f32) * root[None, :]).astype(bf16)
    clipped_key = (w_key.astype(f32) * root[None, :]).astype(bf16)

    res, base, a2, comb = forward_rows(place, hidden_in, att, wo, gain_moe, wrc, vec, prev, routes)

    routes_all = lax.all_gather(routes, "ctx", axis=0, tiled=True)
    row_at, col_at = place_rows(routes_all, per)
    cot = (cotangent.astype(f32) * valid).astype(bf16)
    cot_all = lax.all_gather(cot, plane, axis=0, tiled=True)
    (g_slots,) = fetch_rows(first, row_at, None, cot_all, per, local, False)
    a2_all = lax.all_gather(a2, plane, axis=0, tiled=True)
    comb_all = lax.all_gather(comb, plane, axis=0, tiled=False)
    comb_all = comb_all.transpose(1, 0, 2).reshape(16, total)
    x_slots, gate_slots = fetch_rows(first, row_at, comb_all, a2_all, per, local, True)
    feeds, backs, grads = [], [], []
    for j in range(local):
        feed, back, grad = expert(j, first, x_slots, g_slots, gate_slots, expert_w[j])
        feeds.append(feed)
        backs.append(back)
        grads.append(grad)
    back = spread_rows(first, col_at, backs, per)
    back = lax.psum_scatter(back, plane, scatter_dimension=0, tiled=True)
    feed = spread_rows(first, col_at, feeds, per)
    feed = lax.psum_scatter(feed, plane, scatter_dimension=0, tiled=True)
    grads = [lax.psum_scatter(g, "shard", scatter_dimension=0, tiled=True)[0] for g in grads]

    dres, got, grad_out, small = backward_rows(
        place, res, back, cotangent, valid, att, wo, gain_moe, wrc, vec, prev, routes
    )
    got = exchange(to_heads_kernel, got, count, 1, "to_heads")
    dq, dk, dv = revisit(table, qt, k, kt, v, ot, got, lse)
    part, grad_qkv = unproject(owned, dq, dk, dv, cosine, sine, a1, wt)
    part = lax.psum_scatter(part, plane, scatter_dimension=0, tiled=True)
    grad_input, output, gain_row = finish_rows(
        hidden_in, part, dres, gain_attn, base, feed, valid
    )

    grad_expert = lax.all_gather(jnp.stack(grads), "ctx", axis=0, tiled=True).astype(f32)
    grad_gate, grad_up, grad_down = [grad_expert[:, k] for k in range(3)]
    grad_qkv = lax.psum_scatter(
        lax.psum(grad_qkv, "ctx").reshape(3 * head_width, ns, depth).transpose(1, 0, 2),
        "shard",
        scatter_dimension=0,
        tiled=False,
    )
    grad_q, grad_k, grad_v = [
        grad_qkv[i * head_width : (i + 1) * head_width].T.astype(f32) for i in range(3)
    ]
    grad_out = lax.psum_scatter(grad_out, "tp", scatter_dimension=0, tiled=True)
    grad_out = lax.psum(grad_out, "ctx").reshape(head_width, ns, depth).transpose(1, 0, 2)
    grad_out = lax.psum_scatter(grad_out, "shard", scatter_dimension=0, tiled=False).astype(f32)
    small = jnp.concatenate([small[:19], gain_row], axis=0)
    small = lax.psum(small, ("shard", "ctx", "tp"))
    small = lax.dynamic_slice_in_dim(small, lax.axis_index("shard") * depth, depth, 1)
    return (
        output,
        grad_input,
        small[19],
        grad_q,
        grad_k,
        grad_v,
        grad_out,
        small[18],
        small[:EXPERTS].T,
        small[EXPERTS : EXPERTS + 4].T,
        small[16:18],
        grad_gate,
        grad_up,
        grad_down,
        factors,
        clipped_query,
        clipped_key,
    )


def solution(mesh):
    return jax.shard_map(
        shards,
        mesh=mesh,
        in_specs=(
            P(("shard", "ctx", "tp"), None),
            P(("shard", "ctx", "tp"), None),
            P("shard"),
            P(("shard", "ctx"), None),
            P(("shard", "ctx"), None),
            P("shard"),
            P("shard", "tp"),
            P("shard", "tp"),
            P("shard", "tp"),
            P("tp", "shard"),
            P("shard"),
            P("shard", None),
            P("shard", None),
            P(None, "shard"),
            P(None, "shard", "tp"),
            P(None, "shard", "tp"),
            P(None, "shard", "tp"),
            P(),
        ),
        out_specs=(
            P(("shard", "ctx", "tp"), None),
            P(("shard", "ctx", "tp"), None),
            P("shard"),
            P("shard", "tp"),
            P("shard", "tp"),
            P("shard", "tp"),
            P("tp", "shard"),
            P("shard"),
            P("shard", None),
            P("shard", None),
            P(None, "shard"),
            P(None, "shard", "tp"),
            P(None, "shard", "tp"),
            P(None, "shard", "tp"),
            P("tp"),
            P("shard", "tp"),
            P("shard", "tp"),
        ),
        check_vma=False,
    )
```

time: 2490 us -> 1090 us (0.44)
  matrix products: 748 us -> 0 us
  waiting for transfers between devices: 952 us -> 612 us
  Pallas kernels: 0 us -> 314 us
  local copies, waits for them, and re-layouts: 305 us -> 32.8 us
  other arithmetic: 266 us -> 21.9 us
  blocking collectives: 176 us -> 83.6 us
    dot_general x56 -> x0, matrix products: 730 us -> none  [the longest x4 151 us: revisit(): jnp.einsum('hqk,qhd->khd', grad_scores, block, preferred_element_type=jnp...]
    pallas_call x0 -> x18, Pallas kernels: none -> 314 us  [the longest x4 56.3 us: expert(): pl.pallas_call(functools.partial(expert_kernel, j), grid_spec=pltpu.Prefe...]
    psum x3 -> x1, waiting for transfers between devices: 180 us -> 0.01 us  [shards(): lax.psum(grad_qkv, 'ctx').reshape(3 * head_width, ns, depth)]
    gather x11 -> x0, local copies, waits for them, and re-layouts: 112 us -> none  [the longest x7 37.7 us: mixture(): picked = jnp.take_along_axis(logits, chosen, axis=1)]
    unnamed x30 -> x21, waiting for transfers between devices: 96.4 us -> 3.83 us
    all_gather x14 -> x2, blocking collectives: 112 us -> 30 us  [the longest x1 24.2 us: shards(): comb_all = lax.all_gather(comb, plane, axis=0, tiled=False)]
    reduce_scatter x9 -> x10, waiting for transfers between devices: 449 us -> 376 us  [the longest x4 142 us: shards(): lax.psum_scatter(g, 'shard', scatter_dimension=0, tiled=True)[0]]
    reduce_max x6 -> x1, other arithmetic: 63.3 us -> 0.12 us  [shards(): head_max = lax.pmax(jnp.max(top, axis=(1, 2, 3)), ('shard', 'ctx'))]
  transfers between devices with their start and end apart: 26 -> 21, of which waited for: 17 -> 15; matrix products, arithmetic and copies ran while one was open for 20% -> 4% of each run, Pallas kernels for 0% -> 24%
where the time goes in v1:
time: 1090 us; the launch traced here: 1080 us
  waiting for transfers between devices  612 us (56%)
  Pallas kernels  314 us (29%)
  blocking collectives  83.6 us (8%)
  local copies, waits for them, and re-layouts  32.8 us (3%)
  other arithmetic  21.9 us (2%)
  between operations  16.4 us (2%)
    reduce_scatter x4, waiting for transfers between devices, shards(): lax.psum_scatter(g, 'shard', scatter_dimension=0, tiled=True)[0]  142 us
    all_gather x4, waiting for transfers between devices, shards(): gathered = lax.all_gather(jnp.stack(pieces), 'shard', axis=0, tiled=False)  133 us
    reduce_scatter x1, waiting for transfers between devices, shards(): part = lax.psum_scatter(part, plane, scatter_dimension=0, tiled=True)  65.2 us
    reduce_scatter x1, waiting for transfers between devices, shards(): back = lax.psum_scatter(back, plane, scatter_dimension=0, tiled=True)  64.9 us
    reduce_scatter x1, waiting for transfers between devices, shards(): feed = lax.psum_scatter(feed, plane, scatter_dimension=0, tiled=True)  56.9 us
    pallas_call x4, Pallas kernels, expert(): pl.pallas_call(functools.partial(expert_kernel, j), grid_spec=pltpu.Prefe...  56.3 us
    pallas_call x1, Pallas kernels, revisit(): pl.pallas_call(revisit_kernel, grid_spec=pltpu.PrefetchScalarGridSpec(num...  50.1 us
    all_gather x1, waiting for transfers between devices, shards(): rows_all = lax.all_gather(hidden_in, plane, axis=0, tiled=True)  45 us
  transfers between devices with their start and end apart: 21, of which 15 were waited for; matrix products, arithmetic and copies ran while one was open for 4% of the time, Pallas kernels for 24%

profile of v1, /device:TPU:0, one launch (start us, length us, event | category | flops | bytes accessed | tf_op | source)
XLA Modules:
  0.0 1081.9 jit_solution(7734053188610688394)
XLA Ops:
  14.3 36.6 %all-gather.19.cloned.1.call-done = bf16[768,800]{1,0:T(8,128)(2,1)} async-done(((bf16[192,800]{1,0:T(8,128)(2,1)}), bf16[768,800]{1,0:T(8,128)(2,1)}) %all-gather.19.cloned.1.call-update) | async-done | bytes 1228816 | tf_op jit(solution)/shard_map/all_gather | solution.py:856
  65.5 17.9 %all-gather.27.cloned.1.call-done = bf16[3072,192]{1,0:T(8,128)(2,1)} async-done(((bf16[768,192]{1,0:T(8,128)(2,1)}), bf16[3072,192]{1,0:T(8,128)(2,1)}) %all-gather.27.cloned.1.call-update) | async-done | bytes 1179664 | tf_op jit(solution)/shard_map/all_gather | solution.py:868
  85.8 45.0 %all-gather.17.cloned.1.call-done.x_ref = bf16[4096,768]{1,0:T(8,128)(2,1)} async-done(((bf16[512,768]{1,0:T(8,128)(2,1)}), bf16[4096,768]{1,0:T(8,128)(2,1)}) %all-gather.17.cloned.1.call-update) | async-done | bytes 6291472 | tf_op jit(solution)/shard_map/all_gather | solution.py:855
  130.8 13.1 %project.1 = (bf16[4096,768]{1,0:T(8,128)(2,1)}, bf16[3,64,4096]{2,1,0:T(8,128)(2,1)}, bf16[3,64,4096]{2,1,0:T(8,128)(2,1)}, bf16[3,4096,64]{2,1,0:T(8,128)(2,1)...) custom-call(bf16[4096,768]{1,0:T(8,128)(2,1)} %all-gather.17.cloned.1.call-done.x_ref, ...), custom_call_target="tpu_custom_call" | custom-call | tf_op jit(solution)/shard_map/project/pallas_call | solution.py:78
  143.9 34.8 %attend.1 = (bf16[4,192,512]{2,1,0:T(8,128)(2,1)}, f32[3,4,1,512]{3,2,1,0:T(1,128)}, f32[3,4,1,512]{3,2,1,0:T(1,128)}) custom-call(s32[4]{0:T(128)} %pad_add_fusion.table, s32[1]{0:T(128)} %copy.126.length, bf16[3,64,4096]{2,1,0:T(8,128)(2,1)} %get-tuple-element.58.qt_ref, bf16[3,4096,64]{2,1,0:T(8,128)(2,1)} %get-tuple-element.59.k_ref, ...), custom_call_target="tpu_custom_call" | custom-call | tf_op jit(solution)/shard_map/attend/pallas_call | solution.py:140
  216.6 24.2 %all-gather.1 = f32[128,512]{1,0:T(8,128)S(1)} all-gather(f32[16,512]{1,0:T(8,128)S(1)} %copy-done.8), channel_id=3, replica_groups=mesh['shard'=4,'ctx'=2,'tp'=4] {'ctx','tp'}, dimensions={0}, use_global_device_ids=true | all-gather | bytes 294912 | tf_op jit(solution)/shard_map/all_gather | solution.py:901
  241.6 17.9 %fetch_rows.3.g_ref = bf16[4,1024,768]{2,1,0:T(8,128)(2,1)} custom-call(s32[1]{0:T(128)} %bitcast.14.first.f, f32[16,4096]{1,0:T(8,128)} %get-tuple-element.66.row_ref.p, bf16[4096,768]{1,0:T(8,128)(2,1)} %all-gather.23.cloned.1.call-done.r), custom_call_target="tpu_custom_call" | custom-call | tf_op jit(solution)/shard_map/fetch_rows/pallas_call | solution.py:689
  259.5 19.0 %fetch_rows.2 = (bf16[4,1024,768]{2,1,0:T(8,128)(2,1)}, f32[4,1024,1]{2,1,0:T(8,128)}) custom-call(s32[1]{0:T(128)} %bitcast.14.first.f, f32[16,4096]{1,0:T(8,128)} %get-tuple-element.66.row_ref.p, f32[16,4096]{1,0:T(8,128)} %bitcast.90, bf16[4096,768]{1,0:T(8,128)(2,1)} %all-gather.21.cloned.1.call-done.rows_ref), custom_call_target="tpu_custom_call" | custom-call | tf_op jit(solution)/shard_map/fetch_rows/pallas_call | solution.py:689
  278.5 22.4 %all-gather.35.cloned.1.call-done = bf16[12,192,512]{2,1,0:T(8,128)(2,1)} async-done(((bf16[3,192,512]{2,1,0:T(8,128)(2,1)}), bf16[12,192,512]{2,1,0:T(8,128)(2,1)}) %all-gather.35.cloned.1.call-update) | async-done | bytes 2359312 | tf_op jit(solution)/shard_map/all_gather | solution.py:863
  300.9 14.0 %expert.7 = (bf16[1024,768]{1,0:T(8,128)(2,1)}, bf16[1024,896]{1,0:T(8,128)(2,1)}, bf16[4,3,192,512]{3,2,1,0:T(8,128)(2,1)}) custom-call(s32[1]{0:T(128)} %bitcast.14.first.f, bf16[4,1024,768]{2,1,0:T(8,128)(2,1)} %get-tuple-element.69.x_ref, bf16[4,1024,768]{2,1,0:T(8,128)(2,1)} %fetch_rows.3.g_ref, f32[4,1024,1]{2,1,0:T(8,128)} %get-tuple-element.70.gate_ref, ...), custom_call_target="tpu_custom_call" | custom-call | tf_op jit(solution)/shard_map/expert/pallas_call | solution.py:744
  314.9 36.9 %all-gather.33.cloned.1.call-done = bf16[12,192,512]{2,1,0:T(8,128)(2,1)} async-done(((bf16[3,192,512]{2,1,0:T(8,128)(2,1)}), bf16[12,192,512]{2,1,0:T(8,128)(2,1)}) %all-gather.33.cloned.1.call-update) | async-done | bytes 2359312 | tf_op jit(solution)/shard_map/all_gather | solution.py:863
  351.8 14.0 %expert.6 = (bf16[1024,768]{1,0:T(8,128)(2,1)}, bf16[1024,896]{1,0:T(8,128)(2,1)}, bf16[4,3,192,512]{3,2,1,0:T(8,128)(2,1)}) custom-call(s32[1]{0:T(128)} %bitcast.14.first.f, bf16[4,1024,768]{2,1,0:T(8,128)(2,1)} %get-tuple-element.69.x_ref, bf16[4,1024,768]{2,1,0:T(8,128)(2,1)} %fetch_rows.3.g_ref, f32[4,1024,1]{2,1,0:T(8,128)} %get-tuple-element.70.gate_ref, ...), custom_call_target="tpu_custom_call" | custom-call | tf_op jit(solution)/shard_map/expert/pallas_call | solution.py:744
  365.8 36.9 %all-gather.31.cloned.1.call-done = bf16[12,192,512]{2,1,0:T(8,128)(2,1)} async-done(((bf16[3,192,512]{2,1,0:T(8,128)(2,1)}), bf16[12,192,512]{2,1,0:T(8,128)(2,1)}) %all-gather.31.cloned.1.call-update) | async-done | bytes 2359312 | tf_op jit(solution)/shard_map/all_gather | solution.py:863
  402.7 14.2 %expert.5 = (bf16[1024,768]{1,0:T(8,128)(2,1)}, bf16[1024,896]{1,0:T(8,128)(2,1)}, bf16[4,3,192,512]{3,2,1,0:T(8,128)(2,1)}) custom-call(s32[1]{0:T(128)} %bitcast.14.first.f, bf16[4,1024,768]{2,1,0:T(8,128)(2,1)} %get-tuple-element.69.x_ref, bf16[4,1024,768]{2,1,0:T(8,128)(2,1)} %fetch_rows.3.g_ref, f32[4,1024,1]{2,1,0:T(8,128)} %get-tuple-element.70.gate_ref, ...), custom_call_target="tpu_custom_call" | custom-call | tf_op jit(solution)/shard_map/expert/pallas_call | solution.py:744
  416.9 36.7 %all-gather.29.cloned.1.call-done = bf16[12,192,512]{2,1,0:T(8,128)(2,1)} async-done(((bf16[3,192,512]{2,1,0:T(8,128)(2,1)}), bf16[12,192,512]{2,1,0:T(8,128)(2,1)}) %all-gather.29.cloned.1.call-update) | async-done | bytes 2359312 | tf_op jit(solution)/shard_map/all_gather | solution.py:863
  453.6 14.1 %expert.4 = (bf16[1024,768]{1,0:T(8,128)(2,1)}, bf16[1024,896]{1,0:T(8,128)(2,1)}, bf16[4,3,192,512]{3,2,1,0:T(8,128)(2,1)}) custom-call(s32[1]{0:T(128)} %bitcast.14.first.f, bf16[4,1024,768]{2,1,0:T(8,128)(2,1)} %get-tuple-element.69.x_ref, bf16[4,1024,768]{2,1,0:T(8,128)(2,1)} %fetch_rows.3.g_ref, f32[4,1024,1]{2,1,0:T(8,128)} %get-tuple-element.70.gate_ref, ...), custom_call_target="tpu_custom_call" | custom-call | tf_op jit(solution)/shard_map/expert/pallas_call | solution.py:744
  467.7 22.4 %spread_rows.2 = bf16[4096,896]{1,0:T(8,128)(2,1)} custom-call(s32[1]{0:T(128)} %bitcast.14.first.f, f32[4096,16]{1,0:T(8,128)} %get-tuple-element.65.col_ref, bf16[1024,896]{1,0:T(8,128)(2,1)} %get-tuple-element.71.refs_0_, bf16[1024,896]{1,0:T(8,128)(2,1)} %get-tuple-element.72.refs_1_, bf16[1024,896]{1,0:T(8,128)(2,1)} %get-tuple-element.73.refs_2_, ...), custom_call_target="tpu_custom_call" | custom-call | tf_op jit(solution)/shard_map/spread_rows/pallas_call | solution.py:788
  491.0 64.9 %reduce-scatter.11.cloned.1.call-done.dn_ref = bf16[512,896]{1,0:T(8,128)(2,1)} async-done(((bf16[4096,896]{1,0:T(8,128)(2,1)}), bf16[512,896]{1,0:T(8,128)(2,1)}) %reduce-scatter.11.cloned.1.call-update) | async-done | bytes 917520 | tf_op jit(solution)/shard_map/reduce_scatter | solution.py:911
  556.0 15.4 %backward_rows.1 = (f32[512,768]{1,0:T(8,128)}, bf16[4,192,512]{2,1,0:T(8,128)(2,1)}, bf16[768,768]{1,0:T(8,128)(2,1)}, f32[24,768]{1,0:T(8,128)}) custom-call(s32[1]{0:T(128)} %bitcast.8.place, f32[512,768]{1,0:T(8,128)} %get-tuple-element.64.res_ref, bf16[512,896]{1,0:T(8,128)(2,1)} %reduce-scatter.11.cloned.1.call-done.dn_ref, bf16[512,768]{1,0:T(8,128)(2,1)} %cot_ref.1, ...), custom_call_target="tpu_custom_call" | custom-call | tf_op jit(solution)/shard_map/backward_rows/pallas_call | solution.py:568
  574.5 18.2 %to_heads.1.got_ref = bf16[4,192,512]{2,1,0:T(8,128)(2,1)} custom-call(bf16[4,192,512]{2,1,0:T(8,128)(2,1)} %get-tuple-element.75.o_ref), custom_call_target="tpu_custom_call" | custom-call | tf_op jit(solution)/shard_map/to_heads/pallas_call | solution.py:420
  592.8 50.1 %revisit.1 = (f32[3,64,4096]{2,1,0:T(8,128)}, f32[3,64,4096]{2,1,0:T(8,128)}, f32[3,64,4096]{2,1,0:T(8,128)}) custom-call(s32[4]{0:T(128)} %pad_add_fusion.table, bf16[3,64,4096]{2,1,0:T(8,128)(2,1)} %get-tuple-element.58.qt_ref, bf16[3,4096,64]{2,1,0:T(8,128)(2,1)} %get-tuple-element.59.k_ref, bf16[3,64,4096]{2,1,0:T(8,128)(2,1)} %get-tuple-element.60.kt_ref, ...), custom_call_target="tpu_custom_call" | custom-call | tf_op jit(solution)/shard_map/revisit/pallas_call | solution.py:209
  642.8 18.2 %unproject.1 = (bf16[4096,768]{1,0:T(8,128)(2,1)}, bf16[576,768]{1,0:T(8,128)(2,1)}) custom-call(s32[8]{0:T(128)} %convert_element_type.101.owned, f32[3,64,4096]{2,1,0:T(8,128)} %get-tuple-element.77.dq_ref, f32[3,64,4096]{2,1,0:T(8,128)} %get-tuple-element.78.dk_ref, f32[3,64,4096]{2,1,0:T(8,128)} %get-tuple-element.79.dv_ref, ...), custom_call_target="tpu_custom_call" | custom-call | tf_op jit(solution)/shard_map/unproject/pallas_call | solution.py:269
  665.6 42.1 %reduce-scatter.23.cloned.1.call-done = bf16[1,3,192,512]{3,2,1,0:T(8,128)(2,1)} async-done(((bf16[4,3,192,512]{3,2,1,0:T(8,128)(2,1)}), bf16[1,3,192,512]{3,2,1,0:T(8,128)(2,1)}) %reduce-scatter.23.cloned.1.call-update) | async-done | bytes 589840 | tf_op jit(solution)/shard_map/reduce_scatter | solution.py:914
  707.6 49.8 %reduce-scatter.21.cloned.1.call-done = bf16[1,3,192,512]{3,2,1,0:T(8,128)(2,1)} async-done(((bf16[4,3,192,512]{3,2,1,0:T(8,128)(2,1)}), bf16[1,3,192,512]{3,2,1,0:T(8,128)(2,1)}) %reduce-scatter.21.cloned.1.call-update) | async-done | bytes 589840 | tf_op jit(solution)/shard_map/reduce_scatter | solution.py:914
  757.5 49.8 %reduce-scatter.19.cloned.1.call-done = bf16[1,3,192,512]{3,2,1,0:T(8,128)(2,1)} async-done(((bf16[4,3,192,512]{3,2,1,0:T(8,128)(2,1)}), bf16[1,3,192,512]{3,2,1,0:T(8,128)(2,1)}) %reduce-scatter.19.cloned.1.call-update) | async-done | bytes 589840 | tf_op jit(solution)/shard_map/reduce_scatter | solution.py:914
  810.7 25.1 %reduce-scatter.27.cloned.1.call-done = bf16[1,576,192]{1,2,0:T(8,128)(2,1)} async-done(((bf16[4,576,192]{1,2,0:T(8,128)(2,1)}), bf16[1,576,192]{1,2,0:T(8,128)(2,1)}) %reduce-scatter.27.cloned.1.call-update) | async-done | bytes 221200 | tf_op jit(solution)/shard_map/reduce_scatter | solution.py:929
  835.8 21.9 %reduce-scatter.29.cloned.1.call-done = bf16[1,192,192]{2,1,0:T(8,128)(2,1)} async-done(((bf16[4,192,192]{2,1,0:T(8,128)(2,1)}), bf16[1,192,192]{2,1,0:T(8,128)(2,1)}) %reduce-scatter.29.cloned.1.call-update) | async-done | bytes 73744 | tf_op jit(solution)/shard_map/reduce_scatter | solution.py:940
  857.8 18.9 %spread_rows.3 = bf16[4096,768]{1,0:T(8,128)(2,1)} custom-call(s32[1]{0:T(128)} %bitcast.14.first.f, f32[4096,16]{1,0:T(8,128)} %get-tuple-element.65.col_ref, bf16[1024,768]{1,0:T(8,128)(2,1)} %get-tuple-element.84.refs_0_, bf16[1024,768]{1,0:T(8,128)(2,1)} %get-tuple-element.85.refs_1_, bf16[1024,768]{1,0:T(8,128)(2,1)} %get-tuple-element.86.refs_2_, ...), custom_call_target="tpu_custom_call" | custom-call | tf_op jit(solution)/shard_map/spread_rows/pallas_call | solution.py:788
  878.3 13.6 %pmax.7 = f32[3]{0:T(128)S(1)} all-reduce(f32[3]{0:T(128)S(1)} %reduce_max.9), channel_id=1, replica_groups=mesh['shard'=4,'ctx'=2,'tp'=4] {'shard','ctx'}, use_global_device_ids=true, to_apply=%region_15.16 | all-reduce | flops 3 | bytes 24 | tf_op jit(solution)/shard_map/pmax | solution.py:887
  904.4 56.9 %reduce-scatter.15.cloned.1.call-done.feed_ref = bf16[512,768]{1,0:T(8,128)(2,1)} async-done(((bf16[4096,768]{1,0:T(8,128)(2,1)}), bf16[512,768]{1,0:T(8,128)(2,1)}) %reduce-scatter.15.cloned.1.call-update) | async-done | bytes 786448 | tf_op jit(solution)/shard_map/reduce_scatter | solution.py:913
  961.2 65.2 %reduce-scatter.13.cloned.1.call-done.dn_ref = bf16[512,768]{1,0:T(8,128)(2,1)} async-done(((bf16[4096,768]{1,0:T(8,128)(2,1)}), bf16[512,768]{1,0:T(8,128)(2,1)}) %reduce-scatter.13.cloned.1.call-update) | async-done | bytes 786448 | tf_op jit(solution)/shard_map/reduce_scatter | solution.py:922
  1032.0 40.0 %psum.21 = f32[20,768]{1,0:T(8,128)S(1)} all-reduce(f32[20,768]{1,0:T(8,128)S(1)} %pad_maximum_fusion.5), channel_id=1, replica_groups=mesh['shard'=4,'ctx'=2,'tp'=4] {'shard','ctx','tp'}, use_global_device_ids=true, to_apply=%region_4.5 | all-reduce | flops 15360 | bytes 122880 | tf_op jit(solution)/shard_map/psum | solution.py:942
  (136 shorter events, 95.4 us)
Async XLA Ops:
  7.2 47.3 %copy-start.2 = (bf16[512,768]{1,0:T(8,128)(2,1)S(1)}, bf16[512,768]{1,0:T(8,128)(2,1)}, u32[]{:S(2)}) copy-start(bf16[512,768]{1,0:T(8,128)(2,1)} %cot_ref.1) | copy-start | bytes 2359300
  7.2 43.8 %all-gather.19.cloned.1.call-start = ((), (), s32[]{:S(2)}) async-start(), calls=%async_computation.11 | async-start | bytes 1720320 | tf_op jit(solution)/shard_map/all_gather | solution.py:856
  14.3 41.4 %copy-start.10 = (s32[2048,2]{0,1:T(2,128)S(1)}, s32[2048,2]{0,1:T(2,128)}, u32[]{:S(2)}) copy-start(s32[2048,2]{0,1:T(2,128)} %param.21) | copy-start | bytes 49156
  14.3 69.0 %all-gather.27.cloned.1.call-start = ((), (), s32[]{:S(2)}) async-start(), calls=%async_computation.23 | async-start | bytes 1966080 | tf_op jit(solution)/shard_map/all_gather | solution.py:868
  53.0 4.1 copy-start.6
  53.0 77.8 %all-gather.17.cloned.1.call-start = ((), (), s32[]{:S(2)}) async-start(), calls=%async_computation.10 | async-start | bytes 7077888 | tf_op jit(solution)/shard_map/all_gather | solution.py:855
  53.7 187.9 %all-gather.23.cloned.1.call-start = ((), (), s32[]{:S(2)}) async-start(), calls=%async_computation.13 | async-start | bytes 7077888 | tf_op jit(solution)/shard_map/all_gather | solution.py:898
  55.6 203.9 %all-gather.21.cloned.1.call-start = ((), (), s32[]{:S(2)}) async-start(), calls=%async_computation.12 | async-start | bytes 7077888 | tf_op jit(solution)/shard_map/all_gather | solution.py:900
  57.0 4.8 slice-start
  58.4 3.6 slice-start.1
  191.2 7.9 copy-start.3
  199.0 101.9 %all-gather.35.cloned.1.call-start = ((), (), s32[]{:S(2)}) async-start(), calls=%async_computation.27 | async-start | bytes 2949120 | tf_op jit(solution)/shard_map/all_gather | solution.py:863
  201.7 150.1 %all-gather.33.cloned.1.call-start = ((), (), s32[]{:S(2)}) async-start(), calls=%async_computation.26 | async-start | bytes 2949120 | tf_op jit(solution)/shard_map/all_gather | solution.py:863
  202.6 2.0 copy-start.1
  202.7 200.0 %all-gather.31.cloned.1.call-start = ((), (), s32[]{:S(2)}) async-start(), calls=%async_computation.25 | async-start | bytes 2949120 | tf_op jit(solution)/shard_map/all_gather | solution.py:863
  203.6 250.0 %all-gather.29.cloned.1.call-start = ((), (), s32[]{:S(2)}) async-start(), calls=%async_computation.24 | async-start | bytes 2949120 | tf_op jit(solution)/shard_map/all_gather | solution.py:863
  204.6 351.4 %reduce-scatter.11.cloned.1.call-start = ((), (), s32[]{:S(2)}) async-start(), calls=%async_computation.14 | async-start | bytes 8257536 | tf_op jit(solution)/shard_map/reduce_scatter | solution.py:911
  210.4 6.2 copy-start.8
  490.0 173.3 %reduce-scatter.17.cloned.1.call-start = ((), (), s32[]{:S(2)}) async-start(), calls=%async_computation.17 | async-start | bytes 1474560 | tf_op jit(solution)/shard_map/reduce_scatter | solution.py:938
  571.4 94.2 %reduce-scatter.25.cloned.1.call-start = ((), (), s32[]{:S(2)}) async-start(), calls=%async_computation.21 | async-start | bytes 2949120 | tf_op jit(solution)/shard_map/reduce_scatter | solution.py:914
  571.9 135.7 %reduce-scatter.23.cloned.1.call-start = ((), (), s32[]{:S(2)}) async-start(), calls=%async_computation.20 | async-start | bytes 2949120 | tf_op jit(solution)/shard_map/reduce_scatter | solution.py:914
  572.7 184.8 %reduce-scatter.21.cloned.1.call-start = ((), (), s32[]{:S(2)}) async-start(), calls=%async_computation.19 | async-start | bytes 2949120 | tf_op jit(solution)/shard_map/reduce_scatter | solution.py:914
  573.3 234.0 %reduce-scatter.19.cloned.1.call-start = ((), (), s32[]{:S(2)}) async-start(), calls=%async_computation.18 | async-start | bytes 2949120 | tf_op jit(solution)/shard_map/reduce_scatter | solution.py:914
  573.8 262.0 %reduce-scatter.27.cloned.1.call-start = ((), (), s32[]{:S(2)}) async-start(), calls=%async_computation.28 | async-start | bytes 1228800 | tf_op jit(solution)/shard_map/reduce_scatter | solution.py:929
  663.3 194.4 %reduce-scatter.29.cloned.1.call-start = ((), (), s32[]{:S(2)}) async-start(), calls=%async_computation.29 | async-start | bytes 491520 | tf_op jit(solution)/shard_map/reduce_scatter | solution.py:940
  665.5 227.7 %all-gather.25.cloned.1.call-start = ((), (), s32[]{:S(2)}) async-start(), calls=%async_computation.22 | async-start | bytes 7077888 | tf_op jit(solution)/shard_map/all_gather | solution.py:927
  810.6 90.3 %all-reduce.4.cloned.1.call-start = ((), (), s32[]{:S(2)}) async-start(), calls=%async_computation.30 | async-start | bytes 688128 | tf_op jit(solution)/shard_map/psum | solution.py:930
  857.7 103.5 %reduce-scatter.15.cloned.1.call-start = ((), (), s32[]{:S(2)}) async-start(), calls=%async_computation.16 | async-start | bytes 7077888 | tf_op jit(solution)/shard_map/reduce_scatter | solution.py:913
  876.7 149.7 %reduce-scatter.13.cloned.1.call-start = ((), (), s32[]{:S(2)}) async-start(), calls=%async_computation.15 | async-start | bytes 7077888 | tf_op jit(solution)/shard_map/reduce_scatter | solution.py:922
  876.8 15.7 %copy-start.4 = (bf16[192,192]{1,0:T(8,128)(2,1)S(1)}, bf16[192,192]{1,0:T(8,128)(2,1)}, u32[]{:S(2)}) copy-start(bf16[192,192]{1,0:T(8,128)(2,1)} %param.24) | copy-start | bytes 221188
  876.8 15.7 %copy-start.5 = (bf16[192,192]{1,0:T(8,128)(2,1)S(1)}, bf16[192,192]{1,0:T(8,128)(2,1)}, u32[]{:S(2)}) copy-start(bf16[192,192]{1,0:T(8,128)(2,1)} %param.25) | copy-start | bytes 221188
  1026.4 4.9 copy-start.7
  (3 other events, 3.8 us)
Sparse Core Ops, SparseCore 0:
  14.4 36.5 all-gather.18
  53.4 29.9 all-gather.26
  85.2 45.5 all-gather.16
  132.5 45.5 all-gather.22
  199.1 49.8 all-gather.20
  250.4 50.5 all-gather.34
  302.5 49.2 all-gather.32
  353.4 49.2 all-gather.30
  404.3 49.2 all-gather.28
  490.2 65.7 reduce-scatter.10
  571.5 35.8 reduce-scatter.16
  609.6 48.0 reduce-scatter.24
  660.1 47.5 reduce-scatter.22
  709.9 47.5 reduce-scatter.20
  759.7 47.5 reduce-scatter.18
  810.2 25.5 reduce-scatter.26
  838.5 19.1 reduce-scatter.28
  859.8 12.6 all-gather.24
  875.0 19.5 all-reduce.3
  898.2 62.9 reduce-scatter.14
  964.6 61.7 reduce-scatter.12

commit v2 on v1

--- a/solution.py
+++ b/solution.py
@@ -36,6 +36,10 @@
     return pltpu.CompilerParams(vmem_limit_bytes=mib * 1024 * 1024, **more)
 
 
+def cost(us):
+    return pl.CostEstimate(flops=int(us * 1e9), bytes_accessed=int(us * 3e6), transcendentals=0)
+
+
 def full(shape):
     return pl.BlockSpec(shape, lambda *_: (0,) * len(shape))
 
@@ -44,14 +48,13 @@
     return 4 * (i // 2) + (core if i % 2 == 0 else 3 - core)
 
 
-def qkv_kernel(x_ref, gain_ref, wt_ref, cos_ref, sin_ref, a_ref, qt_ref, kt_ref, k_ref, v_ref, vt_ref):
+def qkv_kernel(x_ref, gain_ref, wt_ref, cos_ref, sin_ref, qt_ref, kt_ref, k_ref, v_ref, vt_ref):
     heads = qt_ref.shape[0]
     width = heads * HEAD_DIM
     half = HEAD_DIM // 2
     x = x_ref[...].astype(f32)
     inverse = lax.rsqrt(jnp.mean(x * x, axis=1, keepdims=True) + epsilon)
     a = (x * inverse * gain_ref[...]).astype(bf16)
-    a_ref[...] = a
     y = mm(wt_ref[...], a, NT)
     c, s = cos_ref[...], sin_ref[...]
 
@@ -86,7 +89,6 @@
             pl.BlockSpec((HEAD_DIM // 2, tile), lambda i: (0, i)),
         ],
         out_specs=[
-            pl.BlockSpec((tile, width), lambda i: (i, 0)),
             pl.BlockSpec((heads, HEAD_DIM, tile), lambda i: (0, 0, i)),
             pl.BlockSpec((heads, HEAD_DIM, tile), lambda i: (0, 0, i)),
             pl.BlockSpec((heads, tile, HEAD_DIM), lambda i: (0, i, 0)),
@@ -94,7 +96,6 @@
             pl.BlockSpec((heads, HEAD_DIM + 16, tile), lambda i: (0, 0, i)),
         ],
         out_shape=[
-            jax.ShapeDtypeStruct((total, width), bf16),
             jax.ShapeDtypeStruct((heads, HEAD_DIM, total), bf16),
             jax.ShapeDtypeStruct((heads, HEAD_DIM, total), bf16),
             jax.ShapeDtypeStruct((heads, total, HEAD_DIM), bf16),
@@ -102,6 +103,7 @@
             jax.ShapeDtypeStruct((heads, HEAD_DIM + 16, total), bf16),
         ],
         compiler_params=params(),
+        cost_estimate=cost(13),
         name="project",
     )(rows, gain, wt, cosine, sine)
 
@@ -159,6 +161,7 @@
             jax.ShapeDtypeStruct((heads, count, 1, BLOCK), f32),
         ],
         compiler_params=params(),
+        cost_estimate=cost(35),
         name="attend",
     )(table, length, qt, k, vt)
 
@@ -228,11 +231,13 @@
         ),
         out_shape=[jax.ShapeDtypeStruct((heads, HEAD_DIM, total), f32)] * 3,
         compiler_params=params(),
+        cost_estimate=cost(50),
         name="revisit",
     )(table, qt, k, kt, v, ot, got, lse)
 
 
-def unproject_kernel(owned, dq_ref, dk_ref, dv_ref, cos_ref, sin_ref, a_ref, wt_ref, part_ref, gw_ref, total):
+def unproject_kernel(owned, dq_ref, dk_ref, dv_ref, cos_ref, sin_ref, x_ref, gain_ref, wt_ref, go_ref, small_ref,
+                     part_ref, gw_ref, smalls_ref, total, row):
     heads = dq_ref.shape[0]
     half = HEAD_DIM // 2
     i = pl.program_id(0)
@@ -242,30 +247,50 @@
         u, w = g[:half], g[half:]
         return jnp.concatenate([u * c + w * s, w * c - u * s], axis=0)
 
+    @pl.when(i == 0)
+    def _():
+        total[...] = jnp.zeros_like(total)
+        row[...] = jnp.zeros_like(row)
+
+    x = x_ref[...].astype(f32)
+    m = x * lax.rsqrt(jnp.mean(x * x, axis=1, keepdims=True) + epsilon)
+    a = (m * gain_ref[...]).astype(bf16)
     mine = owned[i] > 0
     pieces = [turned(jnp.where(mine, dq_ref[h], 0.0)) for h in range(heads)]
     pieces += [turned(dk_ref[h]) for h in range(heads)]
     pieces += [dv_ref[h] for h in range(heads)]
     grads = jnp.concatenate(pieces, axis=0).astype(bf16)
-    part_ref[...] = mm(grads, wt_ref[...], TN).astype(bf16)
-
-    @pl.when(i == 0)
-    def _():
-        total[...] = jnp.zeros_like(total)
-
-    total[...] += mm(grads, a_ref[...])
+    part = mm(grads, wt_ref[...], TN)
+    part_ref[...] = part.astype(bf16)
+    row[...] += jnp.sum(part * m, axis=0, keepdims=True)
+    total[...] += mm(grads, a)
 
     @pl.when(i == pl.num_programs(0) - 1)
     def _():
-        gw_ref[...] = total[...].astype(bf16)
-
-
-def unproject(owned, dq, dk, dv, cosine, sine, a, wt):
+        _, parts, rows, depth = gw_ref.shape
+        mid = rows // 2
+        at = lax.broadcasted_iota(jnp.int32, small_ref.shape, 0)
+        smalls = small_ref[...] + jnp.where(at == 19, row[...], 0.0)
+        for z in range(parts):
+            here = slice(z * depth, (z + 1) * depth)
+            gw_ref[0, z] = total[:rows, here].astype(bf16)
+            gw_ref[1, z, :mid] = total[rows:, here].astype(bf16)
+            gw_ref[1, z, mid:] = go_ref[:, here]
+            smalls_ref[z] = smalls[:, here]
+
+
+def unproject(owned, dq, dk, dv, cosine, sine, x, gain, wt, go, small, parts):
     heads, _, rows = dq.shape
-    width = a.shape[1]
+    width = x.shape[1]
     out = wt.shape[0]
+    depth = width // parts
     piece = pl.BlockSpec((heads, HEAD_DIM, BLOCK), lambda i, o: (0, 0, i))
     table = pl.BlockSpec((HEAD_DIM // 2, BLOCK), lambda i, o: (0, i))
+    shapes = [
+        jax.ShapeDtypeStruct((rows, width), bf16),
+        jax.ShapeDtypeStruct((2, parts, 2 * heads * HEAD_DIM, depth), bf16),
+        jax.ShapeDtypeStruct((parts,) + small.shape[:1] + (depth,), f32),
+    ]
     return pl.pallas_call(
         unproject_kernel,
         grid_spec=pltpu.PrefetchScalarGridSpec(
@@ -278,50 +303,383 @@
                 table,
                 table,
                 pl.BlockSpec((BLOCK, width), lambda i, o: (i, 0)),
-                full((out, width)),
+                full(gain.shape),
+                full(wt.shape),
+                full(go.shape),
+                full(small.shape),
             ],
-            out_specs=[pl.BlockSpec((BLOCK, width), lambda i, o: (i, 0)), full((out, width))],
-            scratch_shapes=[pltpu.VMEM((out, width), f32)],
+            out_specs=[pl.BlockSpec((BLOCK, width), lambda i, o: (i, 0))] + [full(v.shape) for v in shapes[1:]],
+            scratch_shapes=[pltpu.VMEM((out, width), f32), pltpu.VMEM((1, width), f32)],
         ),
-        out_shape=[
-            jax.ShapeDtypeStruct((rows, width), bf16),
-            jax.ShapeDtypeStruct((out, width), bf16),
-        ],
+        out_shape=shapes,
         compiler_params=params(),
+        cost_estimate=cost(18),
         name="unproject",
-    )(owned, dq, dk, dv, cosine, sine, a, wt)
-
-
-def greet(me_c, me_t, nc, nt):
+    )(owned, dq, dk, dv, cosine, sine, x, gain, wt, go, small)
+
+
+def spot():
+    return lax.axis_index("shard"), lax.axis_index("ctx"), lax.axis_index("tp")
+
+
+def across(t):
+    return t + 1 - 2 * lax.rem(t, 2), lax.rem(t + 2, 4), 3 - t
+
+
+def remote(source, target, sends, recvs, **where):
+    return pltpu.make_async_remote_copy(
+        src_ref=source,
+        dst_ref=target,
+        send_sem=sends,
+        recv_sem=recvs,
+        device_id=where,
+        device_id_type=MESH,
+    )
+
+
+def greet(depth=True):
+    z, c, t = spot()
+    nc, nt, ns = lax.axis_size("ctx"), lax.axis_size("tp"), lax.axis_size("shard")
     barrier = pltpu.get_barrier_semaphore()
     for step in range(1, nc * nt):
-        other = lax.rem(me_c * nt + me_t + step, nc * nt)
+        other = lax.rem(c * nt + t + step, nc * nt)
         pl.semaphore_signal(
             barrier,
             inc=1,
             device_id={"ctx": other // nt, "tp": lax.rem(other, nt)},
             device_id_type=MESH,
         )
-    pl.semaphore_wait(barrier, nc * nt - 1)
-
-
-def to_owner_kernel(nc, nt, o_ref, att_ref, send_sem, recv_sem, local_sem):
-    c, t = lax.axis_index("ctx"), lax.axis_index("tp")
+    if depth:
+        for step in range(1, ns):
+            pl.semaphore_signal(
+                barrier,
+                inc=1,
+                device_id={"shard": lax.rem(z + step, ns)},
+                device_id_type=MESH,
+            )
+    pl.semaphore_wait(barrier, nc * nt - 1 + (ns - 1 if depth else 0))
+
+
+class Gather:
+    KINDS = 9
+
+    def __init__(self, x, out, sends, recvs, own, cuts):
+        z, c, t = spot()
+        tx, ty, td = across(t)
+        rows = x.shape[0] // cuts
+        half = rows // 2
+        self.cuts = cuts
+        self.own = pltpu.make_async_copy(x, out.at[4 * c + t], own)
+        sib = {"ctx": 1 - c}
+        px, py = {"tp": tx}, {"tp": ty}
+
+        def copies(s):
+            whole = pl.ds(s * rows, rows)
+            one, two = pl.ds(s * rows, half), pl.ds(s * rows + half, half)
+
+            def at(k, source, target, where):
+                return remote(source, target, sends.at[s, k], recvs.at[s, k], **where)
+
+            def keep(k, slot, part, where):
+                ref = out.at[4 * c + slot, part]
+                return at(k, ref, ref, where)
+
+            mine = [
+                at(k, x.at[whole], out.at[4 * c + t, whole], where)
+                for k, where in enumerate((px, py, sib))
+            ]
+            return mine + [
+                keep(3, tx, whole, sib),
+                keep(4, tx, one, py),
+                keep(5, ty, whole, sib),
+                keep(6, ty, two, px),
+                keep(7, td, one, sib),
+                keep(8, td, two, sib),
+            ]
+
+        self.copies = [copies(s) for s in range(cuts)]
+
+        def arrivals(s):
+            whole = pl.ds(s * rows, rows)
+            one, two = pl.ds(s * rows, half), pl.ds(s * rows + half, half)
+            where = [(c, tx, whole), (c, ty, whole), (1 - c, t, whole)]
+            where += [(1 - c, tx, whole), (c, td, one), (1 - c, ty, whole), (c, td, two)]
+            where += [(1 - c, td, one), (1 - c, td, two)]
+            return [
+                remote(out.at[4 * d + slot, part], out.at[4 * d + slot, part], sends.at[s, k], recvs.at[s, k], **sib)
+                for k, (d, slot, part) in enumerate(where)
+            ]
+
+        self.arrivals = [arrivals(s) for s in range(cuts)]
+
+    @staticmethod
+    def scratch(cuts):
+        return [
+            pltpu.SemaphoreType.DMA((cuts, Gather.KINDS)),
+            pltpu.SemaphoreType.DMA((cuts, Gather.KINDS)),
+            pltpu.SemaphoreType.DMA,
+        ]
+
+    def first(self):
+        for s in range(self.cuts):
+            for k in (0, 1, 2):
+                self.copies[s][k].start()
+        self.own.start()
+
+    def second(self):
+        for s in range(self.cuts):
+            self.arrivals[s][0].wait_recv()
+            self.copies[s][4].start()
+            self.copies[s][3].start()
+            self.arrivals[s][1].wait_recv()
+            self.copies[s][6].start()
+            self.copies[s][5].start()
+
+    def third(self):
+        for s in range(self.cuts):
+            for k in (4, 6):
+                self.arrivals[s][k].wait_recv()
+                self.copies[s][7 if k == 4 else 8].start()
+
+    def last(self):
+        for s in range(self.cuts):
+            for k in (2, 3, 5, 7, 8):
+                self.arrivals[s][k].wait_recv()
+        for s in range(self.cuts):
+            for k in range(self.KINDS):
+                self.copies[s][k].wait_send()
+        self.own.wait()
+
+
+class Sum:
+    def __init__(self, p, held, came, across_in, across_out, sends, recvs, loads):
+        z, c, t = spot()
+        self.t = t
+        tx, ty, td = across(t)
+        half = p.shape[1] // 2
+        self.half = half
+        self.one, self.two = pl.ds(0, half), pl.ds(half, half)
+        self.order = (td, tx, ty, t)
+        self.held, self.came, self.inn = held, came, across_in
+        sib, px, py = {"ctx": 1 - c}, {"tp": tx}, {"tp": ty}
+        self.loads = [pltpu.make_async_copy(p.at[4 * c + o], held.at[o], loads.at[k]) for k, o in enumerate(self.order)]
+        self.core = []
+        for k, o in enumerate(self.order):
+            self.core.append(remote(p.at[4 * (1 - c) + o], came.at[o], sends.at[k], recvs.at[k], **sib))
+
+        def send(k, source, slot, where):
+            return remote(source, across_in.at[slot], sends.at[k], recvs.at[k], **where)
+
+        self.side = {
+            "dx": send(4, held.at[td, self.one], 0, px),
+            "dy": send(5, held.at[td, self.two], 1, py),
+            "x": send(6, held.at[tx, self.one], 2, px),
+            "y": send(7, held.at[ty, self.two], 3, py),
+            "cy": send(8, across_out.at[0], 4, py),
+            "cx": send(9, across_out.at[1], 5, px),
+        }
+        self.out = across_out
+        self.near = (tx, ty, td)
+
+    @staticmethod
+    def scratch(rows, width):
+        return [
+            pltpu.VMEM((4, rows, width), bf16),
+            pltpu.VMEM((4, rows, width), bf16),
+            pltpu.VMEM((6, rows // 2, width), bf16),
+            pltpu.VMEM((2, rows // 2, width), bf16),
+            pltpu.SemaphoreType.DMA((10,)),
+            pltpu.SemaphoreType.DMA((10,)),
+            pltpu.SemaphoreType.DMA((4,)),
+        ]
+
+    def first(self):
+        for k in range(4):
+            self.core[k].start()
+            self.loads[k].start()
+
+    def second(self):
+        for k, o in enumerate(self.order):
+            self.loads[k].wait()
+            self.core[k].wait_recv()
+            self.held[o] = (self.held[o].astype(f32) + self.came[o].astype(f32)).astype(bf16)
+            if k == 0:
+                self.side["dx"].start()
+                self.side["dy"].start()
+            if k == 1:
+                self.side["x"].start()
+            if k == 2:
+                self.side["y"].start()
+
+    def third(self):
+        tx, ty, td = self.near
+        self.side["dx"].wait_recv()
+        self.out[0] = (self.held[ty, self.one].astype(f32) + self.inn[0].astype(f32)).astype(bf16)
+        self.side["cy"].start()
+        self.side["dy"].wait_recv()
+        self.out[1] = (self.held[tx, self.two].astype(f32) + self.inn[1].astype(f32)).astype(bf16)
+        self.side["cx"].start()
+
+    def last(self):
+        for k in ("x", "y", "cy", "cx"):
+            self.side[k].wait_recv()
+        for copy in self.core + list(self.side.values()):
+            copy.wait_send()
+
+    def total(self):
+        def add(part, a, b):
+            return self.held[self.t, part].astype(f32) + self.inn[a].astype(f32) + self.inn[b].astype(f32)
+
+        return add(self.one, 2, 4), add(self.two, 3, 5)
+
+
+def anywhere(count):
+    return [pl.BlockSpec(memory_space=pl.ANY)] * count
+
+
+def opening_kernel(cuts, x_ref, pack_ref, routes_ref, out_ref, packs_ref, all_routes_ref, *sems):
+    gather = Gather(x_ref, out_ref, *sems[:3], cuts)
+    sends, recvs, local = sems[3:]
+    z, c, t = spot()
+    ns = lax.axis_size("shard")
+    greet()
+    gather.first()
+    pairs = []
+    for step in range(1, ns):
+        there, back = lax.rem(z + step, ns), lax.rem(z + ns - step, ns)
+        copy = remote(pack_ref, packs_ref.at[z], sends.at[step], recvs.at[step], shard=there)
+        copy.start()
+        came = remote(pack_ref, packs_ref.at[back], sends.at[step], recvs.at[step], shard=there)
+        pairs.append((copy, came))
+    copy = remote(routes_ref, all_routes_ref.at[c], sends.at[0], recvs.at[0], ctx=1 - c)
+    copy.start()
+    pairs.append((copy, remote(routes_ref, all_routes_ref.at[1 - c], sends.at[0], recvs.at[0], ctx=1 - c)))
+    mine = [
+        pltpu.make_async_copy(pack_ref, packs_ref.at[z], local.at[0]),
+        pltpu.make_async_copy(routes_ref, all_routes_ref.at[c], local.at[1]),
+    ]
+    for copy in mine:
+        copy.start()
+    gather.second()
+    gather.third()
+    gather.last()
+    for copy, came in pairs:
+        came.wait_recv()
+        copy.wait_send()
+    for copy in mine:
+        copy.wait()
+
+
+def opening(x, pack, routes, number):
+    cuts = 2
+    ns = lax.axis_size("shard")
+    return pl.pallas_call(
+        functools.partial(opening_kernel, cuts),
+        in_specs=anywhere(3),
+        out_specs=anywhere(3),
+        out_shape=[
+            jax.ShapeDtypeStruct((8,) + x.shape, x.dtype),
+            jax.ShapeDtypeStruct((ns,) + pack.shape, pack.dtype),
+            jax.ShapeDtypeStruct((2,) + routes.shape, routes.dtype),
+        ],
+        scratch_shapes=Gather.scratch(cuts)
+        + [
+            pltpu.SemaphoreType.DMA((ns,)),
+            pltpu.SemaphoreType.DMA((ns,)),
+            pltpu.SemaphoreType.DMA((2,)),
+        ],
+        compiler_params=params(16, collective_id=number, has_side_effects=True),
+        cost_estimate=cost(30),
+        name="opening",
+    )(x, pack, routes)
+
+
+def gather_kernel(cuts, count, *refs):
+    xs, comb, outs, combs, sems = refs[:count], refs[count], refs[count + 1 : 2 * count + 1], refs[2 * count + 1], refs[2 * count + 2 :]
+    gathers = [Gather(x, out, *sems[3 * i : 3 * i + 3], cuts) for i, (x, out) in enumerate(zip(xs, outs))]
+    sends, recvs, local = sems[3 * count :]
+    z, c, t = spot()
+    own = 4 * c + t
+    greet(False)
+    for gather in gathers:
+        gather.first()
+    pairs = []
+    for step in range(1, 8):
+        other, back = lax.rem(own + step, 8), lax.rem(own + 8 - step, 8)
+        where = {"ctx": other // 4, "tp": lax.rem(other, 4)}
+        copy = remote(comb, combs.at[own], sends.at[step], recvs.at[step], **where)
+        copy.start()
+        pairs.append((copy, remote(comb, combs.at[back], sends.at[step], recvs.at[step], **where)))
+    mine = pltpu.make_async_copy(comb, combs.at[own], local)
+    mine.start()
+    for gather in gathers:
+        gather.second()
+    for gather in gathers:
+        gather.third()
+    for gather in gathers:
+        gather.last()
+    for copy, came in pairs:
+        came.wait_recv()
+        copy.wait_send()
+    mine.wait()
+
+
+def gather_rows(xs, comb, number):
+    cuts = 2
+    return pl.pallas_call(
+        functools.partial(gather_kernel, cuts, len(xs)),
+        in_specs=anywhere(len(xs) + 1),
+        out_specs=anywhere(len(xs) + 1),
+        out_shape=[jax.ShapeDtypeStruct((8,) + x.shape, x.dtype) for x in (*xs, comb)],
+        scratch_shapes=Gather.scratch(cuts) * len(xs)
+        + [
+            pltpu.SemaphoreType.DMA((8,)),
+            pltpu.SemaphoreType.DMA((8,)),
+            pltpu.SemaphoreType.DMA,
+        ],
+        compiler_params=params(16, collective_id=number, has_side_effects=True),
+        cost_estimate=cost(30 * len(xs)),
+        name="gather_rows",
+    )(*xs, comb)
+
+
+def sum_kernel(p_ref, out_ref, *scratch):
+    job = Sum(p_ref, *scratch)
+    greet(False)
+    job.first()
+    job.second()
+    job.third()
+    job.last()
+    one, two = job.total()
+    out_ref[: job.half] = one.astype(out_ref.dtype)
+    out_ref[job.half :] = two.astype(out_ref.dtype)
+
+
+def sum_rows(p, number):
+    _, rows, width = p.shape
+    return pl.pallas_call(
+        sum_kernel,
+        in_specs=anywhere(1),
+        out_specs=pl.BlockSpec(memory_space=pltpu.VMEM),
+        out_shape=jax.ShapeDtypeStruct((rows, width), f32),
+        scratch_shapes=Sum.scratch(rows, width),
+        compiler_params=params(40, collective_id=number, has_side_effects=True),
+        cost_estimate=cost(35),
+        name="sum_rows",
+    )(p)
+
+
+def to_owner_kernel(o_ref, w_ref, att_ref, all_w_ref, send_sem, recv_sem, w_send, w_recv, local_sem):
+    z, c, t = spot()
+    nt = lax.axis_size("tp")
     own = c * nt + t
     count = o_ref.shape[0]
-    greet(c, t, nc, nt)
+    greet(False)
     copies = []
     for i in range(count):
         block = zig(c, i)
-        copy = pltpu.make_async_remote_copy(
-            src_ref=o_ref.at[i],
-            dst_ref=att_ref.at[t],
-            send_sem=send_sem.at[i],
-            recv_sem=recv_sem.at[t],
-            device_id={"ctx": block // nt, "tp": lax.rem(block, nt)},
-            device_id_type=MESH,
-        )
-        local = pltpu.make_async_copy(o_ref.at[i], att_ref.at[t], local_sem)
+        copy = remote(o_ref.at[i], att_ref.at[t], send_sem.at[i], recv_sem.at[t], ctx=block // nt, tp=lax.rem(block, nt))
+        local = pltpu.make_async_copy(o_ref.at[i], att_ref.at[t], local_sem.at[0])
         copies.append((block, copy, local))
     for block, copy, local in copies:
 
@@ -333,6 +691,14 @@
         def _():
             local.start()
 
+    pairs = []
+    for step in range(1, nt):
+        there, back = lax.rem(t + step, nt), lax.rem(t + nt - step, nt)
+        copy = remote(w_ref, all_w_ref.at[t], w_send.at[step], w_recv.at[step], tp=there)
+        copy.start()
+        pairs.append((copy, remote(w_ref, all_w_ref.at[back], w_send.at[step], w_recv.at[step], tp=there)))
+    mine_w = pltpu.make_async_copy(w_ref, all_w_ref.at[t], local_sem.at[1])
+    mine_w.start()
     for block, copy, local in copies:
 
         @pl.when(block != own)
@@ -348,88 +714,227 @@
 
         @pl.when(jnp.logical_or(jnp.logical_not(mine), source != t))
         def _():
-            pltpu.make_async_remote_copy(
-                src_ref=o_ref.at[0],
-                dst_ref=att_ref.at[source],
-                send_sem=send_sem.at[0],
-                recv_sem=recv_sem.at[source],
-                device_id={"ctx": c, "tp": t},
-                device_id_type=MESH,
-            ).wait_recv()
-
-
-def to_heads_kernel(nc, nt, o_ref, got_ref, send_sem, recv_sem, local_sem):
-    c, t = lax.axis_index("ctx"), lax.axis_index("tp")
+            remote(o_ref.at[0], att_ref.at[source], send_sem.at[0], recv_sem.at[source], ctx=c, tp=t).wait_recv()
+
+    for copy, came in pairs:
+        came.wait_recv()
+        copy.wait_send()
+    mine_w.wait()
+
+
+def to_owner(o, w, number):
+    nt = lax.axis_size("tp")
+    return pl.pallas_call(
+        to_owner_kernel,
+        in_specs=anywhere(2),
+        out_specs=anywhere(2),
+        out_shape=[
+            jax.ShapeDtypeStruct((nt,) + o.shape[1:], o.dtype),
+            jax.ShapeDtypeStruct((nt,) + w.shape, w.dtype),
+        ],
+        scratch_shapes=[
+            pltpu.SemaphoreType.DMA((o.shape[0],)),
+            pltpu.SemaphoreType.DMA((nt,)),
+            pltpu.SemaphoreType.DMA((nt,)),
+            pltpu.SemaphoreType.DMA((nt,)),
+            pltpu.SemaphoreType.DMA((2,)),
+        ],
+        compiler_params=params(16, collective_id=number, has_side_effects=True),
+        cost_estimate=cost(10),
+        name="to_owner",
+    )(o, w)
+
+
+def to_heads_kernel(o_ref, w_ref, got_ref, sum_ref, came_ref, own_ref, send_sem, recv_sem, w_send, w_recv, local_sem):
+    z, c, t = spot()
+    nt = lax.axis_size("tp")
     own = c * nt + t
     count = got_ref.shape[0]
-    greet(c, t, nc, nt)
+    greet(False)
     core = lax.rem((own + 1) // 2, 2)
     slot = 2 * (own // 4) + lax.rem(own, 4) // 2
+    copies = []
     for target in range(nt):
         here = jnp.logical_and(core == c, target == t)
+        copy = remote(o_ref.at[target], got_ref.at[slot], send_sem.at[target], recv_sem.at[slot], ctx=core, tp=target)
+        local = pltpu.make_async_copy(o_ref.at[target], got_ref.at[slot], local_sem.at[0])
+        copies.append((here, copy, local))
+    for here, copy, local in copies:
 
         @pl.when(jnp.logical_not(here))
         def _():
-            pltpu.make_async_remote_copy(
-                src_ref=o_ref.at[target],
-                dst_ref=got_ref.at[slot],
-                send_sem=send_sem.at[target],
-                recv_sem=recv_sem.at[slot],
-                device_id={"ctx": core, "tp": target},
-                device_id_type=MESH,
-            ).start()
+            copy.start()
 
         @pl.when(here)
         def _():
-            pltpu.make_async_copy(o_ref.at[target], got_ref.at[slot], local_sem).start()
-
-    for target in range(nt):
-        here = jnp.logical_and(core == c, target == t)
+            local.start()
+
+    pairs = []
+    for step in range(1, nt):
+        there = lax.rem(t + step, nt)
+        copy = remote(w_ref.at[there], came_ref.at[step], w_send.at[step], w_recv.at[step], tp=there)
+        copy.start()
+        pairs.append(copy)
+    mine = pltpu.make_async_copy(w_ref.at[t], own_ref, local_sem.at[1])
+    mine.start()
+    for here, copy, local in copies:
 
         @pl.when(jnp.logical_not(here))
         def _():
-            pltpu.make_async_remote_copy(
-                src_ref=o_ref.at[target],
-                dst_ref=got_ref.at[slot],
-                send_sem=send_sem.at[target],
-                recv_sem=recv_sem.at[slot],
-                device_id={"ctx": core, "tp": target},
-                device_id_type=MESH,
-            ).wait_send()
+            copy.wait_send()
 
         @pl.when(here)
         def _():
-            pltpu.make_async_copy(o_ref.at[target], got_ref.at[slot], local_sem).wait()
+            local.wait()
 
     for i in range(count):
 
         @pl.when(zig(c, i) != own)
         def _():
-            pltpu.make_async_remote_copy(
-                src_ref=o_ref.at[0],
-                dst_ref=got_ref.at[i],
-                send_sem=send_sem.at[0],
-                recv_sem=recv_sem.at[i],
-                device_id={"ctx": c, "tp": t},
-                device_id_type=MESH,
-            ).wait_recv()
-
-
-def exchange(kernel, value, count, number, name):
-    nc, nt = lax.axis_size("ctx"), lax.axis_size("tp")
-    return pl.pallas_call(
-        functools.partial(kernel, nc, nt),
-        in_specs=[pl.BlockSpec(memory_space=pltpu.VMEM)],
-        out_specs=pl.BlockSpec(memory_space=pltpu.VMEM),
-        out_shape=jax.ShapeDtypeStruct((count,) + value.shape[1:], value.dtype),
+            remote(o_ref.at[0], got_ref.at[i], send_sem.at[0], recv_sem.at[i], ctx=c, tp=t).wait_recv()
+
+    mine.wait()
+    total = own_ref[...].astype(f32)
+    for step, copy in enumerate(pairs):
+        copy.wait_recv()
+        total = total + came_ref[step + 1].astype(f32)
+        copy.wait_send()
+    sum_ref[...] = total.astype(bf16)
+
+
+def to_heads(o, w, count, number):
+    nt = lax.axis_size("tp")
+    return pl.pallas_call(
+        to_heads_kernel,
+        in_specs=anywhere(2),
+        out_specs=anywhere(1) + [pl.BlockSpec(memory_space=pltpu.VMEM)],
+        out_shape=[
+            jax.ShapeDtypeStruct((count,) + o.shape[1:], o.dtype),
+            jax.ShapeDtypeStruct(w.shape[1:], w.dtype),
+        ],
         scratch_shapes=[
-            pltpu.SemaphoreType.DMA((value.shape[0],)),
+            pltpu.VMEM(w.shape, w.dtype),
+            pltpu.VMEM(w.shape[1:], w.dtype),
+            pltpu.SemaphoreType.DMA((nt,)),
             pltpu.SemaphoreType.DMA((count,)),
-            pltpu.SemaphoreType.DMA,
-        ],
-        compiler_params=params(collective_id=number, has_side_effects=True),
-        name=name,
-    )(value)
+            pltpu.SemaphoreType.DMA((nt,)),
+            pltpu.SemaphoreType.DMA((nt,)),
+            pltpu.SemaphoreType.DMA((2,)),
+        ],
+        compiler_params=params(16, collective_id=number, has_side_effects=True),
+        cost_estimate=cost(12),
+        name="to_heads",
+    )(o, w)
+
+
+def closing_kernel(p_ref, gw_ref, small_ref, top_ref, ge_ref, out_ref, gsum_ref, ssum_ref, tmax_ref, gall_ref,
+                   gcore, gline, gmine, sline, splane, tline, *sems):
+    job = Sum(p_ref, *sems[:7])
+    sends, recvs, local = sems[7:]
+    z, c, t = spot()
+    ns = lax.axis_size("shard")
+    rows = gw_ref.shape[2]
+    own = 4 * c + t
+    greet()
+    started = []
+
+    def go(k, source, target, **where):
+        copy = remote(source, target, sends.at[k], recvs.at[k], **where)
+        copy.start()
+        started.append(copy)
+        return copy
+
+    core = go(0, gw_ref.at[1 - c], gcore, ctx=1 - c)
+    small = [go(3 + s, small_ref.at[lax.rem(z + s, ns)], sline.at[s], shard=lax.rem(z + s, ns)) for s in range(1, ns)]
+    tops = [go(3 + ns + s, top_ref, tline.at[s], shard=lax.rem(z + s, ns)) for s in range(1, ns)]
+    own_g = pltpu.make_async_copy(gw_ref.at[c], gmine, local.at[0])
+    own_g.start()
+    job.first()
+    experts = go(1, ge_ref, gall_ref.at[c], ctx=1 - c)
+    own_e = pltpu.make_async_copy(ge_ref, gall_ref.at[c], local.at[1])
+    own_e.start()
+    job.second()
+    own_g.wait()
+    core.wait_recv()
+    gmine[...] = (gmine[...].astype(f32) + gcore[...].astype(f32)).astype(bf16)
+    line = [go(3 + 2 * ns + s, gmine.at[lax.rem(z + s, ns)], gline.at[s], shard=lax.rem(z + s, ns)) for s in range(1, ns)]
+    for copy in small:
+        copy.wait_recv()
+    total = small_ref[z]
+    for s in range(1, ns):
+        total = total + sline[s]
+    splane[0] = total
+    plane = []
+    for s in range(1, 8):
+        other = lax.rem(own + s, 8)
+        plane.append(go(3 + 3 * ns + s, splane.at[0], splane.at[s], ctx=other // 4, tp=lax.rem(other, 4)))
+    for copy in tops:
+        copy.wait_recv()
+    high = top_ref[...]
+    for s in range(1, ns):
+        high = jnp.maximum(high, tline[s])
+    tline[0] = high
+    pair = go(2, tline.at[0], tline.at[ns], ctx=1 - c)
+    job.third()
+    for copy in line:
+        copy.wait_recv()
+    total = gmine[z].astype(f32)
+    for s in range(1, ns):
+        total = total + gline[s].astype(f32)
+    gsum_ref[c] = total
+    final = go(3, gsum_ref.at[c], gsum_ref.at[c], ctx=1 - c)
+    for copy in plane:
+        copy.wait_recv()
+    total = splane[0]
+    for s in range(1, 8):
+        total = total + splane[s]
+    ssum_ref[...] = total
+    pair.wait_recv()
+    tmax_ref[...] = jnp.maximum(tline[0], tline[ns])
+    job.last()
+    one, two = job.total()
+    out_ref[: job.half] = one
+    out_ref[job.half :] = two
+    remote(gsum_ref.at[1 - c], gsum_ref.at[1 - c], sends.at[3], recvs.at[3], ctx=1 - c).wait_recv()
+    remote(ge_ref, gall_ref.at[1 - c], sends.at[1], recvs.at[1], ctx=1 - c).wait_recv()
+    own_e.wait()
+    for copy in started:
+        copy.wait_send()
+
+
+def closing(p, gw, small, top, ge, number):
+    _, rows, width = p.shape
+    ns = lax.axis_size("shard")
+    vmem = pl.BlockSpec(memory_space=pltpu.VMEM)
+    return pl.pallas_call(
+        closing_kernel,
+        in_specs=anywhere(2) + [vmem, vmem] + anywhere(1),
+        out_specs=[vmem, vmem, vmem, vmem] + anywhere(1),
+        out_shape=[
+            jax.ShapeDtypeStruct((rows, width), f32),
+            jax.ShapeDtypeStruct((2,) + gw.shape[2:], f32),
+            jax.ShapeDtypeStruct(small.shape[1:], f32),
+            jax.ShapeDtypeStruct(top.shape, f32),
+            jax.ShapeDtypeStruct((2,) + ge.shape, ge.dtype),
+        ],
+        scratch_shapes=[
+            pltpu.VMEM(gw.shape[1:], bf16),
+            pltpu.VMEM(gw.shape[1:], bf16),
+            pltpu.VMEM(gw.shape[1:], bf16),
+            pltpu.VMEM(small.shape, f32),
+            pltpu.VMEM((8,) + small.shape[1:], f32),
+            pltpu.VMEM((ns + 1,) + top.shape, f32),
+        ]
+        + Sum.scratch(rows, width)
+        + [
+            pltpu.SemaphoreType.DMA((3 * ns + 11,)),
+            pltpu.SemaphoreType.DMA((3 * ns + 11,)),
+            pltpu.SemaphoreType.DMA((2,)),
+        ],
+        compiler_params=params(48, collective_id=number, has_side_effects=True),
+        cost_estimate=cost(40),
+        name="closing",
+    )(p, gw, small, top, ge)
 
 
 def mixing(n2, wrc, previous, routes):
@@ -502,6 +1007,7 @@
             jax.ShapeDtypeStruct((16, rows), f32),
         ],
         compiler_params=params(),
+        cost_estimate=cost(8),
         name="forward_rows",
     )(place, x, att, wo, gain, wrc, vec, prev, routes)
 
@@ -592,18 +1098,18 @@
             jax.ShapeDtypeStruct((24, width), f32),
         ],
         compiler_params=params(),
+        cost_estimate=cost(15),
         name="backward_rows",
     )(place, res, dn, cot, valid, att, wo, gain, wrc, vec, prev, routes)
 
 
-def finish_kernel(x_ref, dn_ref, dres_ref, gain_ref, base_ref, feed_ref, valid_ref, gin_ref, out_ref, small_ref):
+def finish_kernel(x_ref, dn_ref, dres_ref, gain_ref, base_ref, feed_ref, valid_ref, gin_ref, out_ref):
     x = x_ref[...].astype(f32)
     inverse = lax.rsqrt(jnp.mean(x * x, axis=1, keepdims=True) + epsilon)
     m = x * inverse
     dn = dn_ref[...].astype(f32)
     q = dn * gain_ref[...]
     gin_ref[...] = dres_ref[...] + inverse * (q - m * jnp.mean(q * m, axis=1, keepdims=True))
-    small_ref[...] = jnp.sum(dn * m, axis=0, keepdims=True)
     out_ref[...] = (valid_ref[...] * (base_ref[...] + feed_ref[...].astype(f32))).astype(bf16)
 
 
@@ -614,9 +1120,9 @@
         out_shape=[
             jax.ShapeDtypeStruct((rows, width), f32),
             jax.ShapeDtypeStruct((rows, width), bf16),
-            jax.ShapeDtypeStruct((1, width), f32),
         ],
         compiler_params=params(),
+        cost_estimate=cost(5),
         name="finish_rows",
     )(x, dn, dres, gain, base, feed, valid)
 
@@ -654,6 +1160,7 @@
             jax.ShapeDtypeStruct((total, 16), f32),
         ],
         compiler_params=params(),
+        cost_estimate=cost(5),
         name="place_rows",
     )(routes.T, routes)
 
@@ -693,15 +1200,16 @@
         ),
         out_shape=outs,
         compiler_params=params(),
+        cost_estimate=cost(18),
         name="fetch_rows",
     )(first, *args)
 
 
 def expert_kernel(j, first, x_ref, g_ref, gate_ref, w_ref, feed_ref, back_ref, gw_ref, total):
     i = pl.program_id(0)
-    parts, _, depth, hidden = w_ref.shape
+    parts, _, _, depth, hidden = w_ref.shape
     width = parts * depth
-    wg, wu, wd = [w_ref[:, k].reshape(width, hidden) for k in range(3)]
+    wg, wu, wd = [w_ref[:, 0, k].reshape(width, hidden) for k in range(3)]
     x, g, gate = x_ref[0], g_ref[0], gate_ref[0]
     gate_pre = mm(x, wg)
     up = mm(x, wu)
@@ -739,7 +1247,8 @@
 
 def expert(j, first, x, g, gate, w):
     slots, width = x.shape[1:]
-    parts, _, depth, hidden = w.shape
+    parts, _, kinds, depth, hidden = w.shape
+    grads = (parts, kinds, depth, hidden)
     pick = lambda i, f: (j, i, 0)
     return pl.pallas_call(
         functools.partial(expert_kernel, j),
@@ -750,21 +1259,22 @@
                 pl.BlockSpec((1, CAP, width), pick),
                 pl.BlockSpec((1, CAP, width), pick),
                 pl.BlockSpec((1, CAP, 1), pick),
-                full(w.shape),
+                pl.BlockSpec((parts, 1, kinds, depth, hidden), lambda i, f: (0, j, 0, 0, 0)),
             ],
             out_specs=[
                 pl.BlockSpec((CAP, width), lambda i, f: (i, 0)),
                 pl.BlockSpec((CAP, width + EXTRA), lambda i, f: (i, 0)),
-                full(w.shape),
+                full(grads),
             ],
             scratch_shapes=[pltpu.VMEM((3, width, hidden), f32)],
         ),
         out_shape=[
             jax.ShapeDtypeStruct((slots, width), bf16),
             jax.ShapeDtypeStruct((slots, width + EXTRA), bf16),
-            jax.ShapeDtypeStruct(w.shape, bf16),
+            jax.ShapeDtypeStruct(grads, bf16),
         ],
         compiler_params=params(),
+        cost_estimate=cost(14),
         name="expert",
     )(first, x, g, gate, w)
 
@@ -796,6 +1306,7 @@
         ),
         out_shape=jax.ShapeDtypeStruct((total, width), bf16),
         compiler_params=params(),
+        cost_estimate=cost(20),
         name="spread_rows",
     )(first, col, *values)
 
@@ -852,21 +1363,17 @@
         ],
         axis=1,
     )
-    rows_all = lax.all_gather(hidden_in, plane, axis=0, tiled=True)
-    packed = lax.all_gather(pack, "shard", axis=0, tiled=True)
-    expert_w = []
-    for j in range(local):
-        pieces = [
-            lax.dynamic_index_in_dim(w, core * local + j, 0, keepdims=False)
-            for w in (w_gate, w_up, w_down)
-        ]
-        gathered = lax.all_gather(jnp.stack(pieces), "shard", axis=0, tiled=False)
-        expert_w.append(gathered)
+    pieces = [
+        lax.dynamic_slice_in_dim(w, core * local, local, 0) for w in (w_gate, w_up, w_down)
+    ]
+    expert_w = lax.all_gather(jnp.stack(pieces, axis=1), "shard", axis=0, tiled=False)
+    rows_all, packed, routes_all = opening(hidden_in, pack, routes, 0)
+    rows_all = rows_all.reshape(total, width)
+    packed = packed.reshape(width, pack.shape[1])
+    routes_all = routes_all.reshape(total, 2)
 
     wt = packed[:, : 3 * head_width].T
     out_t = packed[:, 3 * head_width : 4 * head_width]
-    wo = lax.all_gather(out_t, "tp", axis=0, tiled=False)
-    wo = wo.transpose(0, 2, 1).reshape(nt * head_width, width)
     smalls = packed[:, 4 * head_width :].astype(f32)
     gain_attn = smalls[:, 0][None]
     gain_moe = smalls[:, 1][None]
@@ -878,69 +1385,58 @@
     angles = freqs[:, None] * jnp.arange(total).astype(f32)[None, :]
     cosine, sine = jnp.cos(angles), jnp.sin(angles)
 
-    a1, qt, kt, k, v, vt = project(rows_all, gain_attn, wt, cosine, sine, heads)
+    qt, kt, k, v, vt = project(rows_all, gain_attn, wt, cosine, sine, heads)
     table = jnp.stack([zig(core, i) for i in range(count)]).astype(jnp.int32)
     blocks = jnp.arange(total // BLOCK, dtype=jnp.int32)
     owned = jnp.any(blocks[:, None] == table[None, :], axis=1).astype(jnp.int32)
     ot, lse, top = attend(table, lengths, qt, k, vt)
-    att = exchange(to_owner_kernel, ot, nt, 0, "to_owner")
-    head_max = lax.pmax(jnp.max(top, axis=(1, 2, 3)), ("shard", "ctx"))
-    factors = threshold[0] / jnp.maximum(head_max, threshold[0])
-    root = jnp.repeat(jnp.sqrt(factors), HEAD_DIM)
-    clipped_query = (w_query.astype(f32) * root[None, :]).astype(bf16)
-    clipped_key = (w_key.astype(f32) * root[None, :]).astype(bf16)
+    top = jnp.pad(jnp.max(top, axis=(1, 2, 3))[:, None], ((0, 8 - heads), (0, 127)))
+    att, wo = to_owner(ot, out_t.T, 1)
+    wo = wo.reshape(nt * head_width, width)
 
     res, base, a2, comb = forward_rows(place, hidden_in, att, wo, gain_moe, wrc, vec, prev, routes)
 
-    routes_all = lax.all_gather(routes, "ctx", axis=0, tiled=True)
     row_at, col_at = place_rows(routes_all, per)
     cot = (cotangent.astype(f32) * valid).astype(bf16)
-    cot_all = lax.all_gather(cot, plane, axis=0, tiled=True)
+    a2_all, cot_all, comb_all = gather_rows((a2, cot), comb, 2)
+    a2_all, cot_all = a2_all.reshape(total, width), cot_all.reshape(total, width)
     (g_slots,) = fetch_rows(first, row_at, None, cot_all, per, local, False)
-    a2_all = lax.all_gather(a2, plane, axis=0, tiled=True)
-    comb_all = lax.all_gather(comb, plane, axis=0, tiled=False)
     comb_all = comb_all.transpose(1, 0, 2).reshape(16, total)
     x_slots, gate_slots = fetch_rows(first, row_at, comb_all, a2_all, per, local, True)
     feeds, backs, grads = [], [], []
     for j in range(local):
-        feed, back, grad = expert(j, first, x_slots, g_slots, gate_slots, expert_w[j])
+        feed, back, grad = expert(j, first, x_slots, g_slots, gate_slots, expert_w)
         feeds.append(feed)
         backs.append(back)
         grads.append(grad)
-    back = spread_rows(first, col_at, backs, per)
-    back = lax.psum_scatter(back, plane, scatter_dimension=0, tiled=True)
-    feed = spread_rows(first, col_at, feeds, per)
-    feed = lax.psum_scatter(feed, plane, scatter_dimension=0, tiled=True)
+    back = spread_rows(first, col_at, backs, per).reshape(8, own, width + EXTRA)
+    back = sum_rows(back, 3)
+    feed = spread_rows(first, col_at, feeds, per).reshape(8, own, width)
+    feed = sum_rows(feed, 4)
     grads = [lax.psum_scatter(g, "shard", scatter_dimension=0, tiled=True)[0] for g in grads]
 
     dres, got, grad_out, small = backward_rows(
         place, res, back, cotangent, valid, att, wo, gain_moe, wrc, vec, prev, routes
     )
-    got = exchange(to_heads_kernel, got, count, 1, "to_heads")
+    got, grad_out = to_heads(got, grad_out.reshape(nt, head_width, width), count, 5)
     dq, dk, dv = revisit(table, qt, k, kt, v, ot, got, lse)
-    part, grad_qkv = unproject(owned, dq, dk, dv, cosine, sine, a1, wt)
-    part = lax.psum_scatter(part, plane, scatter_dimension=0, tiled=True)
-    grad_input, output, gain_row = finish_rows(
-        hidden_in, part, dres, gain_attn, base, feed, valid
+    part, grad_w, small = unproject(
+        owned, dq, dk, dv, cosine, sine, rows_all, gain_attn, wt, grad_out, small, ns
     )
-
-    grad_expert = lax.all_gather(jnp.stack(grads), "ctx", axis=0, tiled=True).astype(f32)
+    part, grad_w, small, top, grad_expert = closing(
+        part.reshape(8, own, width), grad_w, small, top, jnp.stack(grads), 6
+    )
+    grad_input, output = finish_rows(hidden_in, part, dres, gain_attn, base, feed, valid)
+
+    factors = threshold[0] / jnp.maximum(top[:heads, 0], threshold[0])
+    root = jnp.repeat(jnp.sqrt(factors), HEAD_DIM)
+    clipped_query = (w_query.astype(f32) * root[None, :]).astype(bf16)
+    clipped_key = (w_key.astype(f32) * root[None, :]).astype(bf16)
+    grad_expert = grad_expert.reshape((FFN_EXPERTS,) + grad_expert.shape[2:]).astype(f32)
     grad_gate, grad_up, grad_down = [grad_expert[:, k] for k in range(3)]
-    grad_qkv = lax.psum_scatter(
-        lax.psum(grad_qkv, "ctx").reshape(3 * head_width, ns, depth).transpose(1, 0, 2),
-        "shard",
-        scatter_dimension=0,
-        tiled=False,
-    )
-    grad_q, grad_k, grad_v = [
-        grad_qkv[i * head_width : (i + 1) * head_width].T.astype(f32) for i in range(3)
-    ]
-    grad_out = lax.psum_scatter(grad_out, "tp", scatter_dimension=0, tiled=True)
-    grad_out = lax.psum(grad_out, "ctx").reshape(head_width, ns, depth).transpose(1, 0, 2)
-    grad_out = lax.psum_scatter(grad_out, "shard", scatter_dimension=0, tiled=False).astype(f32)
-    small = jnp.concatenate([small[:19], gain_row], axis=0)
-    small = lax.psum(small, ("shard", "ctx", "tp"))
-    small = lax.dynamic_slice_in_dim(small, lax.axis_index("shard") * depth, depth, 1)
+    grad_w = grad_w.reshape(4 * head_width, depth)
+    grad_q, grad_k, grad_v = [grad_w[i * head_width : (i + 1) * head_width].T for i in range(3)]
+    grad_out = grad_w[3 * head_width :]
     return (
         output,
         grad_input,

time: 1090 us -> 713 us (0.65)
  waiting for transfers between devices: 612 us -> 0.13 us
  Pallas kernels: 314 us -> 610 us
  blocking collectives: 83.6 us -> 0 us
  local copies, waits for them, and re-layouts: 32.8 us -> 61.7 us
    pallas_call x2 -> x7, Pallas kernels: 30.8 us -> 329 us  [the longest x1 101 us: closing(): pl.pallas_call(closing_kernel, in_specs=anywhere(2) + [vmem, vmem] + anyw...]
    reduce_scatter x6 -> x0, waiting for transfers between devices: 234 us -> none  [the longest x1 65.2 us: shards(): part = lax.psum_scatter(part, plane, scatter_dimension=0, tiled=True)]
    all_gather x10 -> x1, waiting for transfers between devices: 232 us -> 0.01 us  [shards(): lax.all_gather(jnp.stack(pieces, axis=1), 'shard', axis=0, tiled=False)]
    reduce_scatter x4, waiting for transfers between devices: 142 us -> 0.04 us  [shards(): lax.psum_scatter(g, 'shard', scatter_dimension=0, tiled=True)[0]]
    psum x1 -> x0, blocking collectives: 40 us -> none  [shards(): small = lax.psum(small, ('shard', 'ctx', 'tp'))]
    unnamed x33 -> x96, local copies, waits for them, and re-layouts: 7.49 us -> 40 us
    all_gather x2 -> x0, blocking collectives: 30 us -> none  [the longest x1 24.2 us: shards(): comb_all = lax.all_gather(comb, plane, axis=0, tiled=False)]
    pmax x1 -> x0, blocking collectives: 13.6 us -> none  [shards(): head_max = lax.pmax(jnp.max(top, axis=(1, 2, 3)), ('shard', 'ctx'))]
  transfers between devices with their start and end apart: 21 -> 5, of which waited for: 15 -> 0; matrix products, arithmetic and copies ran while one was open for 4% -> 3% of each run, Pallas kernels for 24% -> 69%
where the time goes in v2:
time: 713 us; the launch traced here: 706 us
  Pallas kernels  610 us (86%)
  local copies, waits for them, and re-layouts  61.7 us (9%)
  other arithmetic  18.3 us (3%)
  between operations  15.8 us (2%)
    pallas_call x1, Pallas kernels, closing(): pl.pallas_call(closing_kernel, in_specs=anywhere(2) + [vmem, vmem] + anyw...  101 us
    pallas_call x2, Pallas kernels, sum_rows(): pl.pallas_call(sum_kernel, in_specs=anywhere(1), out_specs=pl.BlockSpec(m...  68.5 us
    pallas_call x1, Pallas kernels, gather_rows(): pl.pallas_call(functools.partial(gather_kernel, cuts, len(xs)), in_specs=...  59.1 us
    pallas_call x4, Pallas kernels, expert(): pl.pallas_call(functools.partial(expert_kernel, j), grid_spec=pltpu.Prefe...  55.9 us
    pallas_call x1, Pallas kernels, opening(): pl.pallas_call(functools.partial(opening_kernel, cuts), in_specs=anywhere...  50.2 us
    pallas_call x1, Pallas kernels, revisit(): pl.pallas_call(revisit_kernel, grid_spec=pltpu.PrefetchScalarGridSpec(num...  50.1 us
    pallas_call x2, Pallas kernels, spread_rows(): pl.pallas_call(functools.partial(spread_kernel, len(values)), grid_spec=p...  40.8 us
    unnamed x96, local copies, waits for them, and re-layouts  40 us
  transfers between devices with their start and end apart: 5, of which 0 were waited for; matrix products, arithmetic and copies ran while one was open for 3% of the time, Pallas kernels for 69%

profile of v2, /device:TPU:0, one launch (start us, length us, event | category | flops | bytes accessed | tf_op | source)
XLA Modules:
  0.0 706.2 jit_solution(11760932748640248011)
XLA Ops:
  19.0 50.2 %opening.1 = (bf16[8,512,768]{2,1,0:T(8,128)(2,1)S(1)}, bf16[4,192,800]{2,1,0:T(8,128)(2,1)S(1)}, s32[2,2048,2]{2,1,0:T(8,128)S(1)}) custom-call(bf16[512,768]{1,0:T(8,128)(2,1)S(1)} %copy-done.5, bf16[192,800]{1,0:T(8,128)(2,1)S(1)} %copy-done.4, s32[2048,2]{1,0:T(8,128)S(1)} %copy-done.3), custom_call_target="tpu_custom_call" | custom-call | flops 30000001024 | bytes 90000000 | tf_op jit(solution)/shard_map/opening/pallas_call | solution.py:576
  69.2 2.6 copy-done.7
  83.3 2.8 multiply_sine_fusion
  87.9 12.6 %project.1 = (bf16[3,64,4096]{2,1,0:T(8,128)(2,1)}, bf16[3,64,4096]{2,1,0:T(8,128)(2,1)}, bf16[3,4096,64]{2,1,0:T(8,128)(2,1)}, bf16[3,4096,64]{2,1,0:T(8,128)(2,1)}, bf16[3,80,4096]{2,1,0:T(8,128)(2,1)}) custom-call(bf16[4096,768]{1,0:T(8,128)(2,1)} %bitcast.81, f32[1,768]{1,0:T(1,128)} %get-tuple-element.203.gain_ref, bf16[576,768]{1,0:T(8,128)(2,1)} %bitcast.89, ...), custom_call_target="tpu_custom_call" | custom-call | flops 12999999488 | bytes 39000000 | tf_op jit(solution)/shard_map/project/pallas_call | solution.py:81
  100.5 34.8 %attend.1 = (bf16[4,192,512]{2,1,0:T(8,128)(2,1)}, f32[3,4,1,512]{3,2,1,0:T(1,128)}, f32[3,4,1,512]{3,2,1,0:T(1,128)}) custom-call(s32[4]{0:T(128)} %pad_add_fusion.table, s32[1]{0:T(128)} %copy.134.length, bf16[3,64,4096]{2,1,0:T(8,128)(2,1)} %get-tuple-element.74.qt_ref, bf16[3,4096,64]{2,1,0:T(8,128)(2,1)} %get-tuple-element.75.k_ref, ...), custom_call_target="tpu_custom_call" | custom-call | flops 35000000512 | bytes 105000000 | tf_op jit(solution)/shard_map/attend/pallas_call | solution.py:142
  136.4 25.1 %to_owner.1 = (bf16[4,192,512]{2,1,0:T(8,128)(2,1)S(1)}, bf16[4,192,768]{2,1,0:T(8,128)(2,1)S(1)}) custom-call(bf16[4,192,512]{2,1,0:T(8,128)(2,1)S(1)} %copy-done.19, bf16[192,768]{1,0:T(8,128)(2,1)S(1)} %bitcast.78), custom_call_target="tpu_custom_call" | custom-call | flops 10000000000 | bytes 30000000 | tf_op jit(solution)/shard_map/to_owner/pallas_call | solution.py:727
  163.5 7.6 %forward_rows.1 = (f32[512,768]{1,0:T(8,128)}, f32[512,768]{1,0:T(8,128)}, bf16[512,768]{1,0:T(8,128)(2,1)}, f32[16,512]{1,0:T(8,128)}) custom-call(s32[1]{0:T(128)} %bitcast.10.place, bf16[512,768]{1,0:T(8,128)(2,1)} %x_ref.5, bf16[4,192,512]{2,1,0:T(8,128)(2,1)} %copy-done.15, bf16[768,768]{1,0:T(8,128)(2,1)} %bitcast.86, ...), custom_call_target="tpu_custom_call" | custom-call | flops 8000000000 | bytes 24000000 | tf_op jit(solution)/shard_map/forward_rows/pallas_call | solution.py:986
  173.0 59.1 %gather_rows.1 = (bf16[8,512,768]{2,1,0:T(8,128)(2,1)S(1)}, bf16[8,512,768]{2,1,0:T(8,128)(2,1)S(1)}, f32[8,16,512]{2,1,0:T(8,128)S(1)}) custom-call(bf16[512,768]{1,0:T(8,128)(2,1)S(1)} %copy-done.16, bf16[512,768]{1,0:T(8,128)(2,1)S(1)} %multiply_convert_fusion.refs_1_, f32[16,512]{1,0:T(8,128)S(1)} %copy-done.23), custom_call_target="tpu_custom_call" | custom-call | flops 60000002048 | bytes 180000000 | tf_op jit(solution)/shard_map/gather_rows/pallas_call | solution.py:629
  232.1 2.6 copy-done.9
  234.8 2.6 copy-done.10
  238.1 5.0 place_rows.1
  243.1 17.9 %fetch_rows.3.g_ref = bf16[4,1024,768]{2,1,0:T(8,128)(2,1)} custom-call(s32[1]{0:T(128)} %bitcast.15.first.f, f32[16,4096]{1,0:T(8,128)} %get-tuple-element.85.row_ref.p, bf16[4096,768]{1,0:T(8,128)(2,1)} %bitcast.85), custom_call_target="tpu_custom_call" | custom-call | flops 17999998976 | bytes 54000000 | tf_op jit(solution)/shard_map/fetch_rows/pallas_call | solution.py:1196
  260.9 19.0 %fetch_rows.2 = (bf16[4,1024,768]{2,1,0:T(8,128)(2,1)}, f32[4,1024,1]{2,1,0:T(8,128)}) custom-call(s32[1]{0:T(128)} %bitcast.15.first.f, f32[16,4096]{1,0:T(8,128)} %get-tuple-element.85.row_ref.p, f32[16,4096]{1,0:T(8,128)} %bitcast.92, bf16[4096,768]{1,0:T(8,128)(2,1)} %bitcast.84), custom_call_target="tpu_custom_call" | custom-call | flops 17999998976 | bytes 54000000 | tf_op jit(solution)/shard_map/fetch_rows/pallas_call | solution.py:1196
  280.0 14.0 %expert.7 = (bf16[1024,768]{1,0:T(8,128)(2,1)}, bf16[1024,896]{1,0:T(8,128)(2,1)}, bf16[4,3,192,512]{3,2,1,0:T(8,128)(2,1)}) custom-call(s32[1]{0:T(128)} %bitcast.15.first.f, bf16[4,1024,768]{2,1,0:T(8,128)(2,1)} %get-tuple-element.90.x_ref, bf16[4,1024,768]{2,1,0:T(8,128)(2,1)} %fetch_rows.3.g_ref, f32[4,1024,1]{2,1,0:T(8,128)} %get-tuple-element.92.gate_ref, ...), custom_call_target="tpu_custom_call" | custom-call | flops 14000000000 | bytes 42000000 | tf_op jit(solution)/shard_map/expert/pallas_call | solution.py:1253
  294.1 13.8 %expert.6 = (bf16[1024,768]{1,0:T(8,128)(2,1)}, bf16[1024,896]{1,0:T(8,128)(2,1)}, bf16[4,3,192,512]{3,2,1,0:T(8,128)(2,1)}) custom-call(s32[1]{0:T(128)} %bitcast.15.first.f, bf16[4,1024,768]{2,1,0:T(8,128)(2,1)} %get-tuple-element.90.x_ref, bf16[4,1024,768]{2,1,0:T(8,128)(2,1)} %fetch_rows.3.g_ref, f32[4,1024,1]{2,1,0:T(8,128)} %get-tuple-element.92.gate_ref, ...), custom_call_target="tpu_custom_call" | custom-call | flops 14000000000 | bytes 42000000 | tf_op jit(solution)/shard_map/expert/pallas_call | solution.py:1253
  310.8 14.2 %expert.5 = (bf16[1024,768]{1,0:T(8,128)(2,1)}, bf16[1024,896]{1,0:T(8,128)(2,1)}, bf16[4,3,192,512]{3,2,1,0:T(8,128)(2,1)}) custom-call(s32[1]{0:T(128)} %bitcast.15.first.f, bf16[4,1024,768]{2,1,0:T(8,128)(2,1)} %get-tuple-element.90.x_ref, bf16[4,1024,768]{2,1,0:T(8,128)(2,1)} %fetch_rows.3.g_ref, f32[4,1024,1]{2,1,0:T(8,128)} %get-tuple-element.92.gate_ref, ...), custom_call_target="tpu_custom_call" | custom-call | flops 14000000000 | bytes 42000000 | tf_op jit(solution)/shard_map/expert/pallas_call | solution.py:1253
  325.0 13.9 %expert.4 = (bf16[1024,768]{1,0:T(8,128)(2,1)}, bf16[1024,896]{1,0:T(8,128)(2,1)}, bf16[4,3,192,512]{3,2,1,0:T(8,128)(2,1)}) custom-call(s32[1]{0:T(128)} %bitcast.15.first.f, bf16[4,1024,768]{2,1,0:T(8,128)(2,1)} %get-tuple-element.90.x_ref, bf16[4,1024,768]{2,1,0:T(8,128)(2,1)} %fetch_rows.3.g_ref, f32[4,1024,1]{2,1,0:T(8,128)} %get-tuple-element.92.gate_ref, ...), custom_call_target="tpu_custom_call" | custom-call | flops 14000000000 | bytes 42000000 | tf_op jit(solution)/shard_map/expert/pallas_call | solution.py:1253
  338.9 22.4 %spread_rows.2 = bf16[4096,896]{1,0:T(8,128)(2,1)} custom-call(s32[1]{0:T(128)} %bitcast.15.first.f, f32[4096,16]{1,0:T(8,128)} %get-tuple-element.84.col_ref, bf16[1024,896]{1,0:T(8,128)(2,1)} %get-tuple-element.93.refs_0_, bf16[1024,896]{1,0:T(8,128)(2,1)} %get-tuple-element.94.refs_1_, bf16[1024,896]{1,0:T(8,128)(2,1)} %get-tuple-element.95.refs_2_, ...), custom_call_target="tpu_custom_call" | custom-call | flops 20000000000 | bytes 60000000 | tf_op jit(solution)/shard_map/spread_rows/pallas_call | solution.py:1298
  361.3 3.1 copy-done.6
  364.4 36.5 %sum_rows.2.dn_ref = f32[512,896]{1,0:T(8,128)S(1)} custom-call(bf16[8,512,896]{2,1,0:T(8,128)(2,1)S(1)} %bitcast.80), custom_call_target="tpu_custom_call" | custom-call | flops 35000000512 | bytes 105000000 | tf_op jit(solution)/shard_map/sum_rows/pallas_call | solution.py:660
  402.2 15.6 %backward_rows.1 = (f32[512,768]{1,0:T(8,128)}, bf16[4,192,512]{2,1,0:T(8,128)(2,1)}, bf16[768,768]{1,0:T(8,128)(2,1)}, f32[24,768]{1,0:T(8,128)}) custom-call(s32[1]{0:T(128)} %bitcast.10.place, f32[512,768]{1,0:T(8,128)} %get-tuple-element.82.res_ref, f32[512,896]{1,0:T(8,128)} %copy-done.17, bf16[512,768]{1,0:T(8,128)(2,1)} %cot_ref.1, ...), custom_call_target="tpu_custom_call" | custom-call | flops 15000000512 | bytes 45000000 | tf_op jit(solution)/shard_map/backward_rows/pallas_call | solution.py:1074
  420.2 24.5 %to_heads.1 = (bf16[4,192,512]{2,1,0:T(8,128)(2,1)S(1)}, bf16[192,768]{1,0:T(8,128)(2,1)S(1)}) custom-call(bf16[4,192,512]{2,1,0:T(8,128)(2,1)S(1)} %copy-done.20, bf16[4,192,768]{2,1,0:T(8,128)(2,1)S(1)} %bitcast.88), custom_call_target="tpu_custom_call" | custom-call | flops 12000000000 | bytes 36000000 | tf_op jit(solution)/shard_map/to_heads/pallas_call | solution.py:807
  446.3 50.1 %revisit.1 = (f32[3,64,4096]{2,1,0:T(8,128)}, f32[3,64,4096]{2,1,0:T(8,128)}, f32[3,64,4096]{2,1,0:T(8,128)}) custom-call(s32[4]{0:T(128)} %pad_add_fusion.table, bf16[3,64,4096]{2,1,0:T(8,128)(2,1)} %get-tuple-element.74.qt_ref, bf16[3,4096,64]{2,1,0:T(8,128)(2,1)} %get-tuple-element.75.k_ref, bf16[3,64,4096]{2,1,0:T(8,128)(2,1)} %get-tuple-element.76.kt_ref, ...), custom_call_target="tpu_custom_call" | custom-call | flops 49999998976 | bytes 150000000 | tf_op jit(solution)/shard_map/revisit/pallas_call | solution.py:212
  496.4 18.4 %spread_rows.3 = bf16[4096,768]{1,0:T(8,128)(2,1)} custom-call(s32[1]{0:T(128)} %bitcast.15.first.f, f32[4096,16]{1,0:T(8,128)} %get-tuple-element.84.col_ref, bf16[1024,768]{1,0:T(8,128)(2,1)} %get-tuple-element.117.refs_0_, bf16[1024,768]{1,0:T(8,128)(2,1)} %get-tuple-element.118.refs_1_, bf16[1024,768]{1,0:T(8,128)(2,1)} %get-tuple-element.119.refs_2_, ...), custom_call_target="tpu_custom_call" | custom-call | flops 20000000000 | bytes 60000000 | tf_op jit(solution)/shard_map/spread_rows/pallas_call | solution.py:1298
  514.8 17.0 %unproject.1 = (bf16[4096,768]{1,0:T(8,128)(2,1)}, bf16[2,4,384,192]{3,2,1,0:T(8,128)(2,1)}, f32[4,24,192]{2,1,0:T(8,128)}) custom-call(s32[8]{0:T(128)} %convert_element_type.73.owned, f32[3,64,4096]{2,1,0:T(8,128)} %get-tuple-element.101.dq_ref, f32[3,64,4096]{2,1,0:T(8,128)} %get-tuple-element.102.dk_ref, f32[3,64,4096]{2,1,0:T(8,128)} %get-tuple-element.103.dv_ref, ...), custom_call_target="tpu_custom_call" | custom-call | flops 17999998976 | bytes 54000000 | tf_op jit(solution)/shard_map/unproject/pallas_call | solution.py:294
  531.8 2.8 copy-done.8
  534.6 32.0 %sum_rows.3.feed_ref = f32[512,768]{1,0:T(8,128)S(1)} custom-call(bf16[8,512,768]{2,1,0:T(8,128)(2,1)S(1)} %bitcast.83), custom_call_target="tpu_custom_call" | custom-call | flops 35000000512 | bytes 105000000 | tf_op jit(solution)/shard_map/sum_rows/pallas_call | solution.py:660
  567.8 3.4 pad_maximum_fusion.1.ge_ref
  571.2 101.2 %closing.1 = (f32[512,768]{1,0:T(8,128)S(1)}, f32[2,384,192]{2,1,0:T(8,128)S(1)}, f32[24,192]{1,0:T(8,128)S(1)}, f32[8,128]{1,0:T(8,128)S(1)}, bf16[2,4,3,192,512]{4,3,2,1,0:T(8,128)(2,1)}) custom-call(bf16[8,512,768]{2,1,0:T(8,128)(2,1)} %bitcast.101, bf16[2,4,384,192]{3,2,1,0:T(8,128)(2,1)S(1)} %copy-done.18, f32[4,24,192]{2,1,0:T(8,128)S(1)} %copy-done.24, ...), custom_call_target="tpu_custom_call" | custom-call | flops 40000000000 | bytes 120000000 | tf_op jit(solution)/shard_map/closing/pallas_call | solution.py:909
  674.9 7.3 %bitcast_convert_fusion = f32[8,3,192,512]{3,2,1,0:T(8,128)} fusion(bf16[2,4,3,192,512]{4,3,2,1,0:T(8,128)(2,1)} %get-tuple-element.125), kind=kLoop, calls=%fused_computation | loop fusion | flops 2359296 | bytes 14155776 | tf_op jit(solution)/shard_map/convert_element_type | solution.py:1435
  682.2 7.8 %slice_bitcast_fusion = (f32[8,192,512]{2,1,0:T(8,128)}, f32[8,192,512]{2,1,0:T(8,128)}, f32[8,192,512]{2,1,0:T(8,128)}) fusion(f32[8,3,192,512]{3,2,1,0:T(8,128)} %bitcast_convert_fusion), kind=kLoop, calls=%fused_computation.1 | loop fusion | bytes 18874368 | tf_op jit(solution)/shard_map/squeeze | solution.py:1436
  694.1 5.3 finish_rows.1
  (145 shorter events, 45.2 us)
Async XLA Ops:
  7.2 1.4 copy-start
  7.2 272.8 %all-gather.3.cloned.1.call-start = ((), (), s32[]{:S(2)}) async-start(), calls=%async_computation.8 | async-start | bytes 11796480 | tf_op jit(solution)/shard_map/all_gather | solution.py:1369
  11.8 2.1 copy-start.31
  11.8 2.2 copy-start.37
  11.8 2.3 copy-start.38
  11.8 2.4 copy-start.39
  11.8 2.5 copy-start.35
  11.8 2.6 copy-start.36
  11.8 2.8 copy-start.27
  11.9 2.8 copy-start.29
  11.9 2.8 copy-start.32
  11.9 555.8 %reduce-scatter.11.cloned.1.call-start = ((), (), s32[]{:S(2)}) async-start(), calls=%async_computation.7 | async-start | bytes 2949120 | tf_op jit(solution)/shard_map/reduce_scatter | solution.py:1416
  69.2 2.6 copy-start.7
  71.8 10.3 %copy-start.2 = (s32[2,2048,2]{2,1,0:T(8,128)}, s32[2,2048,2]{2,1,0:T(8,128)S(1)}, u32[]{:S(2)}) copy-start(s32[2,2048,2]{2,1,0:T(8,128)S(1)} %get-tuple-element.83) | copy-start | bytes 98308
  74.5 5.2 copy-start.25
  83.3 3.9 copy-start.26
  232.1 2.6 copy-start.9
  234.8 2.6 copy-start.10
  294.0 273.7 %reduce-scatter.9.cloned.1.call-start = ((), (), s32[]{:S(2)}) async-start(), calls=%async_computation.6 | async-start | bytes 2949120 | tf_op jit(solution)/shard_map/reduce_scatter | solution.py:1416
  307.9 1.3 copy-start.33
  307.9 259.9 %reduce-scatter.7.cloned.1.call-start = ((), (), s32[]{:S(2)}) async-start(), calls=%async_computation.5 | async-start | bytes 2949120 | tf_op jit(solution)/shard_map/reduce_scatter | solution.py:1416
  338.9 228.9 %reduce-scatter.5.cloned.1.call-start = ((), (), s32[]{:S(2)}) async-start(), calls=%async_computation.4 | async-start | bytes 2949120 | tf_op jit(solution)/shard_map/reduce_scatter | solution.py:1416
  361.3 3.1 copy-start.6
  417.8 1.3 copy-start.12
  531.8 2.8 copy-start.8
  567.7 3.5 copy-start.18
  567.7 3.5 copy-start.24
  672.5 9.7 %copy-start.14 = (f32[512,768]{1,0:T(8,128)}, f32[512,768]{1,0:T(8,128)S(1)}, u32[]{:S(2)}) copy-start(f32[512,768]{1,0:T(8,128)S(1)} %get-tuple-element.114.dn_ref) | copy-start | bytes 4718596
  690.0 3.4 copy-start.28
  690.0 3.4 copy-start.30
  693.2 6.1 copy-start.41
  694.1 5.3 copy-start.1
  (15 other events, 14.8 us)
Sparse Core Ops, SparseCore 0:
  12.0 196.2 all-gather.2
  294.1 71.7 reduce-scatter.10
  368.3 47.5 reduce-scatter.8
  418.0 47.5 reduce-scatter.6
  467.7 47.5 reduce-scatter.4

commit v3 on v2

v3 whole, which is shorter than its diff:
```python
import functools

import jax
import jax.numpy as jnp
import numpy as np
from jax import lax
from jax.experimental import pallas as pl
from jax.experimental.pallas import tpu as pltpu
from jax.sharding import PartitionSpec as P

HEAD_DIM = 64
EXPERTS = 12
FFN_EXPERTS = 8
CAP = 512
BLOCK = 512
EXTRA = 128
SMALL = 32
SLOT = 256
MESH = pl.DeviceIdType.MESH

epsilon = 1e-06
rope_base = 10000.0
bf16 = jnp.bfloat16
f32 = jnp.float32

NN = (((1,), (0,)), ((), ()))
NT = (((1,), (1,)), ((), ()))
TN = (((0,), (0,)), ((), ()))


def mm(left, right, dims=NN, precision=None):
    return lax.dot_general(
        left, right, dims, preferred_element_type=f32, precision=precision
    )


def params(mib=56, **more):
    return pltpu.CompilerParams(vmem_limit_bytes=mib * 1024 * 1024, **more)


def cost(us):
    return pl.CostEstimate(flops=int(us * 1e9), bytes_accessed=int(us * 3e6), transcendentals=0)


def full(shape):
    return pl.BlockSpec(shape, lambda *_: (0,) * len(shape))


def rope_tables(total):
    half = HEAD_DIM // 2
    freqs = np.float32(rope_base) ** (np.float32(-2.0) * np.arange(half, dtype=np.float32) / np.float32(HEAD_DIM))
    angles = freqs.astype(np.float32)[:, None] * np.arange(total, dtype=np.float32)[None, :]
    angles = angles.astype(np.float64)
    return jnp.asarray(np.cos(angles), f32), jnp.asarray(np.sin(angles), f32)


def zig(core, i):
    return 4 * (i // 2) + (core if i % 2 == 0 else 3 - core)


def anywhere(count):
    return [pl.BlockSpec(memory_space=pl.ANY)] * count


def spot():
    return lax.axis_index("shard"), lax.axis_index("ctx"), lax.axis_index("tp")


def across(t):
    return t + 1 - 2 * lax.rem(t, 2), lax.rem(t + 2, 4), 3 - t


def remote(source, target, sends, recvs, **where):
    return pltpu.make_async_remote_copy(
        src_ref=source,
        dst_ref=target,
        send_sem=sends,
        recv_sem=recvs,
        device_id=where,
        device_id_type=MESH,
    )


def greet(depth=True):
    z, c, t = spot()
    nc, nt, ns = lax.axis_size("ctx"), lax.axis_size("tp"), lax.axis_size("shard")
    barrier = pltpu.get_barrier_semaphore()
    for step in range(1, nc * nt):
        other = lax.rem(c * nt + t + step, nc * nt)
        pl.semaphore_signal(
            barrier,
            inc=1,
            device_id={"ctx": other // nt, "tp": lax.rem(other, nt)},
            device_id_type=MESH,
        )
    if depth:
        for step in range(1, ns):
            pl.semaphore_signal(
                barrier,
                inc=1,
                device_id={"shard": lax.rem(z + step, ns)},
                device_id_type=MESH,
            )
    pl.semaphore_wait(barrier, nc * nt - 1 + (ns - 1 if depth else 0))


class Gather:
    KINDS = 9

    def __init__(self, x, out, sends, recvs, own, cuts):
        z, c, t = spot()
        tx, ty, td = across(t)
        rows = x.shape[0] // cuts
        half = rows // 2
        self.cuts = cuts
        self.own = pltpu.make_async_copy(x, out.at[4 * c + t], own)
        sib = {"ctx": 1 - c}
        px, py = {"tp": tx}, {"tp": ty}

        def copies(s):
            whole = pl.ds(s * rows, rows)
            one, two = pl.ds(s * rows, half), pl.ds(s * rows + half, half)

            def at(k, source, target, where):
                return remote(source, target, sends.at[s, k], recvs.at[s, k], **where)

            def keep(k, slot, part, where):
                ref = out.at[4 * c + slot, part]
                return at(k, ref, ref, where)

            mine = [
                at(k, x.at[whole], out.at[4 * c + t, whole], where)
                for k, where in enumerate((px, py, sib))
            ]
            return mine + [
                keep(3, tx, whole, sib),
                keep(4, tx, one, py),
                keep(5, ty, whole, sib),
                keep(6, ty, two, px),
                keep(7, td, one, sib),
                keep(8, td, two, sib),
            ]

        self.copies = [copies(s) for s in range(cuts)]

        def arrivals(s):
            whole = pl.ds(s * rows, rows)
            one, two = pl.ds(s * rows, half), pl.ds(s * rows + half, half)
            where = [(c, tx, whole), (c, ty, whole), (1 - c, t, whole)]
            where += [(1 - c, tx, whole), (c, td, one), (1 - c, ty, whole), (c, td, two)]
            where += [(1 - c, td, one), (1 - c, td, two)]
            return [
                remote(out.at[4 * d + slot, part], out.at[4 * d + slot, part], sends.at[s, k], recvs.at[s, k], **sib)
                for k, (d, slot, part) in enumerate(where)
            ]

        self.arrivals = [arrivals(s) for s in range(cuts)]

    @staticmethod
    def scratch(cuts):
        return [
            pltpu.SemaphoreType.DMA((cuts, Gather.KINDS)),
            pltpu.SemaphoreType.DMA((cuts, Gather.KINDS)),
            pltpu.SemaphoreType.DMA,
        ]

    def first(self):
        for s in range(self.cuts):
            for k in (0, 1, 2):
                self.copies[s][k].start()
        self.own.start()

    def second(self):
        for s in range(self.cuts):
            self.arrivals[s][0].wait_recv()
            self.copies[s][4].start()
            self.copies[s][3].start()
            self.arrivals[s][1].wait_recv()
            self.copies[s][6].start()
            self.copies[s][5].start()

    def third(self):
        for s in range(self.cuts):
            for k in (4, 6):
                self.arrivals[s][k].wait_recv()
                self.copies[s][7 if k == 4 else 8].start()

    def last(self):
        for s in range(self.cuts):
            for k in (2, 3, 5, 7, 8):
                self.arrivals[s][k].wait_recv()
        for s in range(self.cuts):
            for k in range(self.KINDS):
                self.copies[s][k].wait_send()
        self.own.wait()


class Sum:
    def __init__(self, p, held, came, across_in, across_out, sends, recvs, loads):
        z, c, t = spot()
        self.t = t
        tx, ty, td = across(t)
        half = p.shape[1] // 2
        self.half = half
        self.one, self.two = pl.ds(0, half), pl.ds(half, half)
        self.order = (td, tx, ty, t)
        self.held, self.came, self.inn = held, came, across_in
        sib, px, py = {"ctx": 1 - c}, {"tp": tx}, {"tp": ty}
        self.loads = [pltpu.make_async_copy(p.at[4 * c + o], held.at[o], loads.at[k]) for k, o in enumerate(self.order)]
        self.core = []
        for k, o in enumerate(self.order):
            self.core.append(remote(p.at[4 * (1 - c) + o], came.at[o], sends.at[k], recvs.at[k], **sib))

        def send(k, source, slot, where):
            return remote(source, across_in.at[slot], sends.at[k], recvs.at[k], **where)

        self.side = {
            "dx": send(4, held.at[td, self.one], 0, px),
            "dy": send(5, held.at[td, self.two], 1, py),
            "x": send(6, held.at[tx, self.one], 2, px),
            "y": send(7, held.at[ty, self.two], 3, py),
            "cy": send(8, across_out.at[0], 4, py),
            "cx": send(9, across_out.at[1], 5, px),
        }
        self.out = across_out
        self.near = (tx, ty, td)

    @staticmethod
    def scratch(rows, width):
        return [
            pltpu.VMEM((4, rows, width), bf16),
            pltpu.VMEM((4, rows, width), bf16),
            pltpu.VMEM((6, rows // 2, width), bf16),
            pltpu.VMEM((2, rows // 2, width), bf16),
            pltpu.SemaphoreType.DMA((10,)),
            pltpu.SemaphoreType.DMA((10,)),
            pltpu.SemaphoreType.DMA((4,)),
        ]

    def first(self):
        for k in range(4):
            self.core[k].start()
            self.loads[k].start()

    def second(self):
        for k, o in enumerate(self.order):
            self.loads[k].wait()
            self.core[k].wait_recv()
            self.held[o] = (self.held[o].astype(f32) + self.came[o].astype(f32)).astype(bf16)
            if k == 0:
                self.side["dx"].start()
                self.side["dy"].start()
            if k == 1:
                self.side["x"].start()
            if k == 2:
                self.side["y"].start()

    def third(self):
        tx, ty, td = self.near
        self.side["dx"].wait_recv()
        self.out[0] = (self.held[ty, self.one].astype(f32) + self.inn[0].astype(f32)).astype(bf16)
        self.side["cy"].start()
        self.side["dy"].wait_recv()
        self.out[1] = (self.held[tx, self.two].astype(f32) + self.inn[1].astype(f32)).astype(bf16)
        self.side["cx"].start()

    def last(self):
        for k in ("x", "y", "cy", "cx"):
            self.side[k].wait_recv()
        for copy in self.core + list(self.side.values()):
            copy.wait_send()

    def total(self):
        def add(part, a, b):
            return self.held[self.t, part].astype(f32) + self.inn[a].astype(f32) + self.inn[b].astype(f32)

        return add(self.one, 2, 4), add(self.two, 3, 5)


def qkv_kernel(x_ref, w_ref, cos_ref, sin_ref, qt_ref, kt_ref, k_ref, v_ref, vt_ref, wt_ref, wo_ref, small_ref):
    heads = qt_ref.shape[0]
    width = heads * HEAD_DIM
    half = HEAD_DIM // 2

    @pl.when(pl.program_id(0) == 0)
    def _():
        def whole(core, which, here):
            v = w_ref[core, :, which].astype(f32)
            return v.reshape(v.shape[0] * v.shape[1], SLOT)[:, here].T

        mine = slice(0, width)
        wt_ref[:width] = whole(0, 0, mine).astype(bf16)
        wt_ref[width : 2 * width] = whole(0, 1, mine).astype(bf16)
        wt_ref[2 * width :] = whole(1, 0, mine).astype(bf16)
        wo_ref[...] = whole(1, 1, mine).astype(bf16)
        small_ref[...] = whole(0, 0, slice(width, width + SMALL))

    x = x_ref[...].astype(f32)
    inverse = lax.rsqrt(jnp.mean(x * x, axis=1, keepdims=True) + epsilon)
    a = (x * inverse * small_ref[18:19]).astype(bf16)
    y = mm(wt_ref[...], a, NT)
    c, s = cos_ref[...], sin_ref[...]

    def turned(first):
        u, w = y[first : first + half], y[first + half : first + HEAD_DIM]
        return jnp.concatenate([u * c - w * s, w * c + u * s], axis=0)

    for h in range(heads):
        at = h * HEAD_DIM
        qt_ref[h] = (turned(at) * HEAD_DIM**-0.5).astype(bf16)
        key = turned(width + at)
        kt_ref[h] = key.astype(bf16)
        k_ref[h] = key.T.astype(bf16)
        value = y[2 * width + at : 2 * width + at + HEAD_DIM]
        v_ref[h] = value.T.astype(bf16)
        vt_ref[h, :HEAD_DIM] = value.astype(bf16)
        vt_ref[h, HEAD_DIM:] = jnp.ones((16, value.shape[1]), bf16)


def project(rows, w, cosine, sine, heads):
    total, width = rows.shape
    tile = BLOCK
    out = heads * HEAD_DIM
    shapes = [
        jax.ShapeDtypeStruct((heads, HEAD_DIM, total), bf16),
        jax.ShapeDtypeStruct((heads, HEAD_DIM, total), bf16),
        jax.ShapeDtypeStruct((heads, total, HEAD_DIM), bf16),
        jax.ShapeDtypeStruct((heads, total, HEAD_DIM), bf16),
        jax.ShapeDtypeStruct((heads, HEAD_DIM + 16, total), bf16),
        jax.ShapeDtypeStruct((3 * out, width), bf16),
        jax.ShapeDtypeStruct((out, width), bf16),
        jax.ShapeDtypeStruct((SMALL, width), f32),
    ]
    return pl.pallas_call(
        qkv_kernel,
        grid=(total // tile,),
        in_specs=[
            pl.BlockSpec((tile, width), lambda i: (i, 0)),
            full(w.shape),
            pl.BlockSpec((HEAD_DIM // 2, tile), lambda i: (0, i)),
            pl.BlockSpec((HEAD_DIM // 2, tile), lambda i: (0, i)),
        ],
        out_specs=[
            pl.BlockSpec((heads, HEAD_DIM, tile), lambda i: (0, 0, i)),
            pl.BlockSpec((heads, HEAD_DIM, tile), lambda i: (0, 0, i)),
            pl.BlockSpec((heads, tile, HEAD_DIM), lambda i: (0, i, 0)),
            pl.BlockSpec((heads, tile, HEAD_DIM), lambda i: (0, i, 0)),
            pl.BlockSpec((heads, HEAD_DIM + 16, tile), lambda i: (0, 0, i)),
        ]
        + [full(v.shape) for v in shapes[5:]],
        out_shape=shapes,
        compiler_params=params(),
        cost_estimate=cost(13),
        name="project",
    )(rows, w, cosine, sine)


def dealt(core, i):
    return 4 * (i // 2) + jnp.where(lax.rem(i, 2) == 0, core, 3 - core)


def attend_kernel(cuts, length, qt_ref, k_ref, vt_ref, cot_ref, w_ref, ot_ref, lse_ref, top_ref, cots_ref, ws_ref, mask_cot, w_send, w_recv, w_own, *sems):
    z, c, t = spot()
    nt = lax.axis_size("tp")
    h, i = pl.program_id(0), pl.program_id(1)
    count = pl.num_programs(1)
    at_step = h * count + i
    last = pl.num_programs(0) * count - 1
    gather = Gather(mask_cot, cots_ref, *sems, cuts)
    half = w_ref.shape[0] // 2
    mine = pl.ds(c * half, half)
    theirs = pl.ds((1 - c) * half, half)
    away, came = [], []
    for step in range(1, nt):
        there, back = lax.rem(t + step, nt), lax.rem(t + nt - step, nt)
        away.append(remote(w_ref.at[mine], ws_ref.at[t, mine], w_send.at[step], w_recv.at[step], tp=there))
        ref = ws_ref.at[back, mine]
        came.append(remote(ref, ref, w_send.at[nt + step], w_recv.at[step], ctx=1 - c))
        ref = ws_ref.at[back, theirs]
        came.append(remote(ref, ref, w_send.at[nt + step], w_recv.at[nt + step], ctx=1 - c))
    onward = [
        remote(ws_ref.at[lax.rem(t + nt - step, nt), mine], ws_ref.at[lax.rem(t + nt - step, nt), mine],
               w_send.at[nt + step], w_recv.at[nt + step], ctx=1 - c)
        for step in range(1, nt)
    ]
    own_w = pltpu.make_async_copy(w_ref, ws_ref.at[t], w_own)

    @pl.when(at_step == 0)
    def _():
        rows = cot_ref.shape[0]
        position = (c * nt + t) * rows + lax.broadcasted_iota(jnp.int32, cot_ref.shape, 0)
        mask_cot[...] = jnp.where(position < length[0], cot_ref[...].astype(f32), 0.0).astype(bf16)
        greet(False)
        gather.first()
        for copy in away:
            copy.start()
        own_w.start()

    index = dealt(c, i)
    columns = BLOCK
    qt = qt_ref[0, :, pl.ds(pl.multiple_of(index * BLOCK, BLOCK), BLOCK)]

    def step(at, carry, diagonal):
        peak, total = carry
        start = pl.multiple_of(at * BLOCK, BLOCK)
        scores = mm(k_ref[0, pl.ds(start, BLOCK), :], qt)
        if diagonal:
            keys = lax.broadcasted_iota(jnp.int32, scores.shape, 0)
            queries = lax.broadcasted_iota(jnp.int32, scores.shape, 1)
            scores = jnp.where(keys <= queries, scores, -1e30)
        higher = jnp.maximum(peak, jnp.max(scores, axis=0, keepdims=True))
        weights = jnp.exp(scores - higher).astype(bf16)
        total = total * jnp.exp(peak - higher) + mm(vt_ref[0, :, pl.ds(start, BLOCK)], weights)
        return higher, total

    start = (jnp.full((1, columns), -1e30, f32), jnp.zeros((HEAD_DIM + 16, columns), f32))
    carry = lax.fori_loop(0, index, lambda at, c: step(at, c, False), start)
    peak, total = step(index, carry, True)
    mass = total[HEAD_DIM : HEAD_DIM + 1]
    ot_ref[0] = (total[:HEAD_DIM] / mass).astype(bf16)
    lse_ref[0, 0] = peak + jnp.log(mass)
    position = index * BLOCK + lax.broadcasted_iota(jnp.int32, peak.shape, 1)
    top_ref[0, 0] = jnp.where(position < length[0], peak, -1e30)

    @pl.when(at_step == last // 2 + 1)
    def _():
        gather.second()
        for copy, forth in zip(came[0::2], onward):
            copy.wait_recv()
            forth.start()

    @pl.when(at_step == last - 1)
    def _():
        gather.third()

    @pl.when(at_step == last)
    def _():
        gather.last()
        for copy in came[1::2]:
            copy.wait_recv()
        for copy in away + onward:
            copy.wait_send()
        own_w.wait()


def attend(length, qt, k, vt, cot, w, count, number):
    cuts = 2
    heads, _, total = qt.shape
    nt = lax.axis_size("tp")
    return pl.pallas_call(
        functools.partial(attend_kernel, cuts),
        grid_spec=pltpu.PrefetchScalarGridSpec(
            num_scalar_prefetch=1,
            grid=(heads, count),
            in_specs=[
                pl.BlockSpec((1, HEAD_DIM, total), lambda h, i, n: (h, 0, 0)),
                pl.BlockSpec((1, total, HEAD_DIM), lambda h, i, n: (h, 0, 0)),
                pl.BlockSpec((1, HEAD_DIM + 16, total), lambda h, i, n: (h, 0, 0)),
                full(cot.shape),
                full(w.shape),
            ],
            out_specs=[
                pl.BlockSpec((1, HEAD_DIM, BLOCK), lambda h, i, n: (i, h, 0)),
                pl.BlockSpec((1, 1, 1, BLOCK), lambda h, i, n: (h, i, 0, 0)),
                pl.BlockSpec((1, 1, 1, BLOCK), lambda h, i, n: (h, i, 0, 0)),
            ]
            + anywhere(2),
            scratch_shapes=[
                pltpu.VMEM(cot.shape, bf16),
                pltpu.SemaphoreType.DMA((2 * nt,)),
                pltpu.SemaphoreType.DMA((2 * nt,)),
                pltpu.SemaphoreType.DMA,
            ]
            + Gather.scratch(cuts),
        ),
        out_shape=[
            jax.ShapeDtypeStruct((count, heads * HEAD_DIM, BLOCK), bf16),
            jax.ShapeDtypeStruct((heads, count, 1, BLOCK), f32),
            jax.ShapeDtypeStruct((heads, count, 1, BLOCK), f32),
            jax.ShapeDtypeStruct((8,) + cot.shape, bf16),
            jax.ShapeDtypeStruct((nt,) + w.shape, bf16),
        ],
        compiler_params=params(collective_id=number, has_side_effects=True),
        cost_estimate=cost(35),
        name="attend",
    )(length, qt, k, vt, cot, w)


def revisit_kernel(qt_ref, k_ref, kt_ref, v_ref, ot_ref, got_ref, lse_ref, go_ref, dq_ref, dk_ref, dv_ref, gos_ref, sum_k, sum_v, came_ref, w_send, w_recv):
    z, c, t = spot()
    nt = lax.axis_size("tp")
    h, i = pl.program_id(0), pl.program_id(1)
    count = pl.num_programs(1)
    index = dealt(c, i)
    here = pl.ds(pl.multiple_of(index * BLOCK, BLOCK), BLOCK)
    away = [
        remote(go_ref.at[lax.rem(t + step, nt)], came_ref.at[step], w_send.at[step], w_recv.at[step], tp=lax.rem(t + step, nt))
        for step in range(1, nt)
    ]

    @pl.when(h * count + i == 0)
    def _():
        greet(False)
        for copy in away:
            copy.start()

    qt, got = qt_ref[0, :, here], got_ref[0]
    lse = lse_ref[0, 0]
    centre = jnp.sum(ot_ref[0].astype(f32) * got.astype(f32), axis=0, keepdims=True)

    @pl.when(i == 0)
    def _():
        sum_k[...] = jnp.zeros_like(sum_k)
        sum_v[...] = jnp.zeros_like(sum_v)
        dq_ref[...] = jnp.zeros_like(dq_ref)

    def step(at, grad, diagonal):
        start = pl.multiple_of(at * BLOCK, BLOCK)
        here = pl.ds(start, BLOCK)
        scores = mm(k_ref[0, here, :], qt)
        probs = jnp.exp(scores - lse)
        if diagonal:
            keys = lax.broadcasted_iota(jnp.int32, scores.shape, 0)
            queries = lax.broadcasted_iota(jnp.int32, scores.shape, 1)
            probs = jnp.where(keys <= queries, probs, 0.0)
        grad_probs = mm(v_ref[0, here, :], got)
        grad_scores = (probs * (grad_probs - centre)).astype(bf16)
        sum_v[here, :] += mm(probs.astype(bf16), got, NT)
        sum_k[here, :] += mm(grad_scores, qt, NT)
        return grad + mm(kt_ref[0, :, here], grad_scores)

    grad = lax.fori_loop(0, index, lambda at, c: step(at, c, False), jnp.zeros(qt.shape, f32))
    dq_ref[0, :, here] = step(index, grad, True) * HEAD_DIM**-0.5

    @pl.when(i == count - 1)
    def _():
        dk_ref[0] = sum_k[...].T
        dv_ref[0] = sum_v[...].T

    @pl.when(h * count + i == pl.num_programs(0) * count - 1)
    def _():
        total = go_ref[t].astype(f32)
        for step, copy in enumerate(away):
            copy.wait_recv()
            total = total + came_ref[step + 1].astype(f32)
            copy.wait_send()
        gos_ref[...] = total.astype(bf16)


def revisit(qt, k, kt, v, ot, got, lse, go, number):
    heads, _, total = qt.shape
    count = ot.shape[0]
    nt = lax.axis_size("tp")
    whole = pl.BlockSpec((1, HEAD_DIM, total), lambda h, i: (h, 0, 0))
    tall = pl.BlockSpec((1, total, HEAD_DIM), lambda h, i: (h, 0, 0))
    some = pl.BlockSpec((1, HEAD_DIM, BLOCK), lambda h, i: (i, h, 0))
    return pl.pallas_call(
        revisit_kernel,
        grid=(heads, count),
        in_specs=[
            whole,
            tall,
            whole,
            tall,
            some,
            some,
            pl.BlockSpec((1, 1, 1, BLOCK), lambda h, i: (h, i, 0, 0)),
            full(go.shape),
        ],
        out_specs=[whole, whole, whole, full(go.shape[1:])],
        scratch_shapes=[
            pltpu.VMEM((total, HEAD_DIM), f32),
            pltpu.VMEM((total, HEAD_DIM), f32),
            pltpu.VMEM(go.shape, bf16),
            pltpu.SemaphoreType.DMA((nt,)),
            pltpu.SemaphoreType.DMA((nt,)),
        ],
        out_shape=[jax.ShapeDtypeStruct((heads, HEAD_DIM, total), f32)] * 3 + [jax.ShapeDtypeStruct(go.shape[1:], bf16)],
        compiler_params=params(collective_id=number, has_side_effects=True),
        cost_estimate=cost(50),
        name="revisit",
    )(qt, k, kt, v, ot, got, lse, go)


def unproject_kernel(dq_ref, dk_ref, dv_ref, cos_ref, sin_ref, x_ref, gain_ref, wt_ref, go_ref, small_ref,
                     part_ref, gw_ref, smalls_ref, total, row):
    heads = dq_ref.shape[0]
    half = HEAD_DIM // 2
    i = pl.program_id(0)
    c, s = cos_ref[...], sin_ref[...]

    def turned(g):
        u, w = g[:half], g[half:]
        return jnp.concatenate([u * c + w * s, w * c - u * s], axis=0)

    @pl.when(i == 0)
    def _():
        total[...] = jnp.zeros_like(total)
        row[...] = jnp.zeros_like(row)

    x = x_ref[...].astype(f32)
    m = x * lax.rsqrt(jnp.mean(x * x, axis=1, keepdims=True) + epsilon)
    a = (m * gain_ref[18:19]).astype(bf16)
    pieces = [turned(dq_ref[h]) for h in range(heads)]
    pieces += [turned(dk_ref[h]) for h in range(heads)]
    pieces += [dv_ref[h] for h in range(heads)]
    grads = jnp.concatenate(pieces, axis=0).astype(bf16)
    part = mm(grads, wt_ref[...], TN)
    part_ref[...] = part.astype(bf16)
    row[...] += jnp.sum(part * m, axis=0, keepdims=True)
    total[...] += mm(grads, a)

    @pl.when(i == pl.num_programs(0) - 1)
    def _():
        _, parts, rows, depth = gw_ref.shape
        mid = rows // 2
        at = lax.broadcasted_iota(jnp.int32, small_ref.shape, 0)
        smalls = small_ref[...] + jnp.where(at == 19, row[...], 0.0)
        for z in range(parts):
            here = slice(z * depth, (z + 1) * depth)
            gw_ref[0, z] = total[:rows, here].astype(bf16)
            gw_ref[1, z, :mid] = total[rows:, here].astype(bf16)
            gw_ref[1, z, mid:] = go_ref[:, here]
            smalls_ref[z] = smalls[:, here]


def unproject(dq, dk, dv, cosine, sine, x, gain, wt, go, small, parts):
    heads, _, rows = dq.shape
    width = x.shape[1]
    out = wt.shape[0]
    depth = width // parts
    piece = pl.BlockSpec((heads, HEAD_DIM, BLOCK), lambda i: (0, 0, i))
    table = pl.BlockSpec((HEAD_DIM // 2, BLOCK), lambda i: (0, i))
    shapes = [
        jax.ShapeDtypeStruct((rows, width), bf16),
        jax.ShapeDtypeStruct((2, parts, 2 * heads * HEAD_DIM, depth), bf16),
        jax.ShapeDtypeStruct((parts,) + small.shape[:1] + (depth,), f32),
    ]
    return pl.pallas_call(
        unproject_kernel,
        grid_spec=pl.GridSpec(
            grid=(rows // BLOCK,),
            in_specs=[
                piece,
                piece,
                piece,
                table,
                table,
                pl.BlockSpec((BLOCK, width), lambda i: (i, 0)),
                full(gain.shape),
                full(wt.shape),
                full(go.shape),
                full(small.shape),
            ],
            out_specs=[pl.BlockSpec((BLOCK, width), lambda i: (i, 0))] + [full(v.shape) for v in shapes[1:]],
            scratch_shapes=[pltpu.VMEM((out, width), f32), pltpu.VMEM((1, width), f32)],
        ),
        out_shape=shapes,
        compiler_params=params(),
        cost_estimate=cost(18),
        name="unproject",
    )(dq, dk, dv, cosine, sine, x, gain, wt, go, small)


def opening_kernel(cuts, x_ref, wq_ref, wk_ref, wv_ref, wo_ref, small_ref, routes_ref, out_ref, ws_ref, all_routes_ref, held, *sems):
    gather = Gather(x_ref, out_ref, *sems[:3], cuts)
    sends, recvs, local = sems[3:]
    z, c, t = spot()
    ns = lax.axis_size("shard")
    width = wq_ref.shape[1]
    held[0, :, :width] = jnp.where(c == 0, wq_ref[...].astype(f32), wv_ref[...].astype(f32)).astype(bf16)
    held[0, :, width : width + SMALL] = small_ref[...]
    held[0, :, width + SMALL :] = jnp.zeros((held.shape[1], SLOT - width - SMALL), bf16)
    held[1, :, :width] = jnp.where(c == 0, wk_ref[...].astype(f32), wo_ref[...].astype(f32).T).astype(bf16)
    held[1, :, width:] = jnp.zeros((held.shape[1], SLOT - width), bf16)
    greet()
    started = []

    def go(k, source, target, **where):
        copy = remote(source, target, sends.at[k], recvs.at[k], **where)
        copy.start()
        started.append(copy)

    def came(k, ref):
        remote(ref, ref, sends.at[k], recvs.at[k], ctx=1 - c).wait_recv()

    for step in range(1, ns):
        go(step, held, ws_ref.at[c, z], shard=lax.rem(z + step, ns))
    go(0, held, ws_ref.at[c, z], ctx=1 - c)
    gather.first()
    go(2 * ns, routes_ref, all_routes_ref.at[c], ctx=1 - c)
    mine = [
        pltpu.make_async_copy(held, ws_ref.at[c, z], local.at[0]),
        pltpu.make_async_copy(routes_ref, all_routes_ref.at[c], local.at[1]),
    ]
    for copy in mine:
        copy.start()
    gather.second()
    for step in range(1, ns):
        back = lax.rem(z + ns - step, ns)
        came(step, ws_ref.at[c, back])
        go(ns + step, ws_ref.at[c, back], ws_ref.at[c, back], ctx=1 - c)
    gather.third()
    gather.last()
    came(0, ws_ref.at[1 - c, z])
    came(2 * ns, all_routes_ref.at[1 - c])
    for step in range(1, ns):
        came(ns + step, ws_ref.at[1 - c, lax.rem(z + ns - step, ns)])
    for copy in started:
        copy.wait_send()
    for copy in mine:
        copy.wait()


def opening(x, wq, wk, wv, wo, small, routes, number):
    cuts = 2
    ns = lax.axis_size("shard")
    depth = wq.shape[0]
    vmem = pl.BlockSpec(memory_space=pltpu.VMEM)
    return pl.pallas_call(
        functools.partial(opening_kernel, cuts),
        in_specs=[vmem] * 7,
        out_specs=anywhere(3),
        out_shape=[
            jax.ShapeDtypeStruct((8,) + x.shape, x.dtype),
            jax.ShapeDtypeStruct((2, ns, 2, depth, SLOT), bf16),
            jax.ShapeDtypeStruct((2,) + routes.shape, routes.dtype),
        ],
        scratch_shapes=[pltpu.VMEM((2, depth, SLOT), bf16)]
        + Gather.scratch(cuts)
        + [
            pltpu.SemaphoreType.DMA((2 * ns + 1,)),
            pltpu.SemaphoreType.DMA((2 * ns + 1,)),
            pltpu.SemaphoreType.DMA((2,)),
        ],
        compiler_params=params(24, collective_id=number, has_side_effects=True),
        cost_estimate=cost(30),
        name="opening",
    )(x, wq, wk, wv, wo, small, routes)


def gather_kernel(cuts, count, *refs):
    xs, comb, outs, combs, sems = refs[:count], refs[count], refs[count + 1 : 2 * count + 1], refs[2 * count + 1], refs[2 * count + 2 :]
    gathers = [Gather(x, out, *sems[3 * i : 3 * i + 3], cuts) for i, (x, out) in enumerate(zip(xs, outs))]
    sends, recvs, local = sems[3 * count :]
    z, c, t = spot()
    own = 4 * c + t
    greet(False)
    for gather in gathers:
        gather.first()
    pairs = []
    for step in range(1, 8):
        other, back = lax.rem(own + step, 8), lax.rem(own + 8 - step, 8)
        where = {"ctx": other // 4, "tp": lax.rem(other, 4)}
        copy = remote(comb, combs.at[own], sends.at[step], recvs.at[step], **where)
        copy.start()
        pairs.append((copy, remote(comb, combs.at[back], sends.at[step], recvs.at[step], **where)))
    mine = pltpu.make_async_copy(comb, combs.at[own], local)
    mine.start()
    for gather in gathers:
        gather.second()
    for gather in gathers:
        gather.third()
    for gather in gathers:
        gather.last()
    for copy, came in pairs:
        came.wait_recv()
        copy.wait_send()
    mine.wait()


def gather_rows(xs, comb, number):
    cuts = 2
    return pl.pallas_call(
        functools.partial(gather_kernel, cuts, len(xs)),
        in_specs=[pl.BlockSpec(memory_space=pltpu.VMEM)] * (len(xs) + 1),
        out_specs=anywhere(len(xs) + 1),
        out_shape=[jax.ShapeDtypeStruct((8,) + x.shape, x.dtype) for x in (*xs, comb)],
        scratch_shapes=Gather.scratch(cuts) * len(xs)
        + [
            pltpu.SemaphoreType.DMA((8,)),
            pltpu.SemaphoreType.DMA((8,)),
            pltpu.SemaphoreType.DMA,
        ],
        compiler_params=params(16, collective_id=number, has_side_effects=True),
        cost_estimate=cost(30 * len(xs)),
        name="gather_rows",
    )(*xs, comb)


def sum_kernel(p_ref, out_ref, *scratch):
    job = Sum(p_ref, *scratch)
    greet(False)
    job.first()
    job.second()
    job.third()
    job.last()
    one, two = job.total()
    out_ref[: job.half] = one.astype(out_ref.dtype)
    out_ref[job.half :] = two.astype(out_ref.dtype)


def sum_rows(p, number):
    _, rows, width = p.shape
    return pl.pallas_call(
        sum_kernel,
        in_specs=anywhere(1),
        out_specs=pl.BlockSpec(memory_space=pltpu.VMEM),
        out_shape=jax.ShapeDtypeStruct((rows, width), f32),
        scratch_shapes=Sum.scratch(rows, width),
        compiler_params=params(40, collective_id=number, has_side_effects=True),
        cost_estimate=cost(35),
        name="sum_rows",
    )(p)


def to_owner_kernel(o_ref, att_ref, send_sem, recv_sem, local_sem):
    z, c, t = spot()
    nt = lax.axis_size("tp")
    own = c * nt + t
    greet(False)
    copies = []
    for i in range(o_ref.shape[0]):
        block = zig(c, i)
        copy = remote(o_ref.at[i], att_ref.at[t], send_sem.at[i], recv_sem.at[t], ctx=block // nt, tp=lax.rem(block, nt))
        local = pltpu.make_async_copy(o_ref.at[i], att_ref.at[t], local_sem)
        copies.append((block == own, copy, local))
    settle(copies)
    mine = lax.rem((own + 1) // 2, 2) == c
    for source in range(nt):

        @pl.when(jnp.logical_or(jnp.logical_not(mine), source != t))
        def _():
            remote(o_ref.at[0], att_ref.at[source], send_sem.at[0], recv_sem.at[source], ctx=c, tp=t).wait_recv()


def settle(copies):
    for here, copy, local in copies:

        @pl.when(jnp.logical_not(here))
        def _():
            copy.start()

        @pl.when(here)
        def _():
            local.start()

    for here, copy, local in copies:

        @pl.when(jnp.logical_not(here))
        def _():
            copy.wait_send()

        @pl.when(here)
        def _():
            local.wait()


def to_heads_kernel(o_ref, got_ref, send_sem, recv_sem, local_sem):
    z, c, t = spot()
    nt = lax.axis_size("tp")
    own = c * nt + t
    greet(False)
    core = lax.rem((own + 1) // 2, 2)
    slot = 2 * (own // 4) + lax.rem(own, 4) // 2
    copies = []
    for target in range(nt):
        here = jnp.logical_and(core == c, target == t)
        copy = remote(o_ref.at[target], got_ref.at[slot], send_sem.at[target], recv_sem.at[slot], ctx=core, tp=target)
        local = pltpu.make_async_copy(o_ref.at[target], got_ref.at[slot], local_sem)
        copies.append((here, copy, local))
    settle(copies)
    for i in range(got_ref.shape[0]):

        @pl.when(zig(c, i) != own)
        def _():
            remote(o_ref.at[0], got_ref.at[i], send_sem.at[0], recv_sem.at[i], ctx=c, tp=t).wait_recv()


def exchange(kernel, o, count, number, name):
    vmem = pl.BlockSpec(memory_space=pltpu.VMEM)
    return pl.pallas_call(
        kernel,
        in_specs=[vmem],
        out_specs=vmem,
        out_shape=jax.ShapeDtypeStruct((count,) + o.shape[1:], o.dtype),
        scratch_shapes=[
            pltpu.SemaphoreType.DMA((o.shape[0],)),
            pltpu.SemaphoreType.DMA((count,)),
            pltpu.SemaphoreType.DMA,
        ],
        compiler_params=params(16, collective_id=number, has_side_effects=True),
        cost_estimate=cost(12),
        name=name,
    )(o)


def closing_kernel(p_ref, gw_ref, small_ref, top_ref, ge0, ge1, ge2, ge3, out_ref, gsum_ref, ssum_ref, tmax_ref, gall_ref,
                   gcore, gline, gmine, sline, splane, tline, mytop, *sems):
    job = Sum(p_ref, *sems[:7])
    sends, recvs, local = sems[7:]
    z, c, t = spot()
    ns = lax.axis_size("shard")
    rows = gw_ref.shape[2]
    own = 4 * c + t
    greet()
    row = lax.broadcasted_iota(jnp.int32, mytop.shape, 0)
    high = jnp.full(mytop.shape, -1e30, f32)
    for h in range(top_ref.shape[0]):
        best = jnp.max(jnp.max(top_ref[h], axis=0), axis=1, keepdims=True)
        high = jnp.where(row == h, best, high)
    mytop[...] = high
    started = []

    def go(k, source, target, **where):
        copy = remote(source, target, sends.at[k], recvs.at[k], **where)
        copy.start()
        started.append(copy)
        return copy

    core = go(0, gw_ref.at[1 - c], gcore, ctx=1 - c)
    small = [go(3 + s, small_ref.at[lax.rem(z + s, ns)], sline.at[s], shard=lax.rem(z + s, ns)) for s in range(1, ns)]
    tops = [go(3 + ns + s, mytop, tline.at[s], shard=lax.rem(z + s, ns)) for s in range(1, ns)]
    own_g = pltpu.make_async_copy(gw_ref.at[c], gmine, local.at[0])
    own_g.start()
    job.first()
    experts = [go(11 + 4 * ns + k, ge, gall_ref.at[k], ctx=1 - c) for k, ge in enumerate((ge0, ge1, ge2, ge3))]
    job.second()
    own_g.wait()
    core.wait_recv()
    gmine[...] = (gmine[...].astype(f32) + gcore[...].astype(f32)).astype(bf16)
    line = [go(3 + 2 * ns + s, gmine.at[lax.rem(z + s, ns)], gline.at[s], shard=lax.rem(z + s, ns)) for s in range(1, ns)]
    for copy in small:
        copy.wait_recv()
    total = small_ref[z]
    for s in range(1, ns):
        total = total + sline[s]
    splane[0] = total
    plane = []
    for s in range(1, 8):
        other = lax.rem(own + s, 8)
        plane.append(go(3 + 3 * ns + s, splane.at[0], splane.at[s], ctx=other // 4, tp=lax.rem(other, 4)))
    for copy in tops:
        copy.wait_recv()
    high = mytop[...]
    for s in range(1, ns):
        high = jnp.maximum(high, tline[s])
    tline[0] = high
    pair = go(2, tline.at[0], tline.at[ns], ctx=1 - c)
    job.third()
    for copy in line:
        copy.wait_recv()
    total = gmine[z].astype(f32)
    for s in range(1, ns):
        total = total + gline[s].astype(f32)
    gsum_ref[c] = total
    final = go(3, gsum_ref.at[c], gsum_ref.at[c], ctx=1 - c)
    for copy in plane:
        copy.wait_recv()
    total = splane[0]
    for s in range(1, 8):
        total = total + splane[s]
    ssum_ref[...] = total
    pair.wait_recv()
    tmax_ref[...] = jnp.maximum(tline[0], tline[ns])
    job.last()
    one, two = job.total()
    out_ref[: job.half] = one
    out_ref[job.half :] = two
    remote(gsum_ref.at[1 - c], gsum_ref.at[1 - c], sends.at[3], recvs.at[3], ctx=1 - c).wait_recv()
    for copy in experts:
        copy.wait_recv()
    for copy in started:
        copy.wait_send()


def closing(p, gw, small, top, experts, number):
    _, rows, width = p.shape
    ns = lax.axis_size("shard")
    vmem = pl.BlockSpec(memory_space=pltpu.VMEM)
    return pl.pallas_call(
        closing_kernel,
        in_specs=anywhere(2) + [vmem, vmem] + anywhere(4),
        out_specs=[vmem, vmem, vmem, vmem] + anywhere(1),
        out_shape=[
            jax.ShapeDtypeStruct((rows, width), f32),
            jax.ShapeDtypeStruct((2,) + gw.shape[2:], f32),
            jax.ShapeDtypeStruct(small.shape[1:], f32),
            jax.ShapeDtypeStruct((8, 128), f32),
            jax.ShapeDtypeStruct((4,) + experts[0].shape, bf16),
        ],
        scratch_shapes=[
            pltpu.VMEM(gw.shape[1:], bf16),
            pltpu.VMEM(gw.shape[1:], bf16),
            pltpu.VMEM(gw.shape[1:], bf16),
            pltpu.VMEM(small.shape, f32),
            pltpu.VMEM((8,) + small.shape[1:], f32),
            pltpu.VMEM((ns + 1, 8, 128), f32),
            pltpu.VMEM((8, 128), f32),
        ]
        + Sum.scratch(rows, width)
        + [
            pltpu.SemaphoreType.DMA((4 * ns + 15,)),
            pltpu.SemaphoreType.DMA((4 * ns + 15,)),
            pltpu.SemaphoreType.DMA((2,)),
        ],
        compiler_params=params(48, collective_id=number, has_side_effects=True),
        cost_estimate=cost(40),
        name="closing",
    )(p, gw, small, top, *experts)


def mixing(n2, wrc, previous, routes):
    z = mm(n2, wrc, NT, lax.Precision.HIGHEST)
    lane = lax.broadcasted_iota(jnp.int32, z.shape, 1)
    logits = z + previous
    hot = [lane == routes[:, r : r + 1] for r in range(2)]
    picked = [jnp.sum(jnp.where(hot[r], logits, 0.0), axis=1, keepdims=True) for r in range(2)]
    most = jnp.maximum(picked[0], picked[1])
    e = [jnp.exp(p - most) for p in picked]
    gates = [v / (e[0] + e[1]) for v in e]
    combine = jnp.where(hot[0], gates[0], 0.0) + jnp.where(hot[1], gates[1], 0.0)

    def column(array, at):
        return jnp.sum(jnp.where(lane == at, array, 0.0), axis=1, keepdims=True)

    alphas = []
    for j in range(2):
        first, second = column(z, EXPERTS + 2 * j), column(z, EXPERTS + 2 * j + 1)
        most = jnp.maximum(first, second)
        a, b = jnp.exp(first - most), jnp.exp(second - most)
        alphas.append((a / (a + b), b / (a + b)))
    weights = [column(combine, FFN_EXPERTS + 1 + j) for j in range(3)]
    return hot, gates, combine, alphas, weights


def forward_kernel(place, x_ref, att_ref, wo_ref, small_ref, prev_ref, routes_ref, res_ref, base_ref, a_ref, comb_ref):
    heads_in = att_ref.shape[0] * att_ref.shape[1]
    att = att_ref[...].reshape(heads_in, att_ref.shape[2])
    wo = wo_ref[...].reshape(heads_in, wo_ref.shape[2])
    res = x_ref[...].astype(f32) + mm(att, wo, TN)
    res_ref[...] = res
    inverse = lax.rsqrt(jnp.mean(res * res, axis=1, keepdims=True) + epsilon)
    n2 = res * inverse * small_ref[19:20]
    a_ref[...] = n2.astype(bf16)
    _, _, combine, alphas, weights = mixing(n2, small_ref[:16], prev_ref[...], routes_ref[...])
    scale = weights[0] + weights[1] * alphas[0][0] + weights[2] * alphas[1][0]
    base_ref[...] = (
        res
        + scale * n2
        + (weights[1] * alphas[0][1]) * small_ref[16:17]
        + (weights[2] * alphas[1][1]) * small_ref[17:18]
    )
    comb_ref[...] = combine.T[:16]


def forward_rows(place, x, att, wo, small, prev, routes):
    rows, width = x.shape
    own = lambda i, p: (p[0], 0)
    return pl.pallas_call(
        forward_kernel,
        grid_spec=pltpu.PrefetchScalarGridSpec(
            num_scalar_prefetch=1,
            grid=(1,),
            in_specs=[
                full(x.shape),
                full(att.shape),
                full(wo.shape),
                full(small.shape),
                pl.BlockSpec((rows, prev.shape[1]), own),
                pl.BlockSpec((rows, 2), own),
            ],
            out_specs=[full((rows, width)), full((rows, width)), full((rows, width)), full((16, rows))],
        ),
        out_shape=[
            jax.ShapeDtypeStruct((rows, width), f32),
            jax.ShapeDtypeStruct((rows, width), f32),
            jax.ShapeDtypeStruct((rows, width), bf16),
            jax.ShapeDtypeStruct((16, rows), f32),
        ],
        compiler_params=params(),
        cost_estimate=cost(8),
        name="forward_rows",
    )(place, x, att, wo, small, prev, routes)


def backward_kernel(place, res_ref, dn_ref, cot_ref, valid_ref, att_ref, wo_ref, par_ref, prev_ref, routes_ref,
                    dres_ref, got_ref, gwo_ref, small_ref):
    width = res_ref.shape[1]
    res = res_ref[...]
    gain = par_ref[19:20]
    inverse = lax.rsqrt(jnp.mean(res * res, axis=1, keepdims=True) + epsilon)
    m = res * inverse
    n2 = m * gain
    hot, gates, _, alphas, weights = mixing(n2, par_ref[:16], prev_ref[...], routes_ref[...])
    g = cot_ref[...].astype(f32) * valid_ref[...]
    inner = jnp.sum(g * n2, axis=1, keepdims=True)
    onto = [jnp.sum(g * par_ref[16 + j : 17 + j], axis=1, keepdims=True) for j in range(2)]
    named = dn_ref[:, width:].astype(f32)
    lane = lax.broadcasted_iota(jnp.int32, hot[0].shape, 1)
    wide = lax.broadcasted_iota(jnp.int32, named.shape, 1)
    local = {
        FFN_EXPERTS + 1: inner,
        FFN_EXPERTS + 2: alphas[0][0] * inner + alphas[0][1] * onto[0],
        FFN_EXPERTS + 3: alphas[1][0] * inner + alphas[1][1] * onto[1],
    }
    routes = routes_ref[...]
    dgates = []
    for r in range(2):
        name = routes[:, r : r + 1]
        there = jnp.where((wide == name) | (wide == name + 16), named, 0.0)
        there = jnp.where(name < FFN_EXPERTS, jnp.sum(there, axis=1, keepdims=True), 0.0)
        for e, value in local.items():
            there = there + jnp.where(name == e, value, 0.0)
        dgates.append(there)
    mean = gates[0] * dgates[0] + gates[1] * dgates[1]
    dz = jnp.where(hot[0], gates[0] * (dgates[0] - mean), 0.0)
    dz = dz + jnp.where(hot[1], gates[1] * (dgates[1] - mean), 0.0)
    for j in range(2):
        da = weights[1 + j] * inner
        db = weights[1 + j] * onto[j]
        centre = alphas[j][0] * da + alphas[j][1] * db
        dz = dz + jnp.where(lane == EXPERTS + 2 * j, alphas[j][0] * (da - centre), 0.0)
        dz = dz + jnp.where(lane == EXPERTS + 2 * j + 1, alphas[j][1] * (db - centre), 0.0)
    scale = weights[0] + weights[1] * alphas[0][0] + weights[2] * alphas[1][0]
    highest = lax.Precision.HIGHEST
    dn2 = dn_ref[:, :width].astype(f32) + scale * g + mm(dz, par_ref[:16], NN, highest)
    small_ref[0:16] = mm(dz, n2, TN, highest)
    small_ref[16:24] = jnp.zeros((8, width), f32)
    small_ref[16:17] = jnp.sum((weights[1] * alphas[0][1]) * g, axis=0, keepdims=True)
    small_ref[17:18] = jnp.sum((weights[2] * alphas[1][1]) * g, axis=0, keepdims=True)
    small_ref[18:19] = jnp.sum(dn2 * m, axis=0, keepdims=True)
    q = dn2 * gain
    dres = g + inverse * (q - m * jnp.mean(q * m, axis=1, keepdims=True))
    dres_ref[...] = dres
    da = dres.astype(bf16)
    wo = wo_ref[...].reshape(-1, width)
    got = mm(wo, da, NT).astype(bf16)
    got_ref[...] = got.reshape(got_ref.shape)
    att = att_ref[...].reshape(got.shape)
    gwo_ref[...] = mm(att, da).astype(bf16).reshape(gwo_ref.shape)


def backward_rows(place, res, dn, cot, valid, att, wo, small, prev, routes):
    rows, width = res.shape
    own = lambda i, p: (p[0], 0)
    return pl.pallas_call(
        backward_kernel,
        grid_spec=pltpu.PrefetchScalarGridSpec(
            num_scalar_prefetch=1,
            grid=(1,),
            in_specs=[
                full(res.shape),
                full(dn.shape),
                full(cot.shape),
                full(valid.shape),
                full(att.shape),
                full(wo.shape),
                full(small.shape),
                pl.BlockSpec((rows, prev.shape[1]), own),
                pl.BlockSpec((rows, 2), own),
            ],
            out_specs=[full((rows, width)), full(att.shape), full(wo.shape), full((24, width))],
        ),
        out_shape=[
            jax.ShapeDtypeStruct((rows, width), f32),
            jax.ShapeDtypeStruct(att.shape, bf16),
            jax.ShapeDtypeStruct(wo.shape, bf16),
            jax.ShapeDtypeStruct((24, width), f32),
        ],
        compiler_params=params(),
        cost_estimate=cost(15),
        name="backward_rows",
    )(place, res, dn, cot, valid, att, wo, small, prev, routes)


def finish_kernel(x_ref, dn_ref, dres_ref, small_ref, base_ref, feed_ref, valid_ref, gw_ref, gs_ref, top_ref, wq_ref, wk_ref, limit_ref, other_ref, *refs):
    local = other_ref.shape[0]
    own, outs = refs[:local], refs[local:]
    gin_ref, out_ref, gate_ref, up_ref, down_ref = outs[:5]
    x = x_ref[...].astype(f32)
    inverse = lax.rsqrt(jnp.mean(x * x, axis=1, keepdims=True) + epsilon)
    m = x * inverse
    q = dn_ref[...] * small_ref[18:19]
    gin_ref[...] = dres_ref[...] + inverse * (q - m * jnp.mean(q * m, axis=1, keepdims=True))
    out_ref[...] = (valid_ref[...] * (base_ref[...] + feed_ref[...])).astype(bf16)
    core = lax.axis_index("ctx")
    for k, target in enumerate((gate_ref, up_ref, down_ref)):
        for j in range(local):
            mine, theirs = own[j][k].astype(f32), other_ref[j, k].astype(f32)
            target[j] = jnp.where(core == 0, mine, theirs)
            target[local + j] = jnp.where(core == 0, theirs, mine)

    @pl.when(pl.program_id(0) == 0)
    def _():
        gq, gk, gv, go, gnorm, gmoe, grouter, gconst, gvec, fac_ref, cq_ref, ck_ref = outs[5:]
        width = wq_ref.shape[1]
        flat = gw_ref[...].reshape(4 * width, gw_ref.shape[2])
        for k, target in enumerate((gq, gk, gv)):
            target[...] = flat[k * width : (k + 1) * width].T
        go[...] = flat[3 * width :]
        sums = gs_ref[...]
        across_rows = sums.T
        grouter[...] = across_rows[:, :EXPERTS]
        gconst[...] = across_rows[:, EXPERTS : EXPERTS + 4]
        gvec[...] = sums[16:18]
        gmoe[...] = sums[18:19]
        gnorm[...] = sums[19:20]
        factors = limit_ref[...] / jnp.maximum(top_ref[...], limit_ref[...])
        fac_ref[...] = factors
        lane = lax.broadcasted_iota(jnp.int32, (1, width), 1)
        root = jnp.zeros((1, width), f32)
        for h in range(width // HEAD_DIM):
            root = jnp.where(lane // HEAD_DIM == h, jnp.sqrt(factors[h : h + 1, :1]), root)
        cq_ref[...] = (wq_ref[...].astype(f32) * root).astype(bf16)
        ck_ref[...] = (wk_ref[...].astype(f32) * root).astype(bf16)


def finish_rows(x, dn, dres, small, base, feed, valid, gw, gs, top, wq, wk, limit, other, own):
    rows, width = x.shape
    local, kinds, depth, hidden = other.shape
    steps = 4 if depth % 64 == 0 else 1
    tile, deep = rows // steps, depth // steps
    by_row = pl.BlockSpec((tile, width), lambda i: (i, 0))
    expert_out = pl.BlockSpec((2 * local, deep, hidden), lambda i: (0, i, 0))
    once = [
        jax.ShapeDtypeStruct(shape, f32)
        for shape in [wq.shape] * 3
        + [(wq.shape[1], depth), (1, depth), (1, depth), (depth, EXPERTS), (depth, 4), (2, depth), (8, 128)]
    ] + [jax.ShapeDtypeStruct(wq.shape, bf16)] * 2
    return pl.pallas_call(
        finish_kernel,
        grid=(steps,),
        in_specs=[
            by_row,
            by_row,
            by_row,
            full(small.shape),
            by_row,
            by_row,
            pl.BlockSpec((tile, 1), lambda i: (i, 0)),
            full(gw.shape),
            full(gs.shape),
            full(top.shape),
            full(wq.shape),
            full(wk.shape),
            full(limit.shape),
            pl.BlockSpec((local, kinds, deep, hidden), lambda i: (0, 0, i, 0)),
        ]
        + [pl.BlockSpec((kinds, deep, hidden), lambda i: (0, i, 0))] * local,
        out_specs=[by_row, by_row, expert_out, expert_out, expert_out] + [full(v.shape) for v in once],
        out_shape=[
            jax.ShapeDtypeStruct((rows, width), f32),
            jax.ShapeDtypeStruct((rows, width), bf16),
        ]
        + [jax.ShapeDtypeStruct((2 * local, depth, hidden), f32)] * 3
        + once,
        compiler_params=params(),
        cost_estimate=cost(8),
        name="finish_rows",
    )(x, dn, dres, small, base, feed, valid, gw, gs, top, wq, wk, limit, other, *own)


def place_kernel(per, rt_ref, rc_ref, row_ref, col_ref):
    total = rt_ref.shape[1]
    one = lax.broadcasted_iota(jnp.int32, (BLOCK, BLOCK), 0)
    two = lax.broadcasted_iota(jnp.int32, (BLOCK, BLOCK), 1)
    before_row = (one < two).astype(bf16)
    before_col = (two < one).astype(bf16)
    row_carry = col_carry = None
    for at in range(0, total, BLOCK):
        if at % per == 0:
            row_carry = jnp.zeros((16, 1), f32)
            col_carry = jnp.zeros((1, 16), f32)
        here = slice(at, at + BLOCK)
        expert = lax.broadcasted_iota(jnp.int32, (16, BLOCK), 0)
        member = (rt_ref[0:1, here] == expert) | (rt_ref[1:2, here] == expert)
        rank = mm(member.astype(bf16), before_row) + row_carry
        row_ref[:, here] = jnp.where(member, rank, -1.0)
        row_carry = row_carry + jnp.sum(member.astype(f32), axis=1, keepdims=True)
        expert = lax.broadcasted_iota(jnp.int32, (BLOCK, 16), 1)
        member = (rc_ref[here, 0:1] == expert) | (rc_ref[here, 1:2] == expert)
        rank = mm(before_col, member.astype(bf16)) + col_carry
        col_ref[here, :] = jnp.where(member, rank, -1.0)
        col_carry = col_carry + jnp.sum(member.astype(f32), axis=0, keepdims=True)


def place_rows(routes, per):
    total = routes.shape[0]
    return pl.pallas_call(
        functools.partial(place_kernel, per),
        out_shape=[
            jax.ShapeDtypeStruct((16, total), f32),
            jax.ShapeDtypeStruct((total, 16), f32),
        ],
        compiler_params=params(),
        cost_estimate=cost(5),
        name="place_rows",
    )(routes.T, routes)


def fetch_kernel(first, row_ref, comb_ref, rows_ref, out_ref, gate_ref):
    expert = first[0] + pl.program_id(1)
    slot = lax.broadcasted_iota(jnp.int32, (CAP, row_ref.shape[1]), 0).astype(f32)
    hot = slot == row_ref[pl.ds(expert, 1), :]
    out_ref[0] = mm(hot.astype(bf16), rows_ref[...]).astype(bf16)
    if gate_ref is not None:
        gate_ref[0] = jnp.sum(jnp.where(hot, comb_ref[pl.ds(expert, 1), :], 0.0), axis=1, keepdims=True)


def fetch_rows(first, row, comb, rows, per, local, gated):
    total, width = rows.shape
    blocks = total // per
    outs = [jax.ShapeDtypeStruct((local, blocks * CAP, width), bf16)]
    specs = [pl.BlockSpec((1, CAP, width), lambda b, j, f: (j, b, 0))]
    ins = [
        pl.BlockSpec((16, per), lambda b, j, f: (0, b)),
        pl.BlockSpec((16, per), lambda b, j, f: (0, b)),
        pl.BlockSpec((per, width), lambda b, j, f: (b, 0)),
    ]
    args = (row, comb, rows)
    if gated:
        outs.append(jax.ShapeDtypeStruct((local, blocks * CAP, 1), f32))
        specs.append(pl.BlockSpec((1, CAP, 1), lambda b, j, f: (j, b, 0)))
        body = fetch_kernel
    else:
        body = lambda f, p, r, o: fetch_kernel(f, p, None, r, o, None)
        del ins[1]
        args = (row, rows)
    return pl.pallas_call(
        body,
        grid_spec=pltpu.PrefetchScalarGridSpec(
            num_scalar_prefetch=1, grid=(blocks, local), in_specs=ins, out_specs=specs
        ),
        out_shape=outs,
        compiler_params=params(),
        cost_estimate=cost(18),
        name="fetch_rows",
    )(first, *args)


def expert_kernel(j, first, x_ref, g_ref, gate_ref, w_ref, feed_ref, back_ref, gw_ref, total):
    i = pl.program_id(0)
    parts, _, _, depth, hidden = w_ref.shape
    width = parts * depth
    wg, wu, wd = [w_ref[:, 0, k].reshape(width, hidden) for k in range(3)]
    x, g, gate = x_ref[0], g_ref[0], gate_ref[0]
    gate_pre = mm(x, wg)
    up = mm(x, wu)
    sigmoid = 1.0 / (1.0 + jnp.exp(-gate_pre))
    activated = gate_pre * sigmoid
    inner = (activated * up).astype(bf16)
    out = mm(inner, wd, NT)
    g32 = g.astype(f32)
    feed_ref[...] = (gate * out).astype(bf16)
    dgate = jnp.sum(g32 * out, axis=1, keepdims=True)
    dout = (gate * g32).astype(bf16)
    dinner = mm(dout, wd)
    dpre = (dinner * up * sigmoid * (1.0 + gate_pre * (1.0 - sigmoid))).astype(bf16)
    dup = (dinner * activated).astype(bf16)
    back_ref[:, :width] = (mm(dpre, wg, NT) + mm(dup, wu, NT)).astype(bf16)
    lane = lax.broadcasted_iota(jnp.int32, (dgate.shape[0], back_ref.shape[1] - width), 1)
    coarse = dgate.astype(bf16).astype(f32)
    at = first[0] + j
    extra = jnp.where(lane == at, coarse, jnp.where(lane == at + 16, dgate - coarse, 0.0))
    back_ref[:, width:] = extra.astype(bf16)

    @pl.when(i == 0)
    def _():
        total[...] = jnp.zeros_like(total)

    total[0] += mm(x, dpre, TN)
    total[1] += mm(x, dup, TN)
    total[2] += mm(dout, inner, TN)

    @pl.when(i == pl.num_programs(0) - 1)
    def _():
        for k in range(3):
            gw_ref[:, k] = total[k].reshape(parts, depth, hidden).astype(bf16)


def expert(j, first, x, g, gate, w):
    slots, width = x.shape[1:]
    parts, _, kinds, depth, hidden = w.shape
    grads = (parts, kinds, depth, hidden)
    pick = lambda i, f: (j, i, 0)
    return pl.pallas_call(
        functools.partial(expert_kernel, j),
        grid_spec=pltpu.PrefetchScalarGridSpec(
            num_scalar_prefetch=1,
            grid=(slots // CAP,),
            in_specs=[
                pl.BlockSpec((1, CAP, width), pick),
                pl.BlockSpec((1, CAP, width), pick),
                pl.BlockSpec((1, CAP, 1), pick),
                pl.BlockSpec((parts, 1, kinds, depth, hidden), lambda i, f: (0, j, 0, 0, 0)),
            ],
            out_specs=[
                pl.BlockSpec((CAP, width), lambda i, f: (i, 0)),
                pl.BlockSpec((CAP, width + EXTRA), lambda i, f: (i, 0)),
                full(grads),
            ],
            scratch_shapes=[pltpu.VMEM((3, width, hidden), f32)],
        ),
        out_shape=[
            jax.ShapeDtypeStruct((slots, width), bf16),
            jax.ShapeDtypeStruct((slots, width + EXTRA), bf16),
            jax.ShapeDtypeStruct(grads, bf16),
        ],
        compiler_params=params(),
        cost_estimate=cost(14),
        name="expert",
    )(first, x, g, gate, w)


def spread_kernel(local, first, col_ref, *refs):
    out_ref = refs[-1]
    lane = lax.broadcasted_iota(jnp.int32, col_ref.shape, 1)
    slot = lax.broadcasted_iota(jnp.int32, (col_ref.shape[0], CAP), 1).astype(f32)
    total = None
    for j in range(local):
        mine = jnp.sum(jnp.where(lane == first[0] + j, col_ref[...], 0.0), axis=1, keepdims=True)
        term = mm((slot == mine).astype(bf16), refs[j][...])
        total = term if total is None else total + term
    out_ref[...] = total.astype(bf16)


def spread_rows(first, col, values, per):
    total = col.shape[0]
    tile = BLOCK
    width = values[0].shape[1]
    return pl.pallas_call(
        functools.partial(spread_kernel, len(values)),
        grid_spec=pltpu.PrefetchScalarGridSpec(
            num_scalar_prefetch=1,
            grid=(total // tile,),
            in_specs=[pl.BlockSpec((tile, 16), lambda i, f: (i, 0))]
            + [pl.BlockSpec((CAP, width), lambda i, f: (i // (per // tile), 0)) for _ in values],
            out_specs=pl.BlockSpec((tile, width), lambda i, f: (i, 0)),
        ),
        out_shape=jax.ShapeDtypeStruct((total, width), bf16),
        compiler_params=params(),
        cost_estimate=cost(20),
        name="spread_rows",
    )(first, col, *values)


def shards(
    hidden_in,
    cotangent,
    lengths,
    routes,
    prev_logits,
    norm_attn,
    w_query,
    w_key,
    w_value,
    w_out,
    norm_moe,
    w_router,
    w_const,
    const_vec,
    w_gate,
    w_up,
    w_down,
    threshold,
):
    plane = ("ctx", "tp")
    core, lane = lax.axis_index("ctx"), lax.axis_index("tp")
    nc, nt, ns = lax.axis_size("ctx"), lax.axis_size("tp"), lax.axis_size("shard")
    own, width = hidden_in.shape
    per = own * nt
    total = per * nc
    depth = w_gate.shape[1]
    heads = w_query.shape[1] // HEAD_DIM
    head_width = heads * HEAD_DIM
    local = FFN_EXPERTS // nc
    count = total // BLOCK // nc
    first_row = core * per + lane * own
    length = lengths[0]
    valid = (first_row + jnp.arange(own, dtype=jnp.int32) < length).astype(f32)[:, None]
    place = lane.astype(jnp.int32)[None]
    first = (core * local).astype(jnp.int32)[None]

    pieces = [
        lax.dynamic_slice_in_dim(w, core * local, local, 0) for w in (w_gate, w_up, w_down)
    ]
    expert_w = lax.all_gather(jnp.stack(pieces, axis=1), "shard", axis=0, tiled=False)
    small = jnp.concatenate(
        [
            w_router,
            w_const,
            const_vec.T,
            norm_attn[:, None],
            norm_moe[:, None],
            jnp.zeros((depth, SMALL - EXPERTS - 8), bf16),
        ],
        axis=1,
    )
    rows_all, attention_w, routes_all = opening(
        hidden_in, w_query, w_key, w_value, w_out, small, routes, 0
    )
    rows_all = rows_all.reshape(total, width)
    routes_all = routes_all.reshape(total, 2)
    prev = jnp.pad(prev_logits, ((0, 0), (0, 4)))
    cosine, sine = rope_tables(total)

    qt, kt, k, v, vt, wt, out_w, small = project(rows_all, attention_w, cosine, sine, heads)
    ot, lse, top, cot_all, out_w = attend(lengths, qt, k, vt, cotangent, out_w, count, 1)
    att = exchange(to_owner_kernel, ot, nt, 2, "to_owner")

    res, base, a2, comb = forward_rows(place, hidden_in, att, out_w, small, prev, routes)

    row_at, col_at = place_rows(routes_all, per)
    a2_all, comb_all = gather_rows((a2,), comb, 3)
    a2_all, cot_all = a2_all.reshape(total, width), cot_all.reshape(total, width)
    (g_slots,) = fetch_rows(first, row_at, None, cot_all, per, local, False)
    comb_all = comb_all.transpose(1, 0, 2).reshape(16, total)
    x_slots, gate_slots = fetch_rows(first, row_at, comb_all, a2_all, per, local, True)
    feeds, backs, grads = [], [], []
    for j in range(local):
        feed, back, grad = expert(j, first, x_slots, g_slots, gate_slots, expert_w)
        feeds.append(feed)
        backs.append(back)
        grads.append(grad)
    back = spread_rows(first, col_at, backs, per).reshape(8, own, width + EXTRA)
    back = sum_rows(back, 4)
    feed = spread_rows(first, col_at, feeds, per).reshape(8, own, width)
    feed = sum_rows(feed, 5)
    grads = [lax.psum_scatter(g, "shard", scatter_dimension=0, tiled=True)[0] for g in grads]

    dres, got, grad_out, gsmall = backward_rows(
        place, res, back, cotangent, valid, att, out_w, small, prev, routes
    )
    got = exchange(to_heads_kernel, got, count, 6, "to_heads")
    dq, dk, dv, grad_out = revisit(qt, k, kt, v, ot, got, lse, grad_out, 7)
    part, grad_w, gsmall = unproject(
        dq, dk, dv, cosine, sine, rows_all, small, wt, grad_out, gsmall, ns
    )
    part, grad_w, gsmall, top, others = closing(part.reshape(8, own, width), grad_w, gsmall, top, grads, 8)
    limit = jnp.broadcast_to(threshold[None], (8, 128))
    (grad_input, output, grad_gate, grad_up, grad_down, grad_q, grad_k, grad_v, grad_out, grad_norm_attn, grad_norm_moe,
     grad_router, grad_const, grad_vec, factors, clipped_query, clipped_key) = finish_rows(
        hidden_in, part, dres, small, base, feed, valid, grad_w, gsmall, top, w_query, w_key, limit, others, grads
    )
    return (
        output,
        grad_input,
        grad_norm_attn[0],
        grad_q,
        grad_k,
        grad_v,
        grad_out,
        grad_norm_moe[0],
        grad_router,
        grad_const,
        grad_vec,
        grad_gate,
        grad_up,
        grad_down,
        factors[:heads, 0],
        clipped_query,
        clipped_key,
    )


def solution(mesh):
    return jax.shard_map(
        shards,
        mesh=mesh,
        in_specs=(
            P(("shard", "ctx", "tp"), None),
            P(("shard", "ctx", "tp"), None),
            P("shard"),
            P(("shard", "ctx"), None),
            P(("shard", "ctx"), None),
            P("shard"),
            P("shard", "tp"),
            P("shard", "tp"),
            P("shard", "tp"),
            P("tp", "shard"),
            P("shard"),
            P("shard", None),
            P("shard", None),
            P(None, "shard"),
            P(None, "shard", "tp"),
            P(None, "shard", "tp"),
            P(None, "shard", "tp"),
            P(),
        ),
        out_specs=(
            P(("shard", "ctx", "tp"), None),
            P(("shard", "ctx", "tp"), None),
            P("shard"),
            P("shard", "tp"),
            P("shard", "tp"),
            P("shard", "tp"),
            P("tp", "shard"),
            P("shard"),
            P("shard", None),
            P("shard", None),
            P(None, "shard"),
            P(None, "shard", "tp"),
            P(None, "shard", "tp"),
            P(None, "shard", "tp"),
            P("tp"),
            P("shard", "tp"),
            P("shard", "tp"),
        ),
        check_vma=False,
    )
```

time: 713 us -> 580 us (0.81)
  Pallas kernels: 610 us -> 512 us
  local copies, waits for them, and re-layouts: 61.7 us -> 41.2 us
  other arithmetic: 18.3 us -> 2.41 us
    pallas_call x1, Pallas kernels: 101 us -> 49.2 us  [closing(): pl.pallas_call(closing_kernel, in_specs=anywhere(2) + [vmem, vmem] + anyw...]
    pallas_call x1, Pallas kernels: 59.1 us -> 35.2 us  [gather_rows(): pl.pallas_call(functools.partial(gather_kernel, cuts, len(xs)), in_specs=...]
    pallas_call x7, Pallas kernels: 207 us -> 184 us  [the longest x1 55 us: revisit(): pl.pallas_call(revisit_kernel, grid=(heads, count), in_specs=[whole, tall...]
    convert_element_type x6 -> x0, other arithmetic: 8.73 us -> none  [the longest x1 7.29 us: shards(): grad_expert.reshape((FFN_EXPERTS,) + grad_expert.shape[2:]).astype(f32)]
    squeeze x1 -> x0, local copies, waits for them, and re-layouts: 7.81 us -> none  [shards(): grad_gate, grad_up, grad_down = [grad_expert[:, k] for k in range(3)]]
    unnamed x96 -> x82, local copies, waits for them, and re-layouts: 40 us -> 34.7 us
  transfers between devices with their start and end apart: 5 -> 5, of which waited for: 0 -> 0; matrix products, arithmetic and copies ran while one was open for 3% -> 1% of each run, Pallas kernels for 69% -> 77%
where the time goes in v3:
time: 580 us; the launch traced here: 572 us
  Pallas kernels  512 us (88%)
  local copies, waits for them, and re-layouts  41.2 us (7%)
  between operations  15.9 us (3%)
    pallas_call x2, Pallas kernels, sum_rows(): pl.pallas_call(sum_kernel, in_specs=anywhere(1), out_specs=pl.BlockSpec(m...  68 us
    pallas_call x4, Pallas kernels, expert(): pl.pallas_call(functools.partial(expert_kernel, j), grid_spec=pltpu.Prefe...  55.7 us
    pallas_call x1, Pallas kernels, revisit(): pl.pallas_call(revisit_kernel, grid=(heads, count), in_specs=[whole, tall...  55 us
    pallas_call x1, Pallas kernels, closing(): pl.pallas_call(closing_kernel, in_specs=anywhere(2) + [vmem, vmem] + anyw...  49.2 us
    pallas_call x1, Pallas kernels, attend(): pl.pallas_call(functools.partial(attend_kernel, cuts), grid_spec=pltpu.Pr...  46.9 us
    pallas_call x2, Pallas kernels, spread_rows(): pl.pallas_call(functools.partial(spread_kernel, len(values)), grid_spec=p...  41 us
    pallas_call x2, Pallas kernels, fetch_rows(): pl.pallas_call(body, grid_spec=pltpu.PrefetchScalarGridSpec(num_scalar_pr...  36.8 us
    pallas_call x1, Pallas kernels, gather_rows(): pl.pallas_call(functools.partial(gather_kernel, cuts, len(xs)), in_specs=...  35.2 us
  transfers between devices with their start and end apart: 5, of which 0 were waited for; matrix products, arithmetic and copies ran while one was open for 1% of the time, Pallas kernels for 77%

profile of v3, /device:TPU:0, one launch (start us, length us, event | category | flops | bytes accessed | tf_op | source)
XLA Modules:
  0.0 571.8 jit_solution(12829559919342202009)
XLA Ops:
  7.3 1.3 copy-done
  10.3 1.7 pad_maximum_fusion
  15.5 34.4 %opening.1 = (bf16[8,512,768]{2,1,0:T(8,128)(2,1)S(1)}, bf16[2,4,2,192,256]{4,3,2,1,0:T(8,128)(2,1)S(1)}, s32[2,2048,2]{2,1,0:T(8,128)S(1)}) custom-call(bf16[512,768]{1,0:T(8,128)(2,1)S(1)} %copy-done.4, bf16[192,192]{1,0:T(8,128)(2,1)S(1)} %copy-done.11, bf16[192,192]{1,0:T(8,128)(2,1)S(1)} %copy-done.12, bf16[192,192]{1,0:T(8,128)(2,1)S(1)} %copy-done.9, ...), custom_call_target="tpu_custom_call" | custom-call | flops 30000001024 | bytes 90000000 | tf_op jit(solution)/shard_map/opening/pallas_call | solution.py:720
  49.9 2.6 copy-done.14
  54.3 1.3 copy.63
  57.9 13.8 %project.1 = (bf16[3,64,4096]{2,1,0:T(8,128)(2,1)}, bf16[3,64,4096]{2,1,0:T(8,128)(2,1)}, bf16[3,4096,64]{2,1,0:T(8,128)(2,1)}, bf16[3,4096,64]{2,1,0:T(8,128)(2...) custom-call(bf16[4096,768]{1,0:T(8,128)(2,1)} %bitcast.44, ...), custom_call_target="tpu_custom_call" | custom-call | flops 12999999488 | bytes 39000000 | tf_op jit(solution)/shard_map/project/pallas_call | solution.py:334
  71.7 46.9 %attend.1 = (bf16[4,192,512]{2,1,0:T(8,128)(2,1)}, f32[3,4,1,512]{3,2,1,0:T(1,128)}, f32[3,4,1,512]{3,2,1,0:T(1,128)}, bf16[8,512,768]{2,1,0:T(8,128)(2,1)}, bf16[4,192,768]{2,1,0:T(8,128)(2,1)}) custom-call(s32[1]{0:T(128)} %copy.71.length, bf16[3,64,4096]{2,1,0:T(8,128)(2,1)} %get-tuple-element.90.qt_ref, bf16[3,4096,64]{2,1,0:T(8,128)(2,1)} %get-tuple-element.91.k_ref, ...), custom_call_target="tpu_custom_call" | custom-call | flops 35000000512 | bytes 105000000 | tf_op jit(solution)/shard_map/attend/pallas_call | solution.py:450
  119.7 10.5 %to_owner.1.att_ref = bf16[4,192,512]{2,1,0:T(8,128)(2,1)S(1)} custom-call(bf16[4,192,512]{2,1,0:T(8,128)(2,1)S(1)} %copy-done.24), custom_call_target="tpu_custom_call" | custom-call | flops 12000000000 | bytes 36000000 | tf_op jit(solution)/shard_map/to_owner/pallas_call | solution.py:882
  131.1 7.5 %forward_rows.1 = (f32[512,768]{1,0:T(8,128)}, f32[512,768]{1,0:T(8,128)}, bf16[512,768]{1,0:T(8,128)(2,1)}, f32[16,512]{1,0:T(8,128)}) custom-call(s32[1]{0:T(128)} %bitcast.2.place, bf16[512,768]{1,0:T(8,128)(2,1)} %x_ref.5, bf16[4,192,512]{2,1,0:T(8,128)(2,1)} %copy-done.20, bf16[4,192,768]{2,1,0:T(8,128)(2,1)} %get-tuple-element.97.wo_ref, ...), custom_call_target="tpu_custom_call" | custom-call | flops 8000000000 | bytes 24000000 | tf_op jit(solution)/shard_map/forward_rows/pallas_call | solution.py:1060
  140.5 35.2 %gather_rows.1 = (bf16[8,512,768]{2,1,0:T(8,128)(2,1)S(1)}, f32[8,16,512]{2,1,0:T(8,128)S(1)}) custom-call(bf16[512,768]{1,0:T(8,128)(2,1)S(1)} %copy-done.21, f32[16,512]{1,0:T(8,128)S(1)} %copy-done.28), custom_call_target="tpu_custom_call" | custom-call | flops 30000001024 | bytes 90000000 | tf_op jit(solution)/shard_map/gather_rows/pallas_call | solution.py:774
  175.8 2.6 copy-done.16
  179.1 5.0 place_rows.1
  184.1 17.8 %fetch_rows.3.g_ref = bf16[4,1024,768]{2,1,0:T(8,128)(2,1)} custom-call(s32[1]{0:T(128)} %bitcast.3.first.f, f32[16,4096]{1,0:T(8,128)} %get-tuple-element.102.row_ref.p, bf16[4096,768]{1,0:T(8,128)(2,1)} %bitcast.55), custom_call_target="tpu_custom_call" | custom-call | flops 17999998976 | bytes 54000000 | tf_op jit(solution)/shard_map/fetch_rows/pallas_call | solution.py:1330
  201.9 19.0 %fetch_rows.2 = (bf16[4,1024,768]{2,1,0:T(8,128)(2,1)}, f32[4,1024,1]{2,1,0:T(8,128)}) custom-call(s32[1]{0:T(128)} %bitcast.3.first.f, f32[16,4096]{1,0:T(8,128)} %get-tuple-element.102.row_ref.p, f32[16,4096]{1,0:T(8,128)} %bitcast.48, bf16[4096,768]{1,0:T(8,128)(2,1)} %bitcast.47), custom_call_target="tpu_custom_call" | custom-call | flops 17999998976 | bytes 54000000 | tf_op jit(solution)/shard_map/fetch_rows/pallas_call | solution.py:1330
  220.9 13.8 %expert.7 = (bf16[1024,768]{1,0:T(8,128)(2,1)}, bf16[1024,896]{1,0:T(8,128)(2,1)}, bf16[4,3,192,512]{3,2,1,0:T(8,128)(2,1)}) custom-call(s32[1]{0:T(128)} %bitcast.3.first.f, bf16[4,1024,768]{2,1,0:T(8,128)(2,1)} %get-tuple-element.107.x_ref, bf16[4,1024,768]{2,1,0:T(8,128)(2,1)} %fetch_rows.3.g_ref, f32[4,1024,1]{2,1,0:T(8,128)} %get-tuple-element.109.gate_ref, ...), custom_call_target="tpu_custom_call" | custom-call | flops 14000000000 | bytes 42000000 | tf_op jit(solution)/shard_map/expert/pallas_call | solution.py:1387
  234.9 13.8 %expert.6 = (bf16[1024,768]{1,0:T(8,128)(2,1)}, bf16[1024,896]{1,0:T(8,128)(2,1)}, bf16[4,3,192,512]{3,2,1,0:T(8,128)(2,1)}) custom-call(s32[1]{0:T(128)} %bitcast.3.first.f, bf16[4,1024,768]{2,1,0:T(8,128)(2,1)} %get-tuple-element.107.x_ref, bf16[4,1024,768]{2,1,0:T(8,128)(2,1)} %fetch_rows.3.g_ref, f32[4,1024,1]{2,1,0:T(8,128)} %get-tuple-element.109.gate_ref, ...), custom_call_target="tpu_custom_call" | custom-call | flops 14000000000 | bytes 42000000 | tf_op jit(solution)/shard_map/expert/pallas_call | solution.py:1387
  250.2 14.2 %expert.5 = (bf16[1024,768]{1,0:T(8,128)(2,1)}, bf16[1024,896]{1,0:T(8,128)(2,1)}, bf16[4,3,192,512]{3,2,1,0:T(8,128)(2,1)}) custom-call(s32[1]{0:T(128)} %bitcast.3.first.f, bf16[4,1024,768]{2,1,0:T(8,128)(2,1)} %get-tuple-element.107.x_ref, bf16[4,1024,768]{2,1,0:T(8,128)(2,1)} %fetch_rows.3.g_ref, f32[4,1024,1]{2,1,0:T(8,128)} %get-tuple-element.109.gate_ref, ...), custom_call_target="tpu_custom_call" | custom-call | flops 14000000000 | bytes 42000000 | tf_op jit(solution)/shard_map/expert/pallas_call | solution.py:1387
  264.4 13.8 %expert.4 = (bf16[1024,768]{1,0:T(8,128)(2,1)}, bf16[1024,896]{1,0:T(8,128)(2,1)}, bf16[4,3,192,512]{3,2,1,0:T(8,128)(2,1)}) custom-call(s32[1]{0:T(128)} %bitcast.3.first.f, bf16[4,1024,768]{2,1,0:T(8,128)(2,1)} %get-tuple-element.107.x_ref, bf16[4,1024,768]{2,1,0:T(8,128)(2,1)} %fetch_rows.3.g_ref, f32[4,1024,1]{2,1,0:T(8,128)} %get-tuple-element.109.gate_ref, ...), custom_call_target="tpu_custom_call" | custom-call | flops 14000000000 | bytes 42000000 | tf_op jit(solution)/shard_map/expert/pallas_call | solution.py:1387
  278.3 22.4 %spread_rows.2 = bf16[4096,896]{1,0:T(8,128)(2,1)} custom-call(s32[1]{0:T(128)} %bitcast.3.first.f, f32[4096,16]{1,0:T(8,128)} %get-tuple-element.101.col_ref, bf16[1024,896]{1,0:T(8,128)(2,1)} %get-tuple-element.110.refs_0_, bf16[1024,896]{1,0:T(8,128)(2,1)} %get-tuple-element.111.refs_1_, bf16[1024,896]{1,0:T(8,128)(2,1)} %get-tuple-element.112.refs_2_, ...), custom_call_target="tpu_custom_call" | custom-call | flops 20000000000 | bytes 60000000 | tf_op jit(solution)/shard_map/spread_rows/pallas_call | solution.py:1432
  300.7 3.2 copy-done.13
  303.9 36.7 %sum_rows.2.dn_ref = f32[512,896]{1,0:T(8,128)S(1)} custom-call(bf16[8,512,896]{2,1,0:T(8,128)(2,1)S(1)} %bitcast.43), custom_call_target="tpu_custom_call" | custom-call | flops 35000000512 | bytes 105000000 | tf_op jit(solution)/shard_map/sum_rows/pallas_call | solution.py:805
  341.9 15.6 %backward_rows.1 = (f32[512,768]{1,0:T(8,128)}, bf16[4,192,512]{2,1,0:T(8,128)(2,1)}, bf16[4,192,768]{2,1,0:T(8,128)(2,1)}, f32[24,768]{1,0:T(8,128)}) custom-call(s32[1]{0:T(128)} %bitcast.2.place, f32[512,768]{1,0:T(8,128)} %get-tuple-element.99.res_ref, f32[512,896]{1,0:T(8,128)} %copy-done.23, bf16[512,768]{1,0:T(8,128)(2,1)} %cot_ref.3, ...), custom_call_target="tpu_custom_call" | custom-call | flops 15000000512 | bytes 45000000 | tf_op jit(solution)/shard_map/backward_rows/pallas_call | solution.py:1147
  358.6 10.5 %to_heads.1.got_ref = bf16[4,192,512]{2,1,0:T(8,128)(2,1)S(1)} custom-call(bf16[4,192,512]{2,1,0:T(8,128)(2,1)S(1)} %copy-done.26), custom_call_target="tpu_custom_call" | custom-call | flops 12000000000 | bytes 36000000 | tf_op jit(solution)/shard_map/to_heads/pallas_call | solution.py:882
  370.0 18.7 %spread_rows.3 = bf16[4096,768]{1,0:T(8,128)(2,1)} custom-call(s32[1]{0:T(128)} %bitcast.3.first.f, f32[4096,16]{1,0:T(8,128)} %get-tuple-element.101.col_ref, bf16[1024,768]{1,0:T(8,128)(2,1)} %get-tuple-element.134.refs_0_, bf16[1024,768]{1,0:T(8,128)(2,1)} %get-tuple-element.135.refs_1_, bf16[1024,768]{1,0:T(8,128)(2,1)} %get-tuple-element.136.refs_2_, ...), custom_call_target="tpu_custom_call" | custom-call | flops 20000000000 | bytes 60000000 | tf_op jit(solution)/shard_map/spread_rows/pallas_call | solution.py:1432
  388.7 55.0 %revisit.1 = (f32[3,64,4096]{2,1,0:T(8,128)}, f32[3,64,4096]{2,1,0:T(8,128)}, f32[3,64,4096]{2,1,0:T(8,128)}, bf16[192,768]{1,0:T(8,128)(2,1)}) custom-call(bf16[3,64,4096]{2,1,0:T(8,128)(2,1)} %get-tuple-element.90.qt_ref, bf16[3,4096,64]{2,1,0:T(8,128)(2,1)} %get-tuple-element.91.k_ref, bf16[3,64,4096]{2,1,0:T(8,128)(2,1)} %get-tuple-element.92.kt_ref, ...), custom_call_target="tpu_custom_call" | custom-call | flops 49999998976 | bytes 150000000 | tf_op jit(solution)/shard_map/revisit/pallas_call | solution.py:557
  443.7 16.4 %unproject.1 = (bf16[4096,768]{1,0:T(8,128)(2,1)}, bf16[2,4,384,192]{3,2,1,0:T(8,128)(2,1)}, f32[4,24,192]{2,1,0:T(8,128)}) custom-call(f32[3,64,4096]{2,1,0:T(8,128)} %get-tuple-element.117.dq_ref, f32[3,64,4096]{2,1,0:T(8,128)} %get-tuple-element.118.dk_ref, f32[3,64,4096]{2,1,0:T(8,128)} %get-tuple-element.119.dv_ref, f32[32,4096]{1,0:T(8,128)} %constant.27.clone.cos_ref, ...), custom_call_target="tpu_custom_call" | custom-call | flops 17999998976 | bytes 54000000 | tf_op jit(solution)/shard_map/unproject/pallas_call | solution.py:639
  460.2 31.3 %sum_rows.3.feed_ref = f32[512,768]{1,0:T(8,128)S(1)} custom-call(bf16[8,512,768]{2,1,0:T(8,128)(2,1)S(1)} %bitcast.46), custom_call_target="tpu_custom_call" | custom-call | flops 35000000512 | bytes 105000000 | tf_op jit(solution)/shard_map/sum_rows/pallas_call | solution.py:805
  496.9 49.2 %closing.1 = (f32[512,768]{1,0:T(8,128)S(1)}, f32[2,384,192]{2,1,0:T(8,128)S(1)}, f32[24,192]{1,0:T(8,128)S(1)}, f32[8,128]{1,0:T(8,128)S(1)}, bf16[4,3,192,512]{3,2,1,0:T(8,128)(2,1)}) custom-call(bf16[8,512,768]{2,1,0:T(8,128)(2,1)} %bitcast.54, bf16[2,4,384,192]{3,2,1,0:T(8,128)(2,1)} %get-tuple-element.124.gw_ref, f32[4,24,192]{2,1,0:T(8,128)S(1)} %copy-done.29, ...), custom_call_target="tpu_custom_call" | custom-call | flops 40000000000 | bytes 120000000 | tf_op jit(solution)/shard_map/closing/pallas_call | solution.py:981
  550.0 10.4 %finish_rows.1 = (f32[512,768]{1,0:T(8,128)}, bf16[512,768]{1,0:T(8,128)(2,1)}, f32[8,192,512]{2,1,0:T(8,128)}, f32[8,192,512]{2,1,0:T(8,128)}, f32[8,192,512]{2...) custom-call(bf16[512,768]{1,0:T(8,128)(2,1)} %x_ref.5, ...), custom_call_target="tpu_custom_call" | custom-call | flops 8000000000 | bytes 24000000 | tf_op jit(solution)/shard_map/finish_rows/pallas_call | solution.py:1231
  560.4 1.3 slice_reduce_fusion
  561.7 1.6 copy.69
  563.2 1.6 copy.68
  (102 shorter events, 26.7 us)
Async XLA Ops:
  7.2 1.4 copy-start
  7.2 1.9 copy-start.32
  7.2 213.7 %all-gather.3.cloned.1.call-start = ((), (), s32[]{:S(2)}) async-start(), calls=%async_computation.8 | async-start | bytes 11796480 | tf_op jit(solution)/shard_map/all_gather | solution.py:1488
  12.0 1.0 copy-start.33
  12.0 1.4 copy-start.9
  12.0 1.4 copy-start.10
  12.0 1.4 copy-start.11
  12.1 480.6 %reduce-scatter.11.cloned.1.call-start = ((), (), s32[]{:S(2)}) async-start(), calls=%async_computation.7 | async-start | bytes 2949120 | tf_op jit(solution)/shard_map/reduce_scatter | solution.py:1530
  13.4 1.1 copy-start.4
  15.4 34.4 %copy-start.3 = (s32[2048,2]{1,0:T(8,128)}, s32[2048,2]{1,0:T(8,128)S(1)}, u32[]{:S(2)}) copy-start(s32[2048,2]{1,0:T(8,128)S(1)} %copy.62.routes_ref) | copy-start | bytes 49156
  49.9 2.6 copy-start.14
  52.5 1.1 copy-start.22
  53.6 4.2 copy-start.2
  118.6 1.1 copy-start.24
  138.6 1.1 copy-start.21
  175.8 2.6 copy-start.16
  234.8 257.8 %reduce-scatter.9.cloned.1.call-start = ((), (), s32[]{:S(2)}) async-start(), calls=%async_computation.6 | async-start | bytes 2949120 | tf_op jit(solution)/shard_map/reduce_scatter | solution.py:1530
  248.7 243.9 %reduce-scatter.7.cloned.1.call-start = ((), (), s32[]{:S(2)}) async-start(), calls=%async_computation.5 | async-start | bytes 2949120 | tf_op jit(solution)/shard_map/reduce_scatter | solution.py:1530
  278.3 214.4 %reduce-scatter.5.cloned.1.call-start = ((), (), s32[]{:S(2)}) async-start(), calls=%async_computation.4 | async-start | bytes 2949120 | tf_op jit(solution)/shard_map/reduce_scatter | solution.py:1530
  300.7 3.2 copy-start.13
  340.6 1.3 copy-start.23
  357.5 1.1 copy-start.26
  443.7 16.5 %copy-start.15 = (bf16[4096,768]{1,0:T(8,128)(2,1)S(1)}, bf16[4096,768]{1,0:T(8,128)(2,1)}, u32[]{:S(2)}) copy-start(bf16[4096,768]{1,0:T(8,128)(2,1)} %spread_rows.3) | copy-start | bytes 18874372
  460.1 32.5 %copy-start.29 = (f32[4,24,192]{2,1,0:T(8,128)S(1)}, f32[4,24,192]{2,1,0:T(8,128)}, u32[]{:S(2)}) copy-start(f32[4,24,192]{2,1,0:T(8,128)} %get-tuple-element.125.small_ref) | copy-start | bytes 221188
  460.1 32.5 %copy-start.31 = (f32[3,4,1,512]{3,2,1,0:T(1,128)S(1)}, f32[3,4,1,512]{3,2,1,0:T(1,128)}, u32[]{:S(2)}) copy-start(f32[3,4,1,512]{3,2,1,0:T(1,128)} %get-tuple-element.126.top_ref) | copy-start | bytes 73732
  491.4 1.2 copy-start.17
  492.7 1.1 copy-start.5
  493.7 1.1 copy-start.6
  494.8 1.1 copy-start.7
  495.9 1.1 copy-start.8
  546.1 1.1 copy-start.18
  550.0 14.8 %copy-start.1 = (bf16[8,192,512]{2,1,0:T(8,128)(2,1)S(1)}, bf16[8,192,512]{2,1,0:T(8,128)(2,1)}, u32[]{:S(2)}) copy-start(bf16[8,192,512]{2,1,0:T(8,128)(2,1)} %param.34) | copy-start | bytes 4718596
  (12 other events, 9.1 us)
Sparse Core Ops, SparseCore 0:
  12.2 180.1 all-gather.2
  234.9 58.2 reduce-scatter.10
  295.5 47.5 reduce-scatter.8
  345.2 47.5 reduce-scatter.6
  395.5 47.4 reduce-scatter.4
